TPU v7x, 32 devices: a whole 2x2x4 slice. The times are simulated.
32 devices in a mesh: seq: 16 (over z, x, core), head: 2 (over y).
Axes of the slice: x: 2, y: 2, z: 4, core: 2. Of those that a mesh axis runs over, the one named last changes fastest.
Arguments:
- frames: bfloat16 [4096, 768], P('seq')
- lengths: int32 [3], replicated, may hold values from 75 to 3781, as said below
- gn_gain: float32 [768], replicated, may hold values from 0.5 to 1.5
- gn_bias: float32 [768], replicated, may hold values from -4 to 4
- w_query: bfloat16 [768, 768], P(None, 'head'), may hold values from -0.21875 to 0.21875
- q_bias: float32 [768], P('head'), may hold values from -4 to 4
- w_key: bfloat16 [768, 768], P(None, 'head'), may hold values from -0.21875 to 0.21875
- w_value: bfloat16 [768, 768], P(None, 'head'), may hold values from -0.21875 to 0.21875
- v_bias: float32 [768], P('head'), may hold values from -0.15625 to 0.15625
- w_out: bfloat16 [768, 768], P('head')
- out_bias: float32 [768], replicated, may hold values from -4 to 4
- conv_weight: float32 [768, 7], replicated, may hold values from -2 to 2
- conv_bias: float32 [768], replicated, may hold values from -3 to 3
- ln_gain: float32 [768], replicated, may hold values from 0.5 to 1.5
- ln_bias: float32 [768], replicated, may hold values from -4 to 4
- w_up: bfloat16 [768, 2304], P(None, 'head'), may hold values from -0.21875 to 0.21875
- up_bias: float32 [2304], P('head'), may hold values from -6 to 6
- w_down: bfloat16 [2304, 768], P('head'), may hold values from -0.125 to 0.125
- down_bias: float32 [768], replicated, may hold values from -4 to 4
- layer_scale: float32 [768], replicated, may hold values from 1 to 4
- out_grad: bfloat16 [4096, 768], P('seq'), may hold values from -6 to 6
Outputs:
- output: bfloat16 [4096, 768], P('seq')
- frames_grad: float32 [4096, 768], P('seq')
- grad_gn_gain: float32 [768], P('seq')
- grad_gn_bias: float32 [768], P('seq')
- grad_w_query: float32 [768, 768], P('seq', 'head')
- grad_q_bias: float32 [768], P(('head', 'seq'))
- grad_w_key: float32 [768, 768], P('seq', 'head')
- grad_w_value: float32 [768, 768], P('seq', 'head')
- grad_v_bias: float32 [768], P(('head', 'seq'))
- grad_w_out: float32 [768, 768], P(('head', 'seq'))
- grad_out_bias: float32 [768], P('seq')
- grad_conv_weight: float32 [768, 7], P('seq')
- grad_conv_bias: float32 [768], P('seq')
- grad_ln_gain: float32 [768], P('seq')
- grad_ln_bias: float32 [768], P('seq')
- grad_w_up: float32 [768, 2304], P('seq', 'head')
- grad_up_bias: float32 [2304], P(('head', 'seq'))
- grad_w_down: float32 [2304, 768], P(('head', 'seq'))
- grad_down_bias: float32 [768], P('seq')
- grad_layer_scale: float32 [768], P('seq')
Inputs may be any that keep to these rules, and one draw needn't show every extreme that they name: Clips lie in order along the frames and their lengths sum to 4096. Clip 2 // 2 is a long recording of exactly 4096 - 2 // 2 * (315) frames; it begins on the first index of seq and ends on the last. Clips 0 and 2 have 75 to 240 frames and sum to 315: one has exactly 240 frames, the other 75.
All inputs are finite; a program needn't handle non-finite values.
Results may differ from a plain program's by a relative error of at most 0.015.
Values may be sent and summed in bfloat16 or wider, within the bound.
A program may use at most 256 MiB of HBM per device.

v0:
```python
import jax
import jax.numpy as jnp
from jax import lax
from jax.sharding import PartitionSpec as P

HEAD_DIM = 64
GROUPS = 32
KERNEL = 7


highest = lax.Precision.HIGHEST
eps_norm = 1e-06


def with_halo(cells, sides, width):
    for axis, dim in sides:
        count = lax.axis_size(axis)
        ends = count - 1
        head = lax.slice_in_dim(cells, 0, width, axis=dim)
        tail = lax.slice_in_dim(cells, cells.shape[dim] - width, cells.shape[dim], axis=dim)
        cells = jnp.concatenate(
            [
                lax.ppermute(tail, axis, [(i, (i + 1) % count) for i in range(ends)]),
                cells,
                lax.ppermute(head, axis, [((i + 1) % count, i) for i in range(ends)]),
            ],
            axis=dim,
        )
    return cells


def segment_of(positions, clip_ends):
    return jnp.sum((positions[:, None] >= clip_ends[None, :]).astype(jnp.int32), axis=1)


def block_size(number):
    target = number
    while target > 4096 and target % 2 == 0:
        target = target // 2
    return target


def fold_blocks(update, carry, arrays, start):
    number = arrays[0].shape[0]
    target = block_size(number)
    if target == number:
        return update(carry, arrays, start)
    pieces = tuple(
        (member.reshape((number // target, target) + member.shape[1:]) for member in arrays)
    )

    def inner(state, entry):
        block_index, block_parts = entry
        return (update(state, block_parts, start + block_index * target), None)

    carry, unused = lax.scan(inner, carry, (jnp.arange(number // target, dtype=jnp.int32), pieces))
    return carry


def shards(
    frames,
    lengths,
    gn_gain,
    gn_bias,
    w_query,
    q_bias,
    w_key,
    w_value,
    v_bias,
    w_out,
    out_bias,
    conv_weight,
    conv_bias,
    ln_gain,
    ln_bias,
    w_up,
    up_bias,
    w_down,
    down_bias,
    layer_scale,
    out_grad,
):
    rows_local = frames.shape[0]
    model_width = frames.shape[1]
    heads_local = w_query.shape[1] // HEAD_DIM
    group_width = model_width // GROUPS
    half_width = KERNEL // 2
    score_scale = HEAD_DIM ** (-0.5)
    clip_ends = jnp.cumsum(lengths)
    first_row = lax.axis_index("seq") * rows_local
    own_segment = segment_of(first_row + jnp.arange(rows_local, dtype=jnp.int32), clip_ends)
    onehot = (
        own_segment[:, None] == jnp.arange(lengths.shape[0], dtype=jnp.int32)[None, :]
    ).astype(jnp.float32)
    members = (lengths * group_width).astype(jnp.float32)[:, None]

    def key_segments(start, number):
        return segment_of(start + jnp.arange(number, dtype=jnp.int32), clip_ends)

    inputs = frames.astype(jnp.float32)
    grouped = inputs.reshape(rows_local, GROUPS, group_width)
    sums_one = jnp.dot(onehot.T, jnp.sum(grouped, axis=2), precision=highest)
    sums_two = jnp.dot(onehot.T, jnp.sum(grouped * grouped, axis=2), precision=highest)
    sums_one, sums_two = lax.psum((sums_one, sums_two), "seq")
    group_mean = sums_one / members
    group_rstd = lax.rsqrt(sums_two / members - group_mean * group_mean + eps_norm)
    frame_mean = jnp.dot(onehot, group_mean, precision=highest)
    frame_rstd = jnp.dot(onehot, group_rstd, precision=highest)
    grouped_hat = (grouped - frame_mean[:, :, None]) * frame_rstd[:, :, None]
    normed_hat = grouped_hat.reshape(rows_local, model_width)
    normed = (normed_hat * gn_gain + gn_bias).astype(jnp.bfloat16)
    query = (jnp.dot(normed, w_query, preferred_element_type=jnp.float32) + q_bias).astype(
        jnp.bfloat16
    )
    keys = jnp.dot(normed, w_key, preferred_element_type=jnp.float32).astype(jnp.bfloat16)
    values = (jnp.dot(normed, w_value, preferred_element_type=jnp.float32) + v_bias).astype(
        jnp.bfloat16
    )
    query_heads = query.reshape(rows_local, heads_local, HEAD_DIM)
    key_heads = keys.reshape(rows_local, heads_local, HEAD_DIM)
    value_heads = values.reshape(rows_local, heads_local, HEAD_DIM)

    def forward_step(carry, pieces, start):
        running_max, running_sum, accum = carry
        key_part, value_part = pieces
        number = key_part.shape[0]
        same = (own_segment[:, None] == key_segments(start, number)[None, :])[None]
        scores = (
            jnp.einsum(
                "qhd,khd->hqk",
                query_heads,
                key_part.reshape(number, heads_local, HEAD_DIM),
                preferred_element_type=jnp.float32,
            )
            * score_scale
        )
        scores = jnp.where(same, scores, -1e30)
        new_max = jnp.maximum(running_max, jnp.max(scores, axis=2))
        weights = jnp.where(same, jnp.exp(scores - new_max[:, :, None]), 0.0)
        factor = jnp.exp(running_max - new_max)
        running_sum = running_sum * factor + jnp.sum(weights, axis=2)
        update = jnp.einsum(
            "hqk,khd->hqd",
            weights.astype(jnp.bfloat16),
            value_part.reshape(number, heads_local, HEAD_DIM),
            preferred_element_type=jnp.float32,
        )
        return (new_max, running_sum, accum * factor[:, :, None] + update)

    start_state = (
        jnp.full((heads_local, rows_local), -1e30, jnp.float32),
        jnp.zeros((heads_local, rows_local), jnp.float32),
        jnp.zeros((heads_local, rows_local, HEAD_DIM), jnp.float32),
    )
    final_state = fold_blocks(
        forward_step,
        start_state,
        (
            lax.all_gather(keys, "seq", axis=0, tiled=True),
            lax.all_gather(values, "seq", axis=0, tiled=True),
        ),
        jnp.int32(0),
    )
    running_max, running_sum, accum = final_state
    log_total = running_max + jnp.log(running_sum)
    attended_heads = (accum / running_sum[:, :, None]).transpose(1, 0, 2)
    attended_low = attended_heads.reshape(rows_local, heads_local * HEAD_DIM).astype(jnp.bfloat16)
    branch = (
        lax.psum(jnp.dot(attended_low, w_out, preferred_element_type=jnp.float32), "head")
        + out_bias
    )
    hidden = inputs + branch
    padded = with_halo(hidden, (("seq", 0),), half_width)
    rim_segment = segment_of(
        first_row - half_width + jnp.arange(rows_local + 2 * half_width, dtype=jnp.int32), clip_ends
    )
    tap_masks = []
    mixed = jnp.zeros((rows_local, model_width), jnp.float32) + conv_bias
    for offset in range(KERNEL):
        inside = (rim_segment[offset : offset + rows_local] == own_segment).astype(jnp.float32)[
            :, None
        ]
        tap_masks.append(inside)
        mixed = mixed + padded[offset : offset + rows_local] * conv_weight[:, offset] * inside
    center = mixed - jnp.mean(mixed, axis=1, keepdims=True)
    ln_rstd = lax.rsqrt(jnp.mean(center * center, axis=1, keepdims=True) + eps_norm)
    ln_hat = center * ln_rstd
    ln_low = (ln_hat * ln_gain + ln_bias).astype(jnp.bfloat16)
    pre_act = jnp.dot(ln_low, w_up, preferred_element_type=jnp.float32) + up_bias
    activated, gelu_back = jax.vjp(jax.nn.gelu, pre_act)
    act_low = activated.astype(jnp.bfloat16)
    projected = (
        lax.psum(jnp.dot(act_low, w_down, preferred_element_type=jnp.float32), "head") + down_bias
    )
    output = (hidden + layer_scale * projected).astype(jnp.bfloat16)
    cotangent = out_grad.astype(jnp.float32)
    proj_grad = (cotangent * layer_scale).astype(jnp.bfloat16)
    grad_layer_scale = jnp.sum(cotangent * projected, axis=0)
    grad_down_bias = jnp.sum(proj_grad.astype(jnp.float32), axis=0)
    grad_w_down = jnp.dot(act_low.T, proj_grad, preferred_element_type=jnp.float32)
    act_grad = jnp.dot(proj_grad, w_down.T, preferred_element_type=jnp.float32)
    (pre_grad,) = gelu_back(act_grad)
    pre_low = pre_grad.astype(jnp.bfloat16)
    grad_up_bias = jnp.sum(pre_low.astype(jnp.float32), axis=0)
    grad_w_up = jnp.dot(ln_low.T, pre_low, preferred_element_type=jnp.float32)
    ln_grad = lax.psum(jnp.dot(pre_low, w_up.T, preferred_element_type=jnp.float32), "head")
    grad_ln_gain = jnp.sum(ln_grad * ln_hat, axis=0)
    grad_ln_bias = jnp.sum(ln_grad, axis=0)
    hat_grad = ln_grad * ln_gain
    mixed_grad = ln_rstd * (
        hat_grad
        - jnp.mean(hat_grad, axis=1, keepdims=True)
        - ln_hat * jnp.mean(hat_grad * ln_hat, axis=1, keepdims=True)
    )
    grad_conv_bias = jnp.sum(mixed_grad, axis=0)
    grad_conv_weight = jnp.stack(
        [
            jnp.sum(mixed_grad * padded[offset : offset + rows_local] * tap_masks[offset], axis=0)
            for offset in range(KERNEL)
        ],
        axis=1,
    )
    padded_grad = with_halo(mixed_grad, (("seq", 0),), half_width)
    hidden_grad = cotangent
    for offset in range(KERNEL):
        mirror = KERNEL - 1 - offset
        inside = (rim_segment[mirror : mirror + rows_local] == own_segment).astype(jnp.float32)[
            :, None
        ]
        hidden_grad = (
            hidden_grad
            + padded_grad[mirror : mirror + rows_local] * conv_weight[:, offset] * inside
        )
    branch_grad = hidden_grad.astype(jnp.bfloat16)
    grad_out_bias = jnp.sum(branch_grad.astype(jnp.float32), axis=0)
    grad_w_out = jnp.dot(attended_low.T, branch_grad, preferred_element_type=jnp.float32)
    attended_grad = jnp.dot(branch_grad, w_out.T, preferred_element_type=jnp.float32).astype(
        jnp.bfloat16
    )
    grad_heads = attended_grad.reshape(rows_local, heads_local, HEAD_DIM)
    offset_rows = jnp.sum(grad_heads.astype(jnp.float32) * attended_heads, axis=2)
    offset_heads = offset_rows.T

    def query_step(carry, pieces, start):
        key_part, value_part = pieces
        number = key_part.shape[0]
        part_keys = key_part.reshape(number, heads_local, HEAD_DIM)
        same = (own_segment[:, None] == key_segments(start, number)[None, :])[None]
        scores = (
            jnp.einsum("qhd,khd->hqk", query_heads, part_keys, preferred_element_type=jnp.float32)
            * score_scale
        )
        probs = jnp.where(same, jnp.exp(scores - log_total[:, :, None]), 0.0)
        prob_grad = jnp.einsum(
            "qhd,khd->hqk",
            grad_heads,
            value_part.reshape(number, heads_local, HEAD_DIM),
            preferred_element_type=jnp.float32,
        )
        score_grad = (probs * (prob_grad - offset_heads[:, :, None])).astype(jnp.bfloat16)
        return (
            carry
            + jnp.einsum("hqk,khd->qhd", score_grad, part_keys, preferred_element_type=jnp.float32)
            * score_scale
        )

    query_zero = jnp.zeros((rows_local, heads_local, HEAD_DIM), jnp.float32)
    query_grad_sum = fold_blocks(
        query_step,
        query_zero,
        (
            lax.all_gather(keys, "seq", axis=0, tiled=True),
            lax.all_gather(values, "seq", axis=0, tiled=True),
        ),
        jnp.int32(0),
    )

    def key_step(carry, pieces, start):
        key_grad_sum, value_grad_sum = carry
        query_part, grad_part, total_part, offset_part = pieces
        number = query_part.shape[0]
        part_queries = query_part.astype(jnp.bfloat16).reshape(number, heads_local, HEAD_DIM)
        part_grads = grad_part.astype(jnp.bfloat16).reshape(number, heads_local, HEAD_DIM)
        same = (key_segments(start, number)[:, None] == own_segment[None, :])[None]
        scores = (
            jnp.einsum("qhd,khd->hqk", part_queries, key_heads, preferred_element_type=jnp.float32)
            * score_scale
        )
        probs = jnp.where(same, jnp.exp(scores - total_part.T[:, :, None]), 0.0)
        value_grad_sum = value_grad_sum + jnp.einsum(
            "hqk,qhd->khd",
            probs.astype(jnp.bfloat16),
            part_grads,
            preferred_element_type=jnp.float32,
        )
        prob_grad = jnp.einsum(
            "qhd,khd->hqk", part_grads, value_heads, preferred_element_type=jnp.float32
        )
        score_grad = (probs * (prob_grad - offset_part.T[:, :, None])).astype(jnp.bfloat16)
        key_grad_sum = (
            key_grad_sum
            + jnp.einsum(
                "hqk,qhd->khd", score_grad, part_queries, preferred_element_type=jnp.float32
            )
            * score_scale
        )
        return (key_grad_sum, value_grad_sum)

    key_grad_sum, value_grad_sum = fold_blocks(
        key_step,
        (query_zero, query_zero),
        (
            lax.all_gather(query.astype(jnp.float32), "seq", axis=0, tiled=True),
            lax.all_gather(attended_grad.astype(jnp.float32), "seq", axis=0, tiled=True),
            lax.all_gather(log_total.T, "seq", axis=0, tiled=True),
            lax.all_gather(offset_rows, "seq", axis=0, tiled=True),
        ),
        jnp.int32(0),
    )
    query_grad = query_grad_sum.reshape(rows_local, heads_local * HEAD_DIM).astype(jnp.bfloat16)
    key_grad = key_grad_sum.reshape(rows_local, heads_local * HEAD_DIM).astype(jnp.bfloat16)
    value_grad = value_grad_sum.reshape(rows_local, heads_local * HEAD_DIM).astype(jnp.bfloat16)
    grad_q_bias = jnp.sum(query_grad.astype(jnp.float32), axis=0)
    grad_v_bias = jnp.sum(value_grad.astype(jnp.float32), axis=0)
    grad_w_query = jnp.dot(normed.T, query_grad, preferred_element_type=jnp.float32)
    grad_w_key = jnp.dot(normed.T, key_grad, preferred_element_type=jnp.float32)
    grad_w_value = jnp.dot(normed.T, value_grad, preferred_element_type=jnp.float32)
    normed_part = (
        jnp.dot(query_grad, w_query.T, preferred_element_type=jnp.float32)
        + jnp.dot(key_grad, w_key.T, preferred_element_type=jnp.float32)
        + jnp.dot(value_grad, w_value.T, preferred_element_type=jnp.float32)
    )
    normed_grad = lax.psum(normed_part, "head")
    grad_gn_gain = jnp.sum(normed_grad * normed_hat, axis=0)
    grad_gn_bias = jnp.sum(normed_grad, axis=0)
    scaled_grad = (normed_grad * gn_gain).reshape(rows_local, GROUPS, group_width)
    part_one = jnp.dot(onehot.T, jnp.sum(scaled_grad, axis=2), precision=highest)
    part_two = jnp.dot(onehot.T, jnp.sum(scaled_grad * grouped_hat, axis=2), precision=highest)
    part_one, part_two = lax.psum((part_one, part_two), "seq")
    mean_one = jnp.dot(onehot, part_one / members, precision=highest)
    mean_two = jnp.dot(onehot, part_two / members, precision=highest)
    frames_grad = hidden_grad + (
        frame_rstd[:, :, None]
        * (scaled_grad - mean_one[:, :, None] - grouped_hat * mean_two[:, :, None])
    ).reshape(rows_local, model_width)
    summed = (
        lax.psum_scatter(grad_gn_gain, "seq", scatter_dimension=0, tiled=True),
        lax.psum_scatter(grad_gn_bias, "seq", scatter_dimension=0, tiled=True),
        lax.psum_scatter(grad_w_query, "seq", scatter_dimension=0, tiled=True),
        lax.psum_scatter(grad_q_bias, "seq", scatter_dimension=0, tiled=True),
        lax.psum_scatter(grad_w_key, "seq", scatter_dimension=0, tiled=True),
        lax.psum_scatter(grad_w_value, "seq", scatter_dimension=0, tiled=True),
        lax.psum_scatter(grad_v_bias, "seq", scatter_dimension=0, tiled=True),
        lax.psum_scatter(grad_w_out, "seq", scatter_dimension=0, tiled=True),
        lax.psum_scatter(grad_out_bias, "seq", scatter_dimension=0, tiled=True),
        lax.psum_scatter(grad_conv_weight, "seq", scatter_dimension=0, tiled=True),
        lax.psum_scatter(grad_conv_bias, "seq", scatter_dimension=0, tiled=True),
        lax.psum_scatter(grad_ln_gain, "seq", scatter_dimension=0, tiled=True),
        lax.psum_scatter(grad_ln_bias, "seq", scatter_dimension=0, tiled=True),
        lax.psum_scatter(grad_w_up, "seq", scatter_dimension=0, tiled=True),
        lax.psum_scatter(grad_up_bias, "seq", scatter_dimension=0, tiled=True),
        lax.psum_scatter(grad_w_down, "seq", scatter_dimension=0, tiled=True),
        lax.psum_scatter(grad_down_bias, "seq", scatter_dimension=0, tiled=True),
        lax.psum_scatter(grad_layer_scale, "seq", scatter_dimension=0, tiled=True),
    )
    return (
        output,
        frames_grad,
        summed[0],
        summed[1],
        summed[2],
        summed[3],
        summed[4],
        summed[5],
        summed[6],
        summed[7],
        summed[8],
        summed[9],
        summed[10],
        summed[11],
        summed[12],
        summed[13],
        summed[14],
        summed[15],
        summed[16],
        summed[17],
    )


def solution(mesh):
    return jax.shard_map(
        shards,
        mesh=mesh,
        in_specs=(
            P("seq", None),
            P(),
            P(),
            P(),
            P(None, "head"),
            P("head"),
            P(None, "head"),
            P(None, "head"),
            P("head"),
            P("head", None),
            P(),
            P(),
            P(),
            P(),
            P(),
            P(None, "head"),
            P("head"),
            P("head", None),
            P(),
            P(),
            P("seq", None),
        ),
        out_specs=(
            P("seq", None),
            P("seq", None),
            P("seq"),
            P("seq"),
            P("seq", "head"),
            P(("head", "seq")),
            P("seq", "head"),
            P("seq", "head"),
            P(("head", "seq")),
            P(("head", "seq"), None),
            P("seq"),
            P("seq", None),
            P("seq"),
            P("seq"),
            P("seq"),
            P("seq", "head"),
            P(("head", "seq")),
            P(("head", "seq"), None),
            P("seq"),
            P("seq"),
        ),
        check_vma=False,
    )
```

profile of v0, /device:TPU:0, one launch (start us, length us, event | category | flops | bytes accessed | tf_op | source)
XLA Modules:
  0.0 922.3 jit_solution(167993044335357667)
XLA Ops:
  11.1 34.9 %all-reduce.12 = (f32[3,32]{1,0:T(4,128)S(1)}, f32[3,32]{1,0:T(4,128)S(1)}) all-reduce(f32[3,32]{1,0:T(4,128)S(1)} %fusion.85, f32[3,32]{1,0:T(4,128)S(1)} %fusion.87), channel_id=1, replica_groups=mesh['seq'=16,'head'=2] {'seq'}, use_global_device_ids=true, to_apply=%region_6.7 | all-reduce | flops 192 | bytes 1536 | tf_op jit(solution)/shard_map/psum | solution.py:104
  50.1 2.3 copy.85
  53.7 2.1 convolution_convert_fusion.1
  55.9 2.1 fusion.33
  61.3 37.1 %all-gather.5.cloned.1.call-done = bf16[4096,384]{1,0:T(8,128)(2,1)} async-done(((bf16[256,384]{1,0:T(8,128)(2,1)}), bf16[4096,384]{1,0:T(8,128)(2,1)}) %all-gather.5.cloned.1.call-update) | async-done | bytes 3145744 | tf_op jit(solution)/shard_map/all_gather | solution.py:159
  98.5 4.7 copy.88
  103.2 12.2 %select_reduce_fusion = (f32[6,256]{1,0:T(8,128)S(1)}, f32[6,256,4096]{2,1,0:T(8,128)}) fusion(pred[256,4096]{1,0:T(8,128)(4,1)S(1)} %broadcast_compare_fusion.1, bf16[256,6,64]{0,2,1:T(8,128)(2,1)} %bitcast.112, bf16[4096,6,64]{0,2,1:T(8,128)(2,1)} %bitcast.98), kind=kOutput, calls=%fused_computation.4 | convolution fusion | flops 824179200 | bytes 29562880 | tf_op jit(solution)/shard_map/qhd,khd->hqk/dot_general | solution.py:129
  115.4 12.9 %fusion.1 = f32[6,256]{1,0:T(8,128)S(1)} fusion(f32[6,256,4096]{2,1,0:T(8,128)} %get-tuple-element.90, f32[6,256]{1,0:T(8,128)S(1)} %broadcast_maximum_fusion, pred[256,4096]{1,0:T(8,128)(4,1)S(1)} %broadcast_compare_fusion.1), kind=kLoop, calls=%fused_computation.6 | loop fusion | flops 31455744 | bytes 26226688 | tf_op jit(solution)/shard_map/reduce_sum | solution.py:141
  128.9 15.8 %all-gather.7.cloned.1.call-done = bf16[4096,384]{1,0:T(8,128)(2,1)} async-done(((bf16[256,384]{1,0:T(8,128)(2,1)}), bf16[4096,384]{1,0:T(8,128)(2,1)}) %all-gather.7.cloned.1.call-update) | async-done | bytes 3145744 | tf_op jit(solution)/shard_map/all_gather | solution.py:160
  144.8 4.7 copy.89
  149.5 13.8 %fusion.129 = (bf16[256,6,64]{0,2,1:T(8,128)(2,1)S(1)}, f32[256,6,64]{0,2,1:T(8,128)}) fusion(f32[256,6]{0,1:T(8,128)S(1)} %get-tuple-element.80, bf16[4096,6,64]{0,2,1:T(8,128)(2,1)} %bitcast.102, f32[6,256,4096]{2,1,0:T(8,128)} %get-tuple-element.90, f32[6,256]{1,0:T(8,128)S(1)} %broadcast_maximum_fusion, ...), kind=kOutput, calls=%fused_computation.203 | convolution fusion | flops 837058560 | bytes 29968384 | tf_op jit(solution)/shard_map/hqk,khd->hqd/dot_general | solution.py:142
  165.7 33.0 %all-reduce.18.cloned.1.call-done = f32[256,768]{1,0:T(8,128)} async-done(((f32[256,768]{1,0:T(8,128)}), f32[256,768]{1,0:T(8,128)}) %all-reduce.18.cloned.1.call-update) | async-done | bytes 786448 | tf_op jit(solution)/shard_map/psum | solution.py:169
  201.4 3.2 collective-permute-start
  205.3 2.0 fusion.126
  213.4 36.5 %all-reduce.20.cloned.1.call-done = f32[256,768]{1,0:T(8,128)} async-done(((f32[256,768]{1,0:T(8,128)}), f32[256,768]{1,0:T(8,128)}) %all-reduce.20.cloned.1.call-update) | async-done | bytes 786448 | tf_op jit(solution)/shard_map/psum | solution.py:206
  249.9 2.1 multiply_reduce_fusion
  252.1 3.8 multiply_reduce_fusion.1
  257.4 2.3 collective-permute-start.3
  263.8 5.6 convert_reduce_fusion.2
  270.2 2.1 convolution_convert_fusion
  272.5 2.7 broadcast_compare_fusion
  275.2 22.1 %all-gather.9.cloned.1.call-done = bf16[4096,384]{1,0:T(8,128)(2,1)} async-done(((bf16[256,384]{1,0:T(8,128)(2,1)}), bf16[4096,384]{1,0:T(8,128)(2,1)}) %all-gather.9.cloned.1.call-update) | async-done | bytes 3145744 | tf_op jit(solution)/shard_map/all_gather | solution.py:313
  297.3 4.8 copy.91
  302.1 21.2 %all_gather.23 = f32[4096,6]{0,1:T(8,128)} all-gather(f32[256,6]{0,1:T(8,128)} %get-tuple-element.79), channel_id=1, replica_groups=mesh['seq'=16,'head'=2] {'seq'}, dimensions={0}, use_global_device_ids=true | all-gather | bytes 104448 | tf_op jit(solution)/shard_map/all_gather | solution.py:315
  323.9 14.3 %fusion.133 = f32[6,4096,256]{2,1,0:T(8,128)} fusion(bf16[4096,6,64]{0,2,1:T(8,128)(2,1)} %bitcast.96, bf16[256,6,64]{0,2,1:T(8,128)(2,1)S(1)} %bitcast.111), kind=kOutput, calls=%fused_computation.207 | convolution fusion | flops 805306368 | bytes 28508160 | tf_op jit(solution)/shard_map/qhd,khd->hqk/dot_general | solution.py:286
  338.2 1.7 fusion.120
  341.2 19.2 %all_gather.25 = f32[4096,6]{0,1:T(8,128)} all-gather(f32[256,6]{0,1:T(8,128)S(1)} %multiply_reduce_fusion.14), channel_id=1, replica_groups=mesh['seq'=16,'head'=2] {'seq'}, dimensions={0}, use_global_device_ids=true | all-gather | bytes 104448 | tf_op jit(solution)/shard_map/all_gather | solution.py:316
  360.4 18.1 %convert_reduce_fusion.4 = (f32[6,64]{1,0:T(8,128)}, bf16[6,64,256]{2,1,0:T(8,128)(2,1)S(1)}) fusion(bf16[4096,6,64]{0,2,1:T(8,128)(2,1)} %bitcast.99, f32[6,256,4096]{2,1,0:T(8,128)} %get-tuple-element.90, f32[6,256]{1,0:T(8,128)S(1)} %bitcast.127, f32[6,256]{1,0:T(8,128)S(1)} %copy-done.86, pred[256,4096]{1,0:T(8,128)(4,1)} %copy-done.2, ...), kind=kOutput, calls=%fused_computation.117 | convolution fusion | flops 1648754304 | bytes 32912896 | tf_op jit(solution)/shard_map/hqk,khd->qhd/dot_general | solution.py:263
  378.9 4.8 copy.93
  383.7 12.0 %convert_reduce_fusion.3 = (f32[6,64]{1,0:T(8,128)}, bf16[6,64,256]{2,1,0:T(8,128)(2,1)S(1)}) fusion(bf16[4096,6,64]{0,2,1:T(8,128)(2,1)} %bitcast.104, f32[6,4096,256]{2,1,0:T(8,128)} %fusion.133, f32[6,4096]{1,0:T(8,128)S(1)} %bitcast.124, pred[4096,256]{1,0:T(8,128)(4,1)} %broadcast_compare_fusion), kind=kOutput, calls=%fused_computation.116 | convolution fusion | flops 830766720 | bytes 29656576 | tf_op jit(solution)/shard_map/hqk,qhd->khd/dot_general | solution.py:290
  395.7 16.8 %fusion.35 = bf16[6,64,256]{2,1,0:T(8,128)(2,1)S(1)} fusion(bf16[4096,6,64]{0,2,1:T(8,128)(2,1)} %bitcast.97, f32[6,4096,256]{2,1,0:T(8,128)} %fusion.133, f32[6,4096]{1,0:T(8,128)S(1)} %bitcast.126, f32[6,4096]{1,0:T(8,128)S(1)} %bitcast.125, pred[4096,256]{1,0:T(8,128)(4,1)} %broadcast_compare_fusion, bf16[4096,6,64]{0,2,1:T(8,128)(2,1)} %bitcast.105, ...), kind=kOutput, calls=%fused_computation.48 | convolution fusion | flops 1648558080 | bytes 33095680 | tf_op jit(solution)/shard_map/hqk,qhd->khd/dot_general | solution.py:302
  414.2 2.4 convolution_add_fusion.1
  419.1 47.7 %all-reduce.22.cloned.1.call-done = (f32[256,768]{1,0:T(8,128)}, f32[256,768]{1,0:T(8,128)}) async-done(((f32[256,768]{1,0:T(8,128)}, f32[256,768]{1,0:T(8,128)}), (f32[256,768]{1,0:T(8,128)}, f32[256,768]{1,0:T(8,128)})) %all-reduce.22.cloned.1.call-update) | async-done | bytes 1572880 | tf_op jit(solution)/shard_map/psum | solution.py:193
  466.8 3.5 fusion.65
  472.2 2.4 fusion.134
  476.3 3.4 fusion.121
  479.7 2.7 fusion.70
  482.6 2.5 fusion.135
  489.5 2.2 fusion.122
  494.1 61.5 %all-reduce.11 = (f32[3,32]{1,0:T(4,128)S(1)}, f32[3,32]{1,0:T(4,128)S(1)}, f32[768]{0:T(1024)S(1)}, f32[768]{0:T(1024)S(1)}, f32[384]{0:T(512)S(1)}, /*index=5*...) all-reduce(f32[3,32]{1,0:T(4,128)S(1)} %fusion.81, ...), channel_id=1, replica_groups=mesh['seq'=16,'head'=2] {'seq'}, use_global_device_ids=true, to_apply=%region_22.23 | all-reduce | flops 8256 | bytes 66048 | tf_op jit(solution)/shard_map/psum | solution.py:339
  558.4 2.4 copy.96
  567.2 3.3 multiply_add_fusion
  571.9 17.4 %reduce-scatter.10.cloned.1.call-done = f32[48,384]{1,0:T(8,128)} async-done(((f32[768,384]{1,0:T(8,128)}), f32[48,384]{1,0:T(8,128)}) %reduce-scatter.10.cloned.1.call-update) | async-done | bytes 73744 | tf_op jit(solution)/shard_map/reduce_scatter | solution.py:349
  589.3 61.2 %reduce-scatter.16.cloned.1.call-done = f32[24,768]{1,0:T(8,128)} async-done(((f32[384,768]{1,0:T(8,128)}), f32[24,768]{1,0:T(8,128)}) %reduce-scatter.16.cloned.1.call-update) | async-done | bytes 73744 | tf_op jit(solution)/shard_map/reduce_scatter | solution.py:354
  650.5 71.5 %reduce-scatter.18.cloned.1.call-done = f32[48,1152]{1,0:T(8,128)} async-done(((f32[768,1152]{1,0:T(8,128)}), f32[48,1152]{1,0:T(8,128)}) %reduce-scatter.18.cloned.1.call-update) | async-done | bytes 221200 | tf_op jit(solution)/shard_map/reduce_scatter | solution.py:360
  722.0 71.3 %reduce-scatter.20.cloned.1.call-done = f32[72,768]{1,0:T(8,128)} async-done(((f32[1152,768]{1,0:T(8,128)}), f32[72,768]{1,0:T(8,128)}) %reduce-scatter.20.cloned.1.call-update) | async-done | bytes 221200 | tf_op jit(solution)/shard_map/reduce_scatter | solution.py:362
  793.2 61.2 %reduce-scatter.12.cloned.1.call-done = f32[48,384]{1,0:T(8,128)} async-done(((f32[768,384]{1,0:T(8,128)}), f32[48,384]{1,0:T(8,128)}) %reduce-scatter.12.cloned.1.call-update) | async-done | bytes 73744 | tf_op jit(solution)/shard_map/reduce_scatter | solution.py:351
  854.4 61.2 %reduce-scatter.14.cloned.1.call-done = f32[48,384]{1,0:T(8,128)} async-done(((f32[768,384]{1,0:T(8,128)}), f32[48,384]{1,0:T(8,128)}) %reduce-scatter.14.cloned.1.call-update) | async-done | bytes 73744 | tf_op jit(solution)/shard_map/reduce_scatter | solution.py:352
  (317 shorter events, 56.1 us)
Async XLA Ops:
  7.2 201.4 %copy-start = (bf16[1152,768]{1,0:T(8,128)(2,1)S(1)}, bf16[1152,768]{1,0:T(8,128)(2,1)}, u32[]{:S(2)}) copy-start(bf16[1152,768]{1,0:T(8,128)(2,1)} %param.38) | copy-start | bytes 5308420
  7.2 91.3 %all-gather.5.cloned.1.call-start = ((), (), s32[]{:S(2)}) async-start(), calls=%async_computation.7 | async-start | bytes 3342336 | tf_op jit(solution)/shard_map/all_gather | solution.py:159
  8.6 43.8 %copy-start.10 = (bf16[256,768]{1,0:T(8,128)(2,1)S(1)}, bf16[256,768]{1,0:T(8,128)(2,1)}, u32[]{:S(2)}) copy-start(bf16[256,768]{1,0:T(8,128)(2,1)} %param.21) | copy-start | bytes 1179652
  8.6 43.8 %copy-start.84 = (f32[768]{0:T(1024)S(1)}, f32[768]{0:T(1024)}, u32[]{:S(2)}) copy-start(f32[768]{0:T(1024)} %param.23) | copy-start | bytes 9220
  8.6 43.8 %copy-start.90 = (f32[768]{0:T(1024)S(1)}, f32[768]{0:T(1024)}, u32[]{:S(2)}) copy-start(f32[768]{0:T(1024)} %param.24) | copy-start | bytes 9220
  9.7 40.4 %copy-start.100 = (f32[3]{0:T(128)}, f32[3]{0:T(128)S(1)}, u32[]{:S(2)}) copy-start(f32[3]{0:T(128)S(1)} %multiply_convert_fusion.13) | copy-start | bytes 40
  10.5 39.6 %copy-start.88 = (s32[3,1]{0,1:T(1,128)}, s32[3,1]{0,1:T(1,128)S(1)}, u32[]{:S(2)}) copy-start(s32[3,1]{0,1:T(1,128)S(1)} %reduce-window.8) | copy-start | bytes 40
  55.8 88.9 %all-gather.7.cloned.1.call-start = ((), (), s32[]{:S(2)}) async-start(), calls=%async_computation.8 | async-start | bytes 3342336 | tf_op jit(solution)/shard_map/all_gather | solution.py:160
  58.0 140.6 %all-reduce.18.cloned.1.call-start = ((), (), s32[]{:S(2)}) async-start(), calls=%async_computation.9 | async-start | bytes 1572864 | tf_op jit(solution)/shard_map/psum | solution.py:169
  59.7 43.5 %copy-start.21 = (bf16[256,384]{1,0:T(8,128)(2,1)}, bf16[256,384]{1,0:T(8,128)(2,1)S(1)}, u32[]{:S(2)}) copy-start(bf16[256,384]{1,0:T(8,128)(2,1)S(1)} %fusion.32) | copy-start | bytes 589828
  61.3 88.2 %copy-start.2 = (pred[256,4096]{1,0:T(8,128)(4,1)}, pred[256,4096]{1,0:T(8,128)(4,1)S(1)}, u32[]{:S(2)}) copy-start(pred[256,4096]{1,0:T(8,128)(4,1)S(1)} %broadcast_compare_fusion.1) | copy-start | bytes 3145732
  149.5 49.1 %copy-start.91 = (f32[768]{0:T(1024)S(1)}, f32[768]{0:T(1024)}, u32[]{:S(2)}) copy-start(f32[768]{0:T(1024)} %param.31) | copy-start | bytes 9220
  163.4 41.3 %copy-start.57 = (f32[768,7]{0,1:T(8,128)S(1)}, f32[768,7]{0,1:T(8,128)}, u32[]{:S(2)}) copy-start(f32[768,7]{0,1:T(8,128)} %param.32) | copy-start | bytes 64516
  163.4 41.9 %copy-start.92 = (f32[768]{0:T(1024)S(1)}, f32[768]{0:T(1024)}, u32[]{:S(2)}) copy-start(f32[768]{0:T(1024)} %param.33) | copy-start | bytes 9220
  164.1 43.5 %copy-start.46 = (f32[768]{0:T(1024)S(1)}, f32[768]{0:T(1024)}, u32[]{:S(2)}) copy-start(f32[768]{0:T(1024)} %param.34) | copy-start | bytes 9220
  164.1 43.5 %copy-start.93 = (f32[768]{0:T(1024)S(1)}, f32[768]{0:T(1024)}, u32[]{:S(2)}) copy-start(f32[768]{0:T(1024)} %param.35) | copy-start | bytes 9220
  164.1 43.5 %copy-start.98 = (f32[1152]{0:T(1024)S(1)}, f32[1152]{0:T(1024)}, u32[]{:S(2)}) copy-start(f32[1152]{0:T(1024)} %param.37) | copy-start | bytes 13828
  165.4 84.6 %all-reduce.20.cloned.1.call-start = ((), (), s32[]{:S(2)}) async-start(), calls=%async_computation.10 | async-start | bytes 1572864 | tf_op jit(solution)/shard_map/psum | solution.py:206
  165.6 42.8 %copy-start.58 = (f32[256]{0:T(256)}, f32[256]{0:T(256)S(1)}, u32[]{:S(2)}) copy-start(f32[256]{0:T(256)S(1)} %get-tuple-element.82) | copy-start | bytes 3076
  165.6 42.8 %copy-start.60 = (f32[256]{0:T(256)}, f32[256]{0:T(256)S(1)}, u32[]{:S(2)}) copy-start(f32[256]{0:T(256)S(1)} %get-tuple-element.87) | copy-start | bytes 3076
  165.6 42.8 %copy-start.61 = (f32[256]{0:T(256)}, f32[256]{0:T(256)S(1)}, u32[]{:S(2)}) copy-start(f32[256]{0:T(256)S(1)} %get-tuple-element.88) | copy-start | bytes 3076
  165.6 42.8 %copy-start.64 = (f32[256]{0:T(256)}, f32[256]{0:T(256)S(1)}, u32[]{:S(2)}) copy-start(f32[256]{0:T(256)S(1)} %get-tuple-element.83) | copy-start | bytes 3076
  165.6 42.8 %copy-start.65 = (f32[256]{0:T(256)}, f32[256]{0:T(256)S(1)}, u32[]{:S(2)}) copy-start(f32[256]{0:T(256)S(1)} %get-tuple-element.84) | copy-start | bytes 3076
  165.6 42.8 %copy-start.66 = (f32[256]{0:T(256)}, f32[256]{0:T(256)S(1)}, u32[]{:S(2)}) copy-start(f32[256]{0:T(256)S(1)} %get-tuple-element.85) | copy-start | bytes 3076
  165.6 42.8 %copy-start.67 = (f32[256]{0:T(256)}, f32[256]{0:T(256)S(1)}, u32[]{:S(2)}) copy-start(f32[256]{0:T(256)S(1)} %get-tuple-element.86) | copy-start | bytes 3076
  200.1 4.7 collective-permute-start.1
  201.4 3.9 collective-permute-start
  212.8 48.2 %copy-start.22 = (bf16[256,384]{1,0:T(8,128)(2,1)S(1)}, bf16[256,384]{1,0:T(8,128)(2,1)}, u32[]{:S(2)}) copy-start(bf16[256,384]{1,0:T(8,128)(2,1)} %convolution_convert_fusion.1) | copy-start | bytes 589828
  212.8 84.5 %all-gather.9.cloned.1.call-start = ((), (), s32[]{:S(2)}) async-start(), calls=%async_computation.11 | async-start | bytes 3342336 | tf_op jit(solution)/shard_map/all_gather | solution.py:313
  213.4 165.6 %all-gather.11.cloned.1.call-start = ((), (), s32[]{:S(2)}) async-start(), calls=%async_computation.12 | async-start | bytes 3342336 | tf_op jit(solution)/shard_map/all_gather | solution.py:314
  257.4 6.2 collective-permute-start.3
  259.7 4.1 collective-permute-start.2
  272.4 194.4 %all-reduce.22.cloned.1.call-start = ((), (), s32[]{:S(2)}) async-start(), calls=%async_computation.20 | async-start | bytes 3145728 | tf_op jit(solution)/shard_map/psum | solution.py:193
  275.2 48.1 %copy-start.40 = (f32[6,256]{1,0:T(8,128)S(1)}, f32[6,256]{1,0:T(8,128)}, u32[]{:S(2)}) copy-start(f32[6,256]{1,0:T(8,128)} %copy-done.39) | copy-start | bytes 18436
  275.2 48.1 %copy-start.42 = (f32[6,256]{1,0:T(8,128)S(1)}, f32[6,256]{1,0:T(8,128)}, u32[]{:S(2)}) copy-start(f32[6,256]{1,0:T(8,128)} %copy-done.41) | copy-start | bytes 18436
  275.2 48.7 %copy-start.24 = (bf16[256,384]{0,1:T(8,128)(2,1)S(1)}, bf16[256,384]{0,1:T(8,128)(2,1)}, u32[]{:S(2)}) copy-start(bf16[256,384]{0,1:T(8,128)(2,1)} %copy.92) | copy-start | bytes 589828
  412.5 54.3 %copy-start.4 = (f32[256,768]{1,0:T(8,128)S(1)}, f32[256,768]{1,0:T(8,128)}, u32[]{:S(2)}) copy-start(f32[256,768]{1,0:T(8,128)} %copy-done.3) | copy-start | bytes 2359300
  412.5 54.3 %copy-start.44 = (f32[3,768]{1,0:T(4,128)S(1)}, f32[3,768]{1,0:T(4,128)}, u32[]{:S(2)}) copy-start(f32[3,768]{1,0:T(4,128)} %copy-done.43) | copy-start | bytes 27652
  412.5 54.3 %copy-start.59 = (f32[256]{0:T(256)S(1)}, f32[256]{0:T(256)}, u32[]{:S(2)}) copy-start(f32[256]{0:T(256)} %copy-done.58) | copy-start | bytes 3076
  416.6 154.0 %reduce-scatter.22.cloned.1.call-start = ((), (), s32[]{:S(2)}) async-start(), calls=%async_computation.19 | async-start | bytes 417792
  472.1 117.2 %reduce-scatter.10.cloned.1.call-start = ((), (), s32[]{:S(2)}) async-start(), calls=%async_computation.13 | async-start | bytes 1253376 | tf_op jit(solution)/shard_map/reduce_scatter | solution.py:349
  474.6 175.8 %reduce-scatter.16.cloned.1.call-start = ((), (), s32[]{:S(2)}) async-start(), calls=%async_computation.16 | async-start | bytes 1253376 | tf_op jit(solution)/shard_map/reduce_scatter | solution.py:354
  476.2 245.8 %reduce-scatter.18.cloned.1.call-start = ((), (), s32[]{:S(2)}) async-start(), calls=%async_computation.17 | async-start | bytes 3760128 | tf_op jit(solution)/shard_map/reduce_scatter | solution.py:360
  479.6 313.6 %reduce-scatter.20.cloned.1.call-start = ((), (), s32[]{:S(2)}) async-start(), calls=%async_computation.18 | async-start | bytes 3760128 | tf_op jit(solution)/shard_map/reduce_scatter | solution.py:362
  482.6 371.9 %reduce-scatter.12.cloned.1.call-start = ((), (), s32[]{:S(2)}) async-start(), calls=%async_computation.14 | async-start | bytes 1253376 | tf_op jit(solution)/shard_map/reduce_scatter | solution.py:351
  485.1 430.5 %reduce-scatter.14.cloned.1.call-start = ((), (), s32[]{:S(2)}) async-start(), calls=%async_computation.15 | async-start | bytes 1253376 | tf_op jit(solution)/shard_map/reduce_scatter | solution.py:352
  489.4 66.2 %copy-start.101 = (f32[3]{0:T(128)S(1)}, f32[3]{0:T(128)}, u32[]{:S(2)}) copy-start(f32[3]{0:T(128)} %copy-done.100) | copy-start | bytes 40
  558.4 357.2 %copy-start.1 = (bf16[1152,768]{1,0:T(8,128)(2,1)S(1)}, bf16[1152,768]{1,0:T(8,128)(2,1)}, u32[]{:S(2)}) copy-start(bf16[1152,768]{1,0:T(8,128)(2,1)} %param.38) | copy-start | bytes 5308420
  (72 other events, 495.8 us)
Sparse Core Ops, SparseCore 0:
  56.0 42.4 all-gather.4
  100.7 43.9 all-gather.6
  165.5 33.1 all-reduce.17
  212.9 36.9 all-reduce.19
  252.1 45.1 all-gather.8
  300.0 44.4 all-gather.10
  416.7 50.0 all-reduce.21
  472.2 55.6 reduce-scatter.21
  532.1 57.1 reduce-scatter.9
  593.4 57.0 reduce-scatter.15
  654.9 66.9 reduce-scatter.17
  726.3 66.9 reduce-scatter.19
  797.4 56.9 reduce-scatter.11
  858.5 57.1 reduce-scatter.13
where the time goes:
time: 926 us; the launch traced here: 922 us
  waiting for transfers between devices  537 us (58%)
  blocking collectives  137 us (15%)
  matrix products  123 us (13%)
  local copies, waits for them, and re-layouts  52.5 us (6%)
  other arithmetic  46.5 us (5%)
  between operations  17.4 us (2%)
    reduce_scatter x1, waiting for transfers between devices, shards(): lax.psum_scatter(grad_w_up, 'seq', scatter_dimension=0, tiled=True)  71.5 us
    reduce_scatter x1, waiting for transfers between devices, shards(): lax.psum_scatter(grad_w_down, 'seq', scatter_dimension=0, tiled=True)  71.3 us
    psum x1, blocking collectives, shards(): part_one, part_two = lax.psum((part_one, part_two), 'seq')  61.5 us
    reduce_scatter x1, waiting for transfers between devices, shards(): lax.psum_scatter(grad_w_value, 'seq', scatter_dimension=0, tiled=True)  61.2 us
    reduce_scatter x1, waiting for transfers between devices, shards(): lax.psum_scatter(grad_w_key, 'seq', scatter_dimension=0, tiled=True)  61.2 us
    reduce_scatter x1, waiting for transfers between devices, shards(): lax.psum_scatter(grad_w_out, 'seq', scatter_dimension=0, tiled=True)  61.2 us
    psum x1, waiting for transfers between devices, shards(): lax.psum(jnp.dot(act_low, w_down, preferred_element_type=jnp.float32), 'h...  47.7 us
    all_gather x1, waiting for transfers between devices, shards(): lax.all_gather(keys, 'seq', axis=0, tiled=True)  37.1 us
  transfers between devices with their start and end apart: 18, of which 14 were waited for; matrix products, arithmetic and copies ran while one was open for 15% of the time, Pallas kernels for 0%

commit v1 on v0

v1 whole, which is shorter than its diff:
```python
import functools

import jax
import jax.numpy as jnp
from jax import lax
from jax.experimental import pallas as pl
from jax.experimental.pallas import tpu as pltpu
from jax.sharding import PartitionSpec as P

HEAD_DIM = 64
GROUPS = 32
KERNEL = 7
CLIPS = 3
SPANS = 8
LANES = 128
HALO = 8
RESIDENT = 8192
EPS = 1e-6
FAR = -1e30
HIGHEST = lax.Precision.HIGHEST
F32 = jnp.float32
BF16 = jnp.bfloat16
MESH = pl.DeviceIdType.MESH


def iota(shape, dim):
    return lax.broadcasted_iota(jnp.int32, shape, dim)


def dot(a, b, dims=((1,), (0,)), precision=None):
    return lax.dot_general(a, b, (dims, ((), ())), precision=precision, preferred_element_type=F32)


def clip_of(pos, lengths_ref):
    end = jnp.int32(0)
    seg = jnp.zeros(pos.shape, jnp.int32)
    for c in range(CLIPS):
        end = end + lengths_ref[c]
        seg = seg + (pos >= end).astype(jnp.int32)
    return seg


def row_of(ref):
    return ref[...].reshape(1, ref.shape[0])


def arrived(ref, sem):
    pltpu.make_async_copy(ref, ref, sem).wait()


def greet_all(seq, head, n_seq, n_head):
    barrier = pltpu.get_barrier_semaphore()
    count = n_seq * n_head

    def hail(i, carry):
        other = lax.rem(seq * n_head + head + i, count)
        pl.semaphore_signal(
            barrier, inc=1, device_id=(other // n_head, lax.rem(other, n_head)), device_id_type=MESH
        )
        return carry

    lax.fori_loop(1, count, hail, 0)
    return lambda: pl.semaphore_wait(barrier, count - 1)


def group_matrix(width):
    channel = iota((width, LANES), 0)
    first = iota((width, LANES), 1) * (width // GROUPS)
    return ((channel >= first) & (channel < first + width // GROUPS)).astype(F32)


def by_clip(rows_clip, table, first):
    out = table[first + CLIPS - 1 : first + CLIPS, :]
    for c in range(CLIPS - 2, -1, -1):
        out = jnp.where(rows_clip == c, table[first + c : first + c + 1, :], out)
    return out


def members_of(lengths_ref, width):
    row = iota((HALO, 1), 0)
    out = jnp.ones((HALO, 1), F32)
    for c in range(CLIPS):
        count = (lengths_ref[c] * (width // GROUPS)).astype(F32)
        out = jnp.where((row == c) | (row == c + CLIPS), count, out)
    return out


def forward_kernel(
    n_seq,
    n_head,
    lengths_ref,
    frames_ref,
    gain_ref,
    bias_ref,
    wq_ref,
    qb_ref,
    wk_ref,
    wv_ref,
    vb_ref,
    wout_ref,
    outb_ref,
    hidden_ref,
    rim_ref,
    att_ref,
    stat_ref,
    kv_out,
    kvt_out,
    qt_out,
    ot_out,
    lse_out,
    stats,
    other_wout,
    kv_send,
    qt_send,
    kv,
    kvt,
    qt,
    ot,
    lse,
    att_send,
    att_recv,
    rim,
    stat_ssem,
    stat_rsem,
    wout_sem,
    kv_ssem,
    kv_rsem,
    qt_ssem,
    qt_rsem,
    att_ssem,
    att_rsem,
    rim_sem,
    keep_sem,
):
    seq = lax.axis_index("seq")
    head = lax.axis_index("head")
    rows, width = frames_ref.shape
    heads = wq_ref.shape[1] // HEAD_DIM
    per_head = n_seq // SPANS
    offset = (SPANS - heads) // 2
    total = n_seq * rows
    met = greet_all(seq, head, n_seq, n_head)

    x = frames_ref[...].astype(F32)
    rows_clip = clip_of(seq * rows + iota((rows, 1), 0), lengths_ref)
    sums = []
    for member in (x, x * x):
        for c in range(CLIPS):
            sums.append(jnp.sum(jnp.where(rows_clip == c, member, 0.0), axis=0, keepdims=True))
    sums.append(jnp.zeros((HALO - 2 * CLIPS, width), F32))
    groups = group_matrix(width)
    stats[seq] = dot(jnp.concatenate(sums, axis=0), groups, precision=HIGHEST)
    met()

    def give_stats(i, carry):
        other = lax.rem(seq + i, n_seq)
        pltpu.make_async_remote_copy(
            src_ref=stats.at[seq],
            dst_ref=stats.at[seq],
            send_sem=stat_ssem.at[i],
            recv_sem=stat_rsem.at[seq],
            device_id=(other, head),
            device_id_type=MESH,
        ).start()
        return carry

    lax.fori_loop(1, n_seq, give_stats, 0)
    wout_copy = pltpu.make_async_remote_copy(
        src_ref=wout_ref,
        dst_ref=other_wout,
        send_sem=wout_sem.at[0],
        recv_sem=wout_sem.at[1],
        device_id=(seq, 1 - head),
        device_id_type=MESH,
    )
    wout_copy.start()

    def key_marks(i, carry):
        place = pl.ds(pl.multiple_of(i * rows, rows), rows)
        lane = iota((rows, LANES), 1)
        clip = clip_of(i * rows + iota((rows, 1), 0), lengths_ref)
        marks = (clip == lane) | ((lane >= CLIPS) & (lane < CLIPS + 3))
        kv[place, LANES : 2 * LANES] = marks.astype(F32).astype(BF16)
        return carry

    lax.fori_loop(0, n_seq, key_marks, 0)

    def take_stats(i, carry):
        other = lax.rem(seq + i, n_seq)
        arrived(stats.at[other], stat_rsem.at[other])
        return carry

    lax.fori_loop(1, n_seq, take_stats, 0)
    summed = lax.fori_loop(
        0, n_seq, lambda i, acc: acc + stats[i], jnp.zeros((HALO, LANES), F32)
    ) / members_of(lengths_ref, width)
    mean = summed[0:CLIPS]
    rstd = lax.rsqrt(summed[CLIPS : 2 * CLIPS] - mean * mean + EPS)
    table = dot(
        jnp.concatenate([mean, rstd, jnp.zeros((HALO - 2 * CLIPS, LANES), F32)], axis=0),
        groups,
        ((1,), (1,)),
        HIGHEST,
    )
    stat_ref[...] = table
    hat = (x - by_clip(rows_clip, table, 0)) * by_clip(rows_clip, table, CLIPS)
    normed = (hat * row_of(gain_ref) + row_of(bias_ref)).astype(BF16)

    def give_kv(i, carry):
        h = i // per_head
        dest = i + offset * per_head
        place = pl.ds(pl.multiple_of(seq * rows, rows), rows)
        source = kv_send.at[h]
        target = kv.at[place, 0:LANES]

        @pl.when(dest != seq)
        def _():
            pltpu.make_async_remote_copy(
                src_ref=source,
                dst_ref=target,
                send_sem=kv_ssem.at[i],
                recv_sem=kv_rsem.at[seq],
                device_id=(dest, head),
                device_id_type=MESH,
            ).start()

        @pl.when(dest == seq)
        def _():
            pltpu.make_async_copy(source, target, kv_rsem.at[seq]).start()

        return carry

    def give_q(h, carry):
        dest = (h + offset) * per_head + seq // SPANS
        tile = lax.rem(seq, SPANS)
        source = qt_send.at[h]
        target = qt.at[tile]

        @pl.when(dest != seq)
        def _():
            pltpu.make_async_remote_copy(
                src_ref=source,
                dst_ref=target,
                send_sem=qt_ssem.at[h],
                recv_sem=qt_rsem.at[tile],
                device_id=(dest, head),
                device_id_type=MESH,
            ).start()

        @pl.when(dest == seq)
        def _():
            pltpu.make_async_copy(source, target, qt_rsem.at[tile]).start()

        return carry

    k_all = dot(normed, wk_ref[...])
    v_all = dot(normed, wv_ref[...]) + row_of(vb_ref)
    for h in range(heads):
        lanes = slice(HEAD_DIM * h, HEAD_DIM * (h + 1))
        kv_send[h] = jnp.concatenate([k_all[:, lanes], v_all[:, lanes]], axis=1).astype(BF16)
    lax.fori_loop(0, heads * per_head, give_kv, 0)
    q_all = (dot(normed, wq_ref[...]) + row_of(qb_ref)).astype(BF16).astype(F32) * HEAD_DIM**-0.5
    q_flip = q_all.T.astype(BF16)
    for h in range(heads):
        qt_send[h] = q_flip[HEAD_DIM * h : HEAD_DIM * (h + 1), :]
    lax.fori_loop(0, heads, give_q, 0)

    span = seq // per_head
    active = (span >= offset) & (span < offset + heads)
    own_head = span - offset
    part = lax.rem(seq, per_head)
    chunk = min(total, 1024)

    def give_att(t, carry):
        home = part * SPANS + t
        for side in range(n_head):
            source = att_send.at[t]
            target = att_recv.at[side, own_head]
            sem = att_rsem.at[side, own_head]

            def far():
                pltpu.make_async_remote_copy(
                    src_ref=source,
                    dst_ref=target,
                    send_sem=att_ssem.at[side, t],
                    recv_sem=sem,
                    device_id=(home, head if side == 0 else 1 - head),
                    device_id_type=MESH,
                ).start()

            if side == 0:
                pl.when(home != seq)(far)

                @pl.when(home == seq)
                def _():
                    pltpu.make_async_copy(source, target, sem).start()
            else:
                far()
        return carry

    @pl.when(active)
    def _():
        def take_kv(i, carry):
            place = pl.ds(pl.multiple_of(i * rows, rows), rows)
            arrived(kv.at[place, 0:LANES], kv_rsem.at[i])
            kvt[:, place] = kv[place, 0:LANES].astype(F32).T.astype(BF16)
            return carry

        lax.fori_loop(0, n_seq, take_kv, 0)

        def take_q(t, carry):
            arrived(qt.at[t], qt_rsem.at[t])
            return carry

        lax.fori_loop(0, SPANS, take_q, 0)
        keep = [
            pltpu.make_async_copy(kv, kv_out, keep_sem.at[0]),
            pltpu.make_async_copy(kvt.at[0:HEAD_DIM], kvt_out, keep_sem.at[1]),
            pltpu.make_async_copy(qt, qt_out, keep_sem.at[2]),
        ]
        for copy in keep:
            copy.start()

        def tile(t, carry):
            queries = query_block(qt[t], part * SPANS * rows + t * rows, lengths_ref, None)

            def step(c, state):
                top, norm, acc = state
                place = pl.ds(pl.multiple_of(c * chunk, chunk), chunk)
                scores = dot(kv[place, :], queries)
                new_top = jnp.maximum(top, jnp.max(scores, axis=0, keepdims=True))
                weights = jnp.exp(scores - new_top)
                factor = jnp.exp(top - new_top)
                norm = norm * factor + jnp.sum(weights, axis=0, keepdims=True)
                acc = acc * factor + dot(kvt[HEAD_DIM:, place], weights.astype(BF16))
                return new_top, norm, acc

            state = (
                jnp.full((1, rows), FAR, F32),
                jnp.zeros((1, rows), F32),
                jnp.zeros((HEAD_DIM, rows), F32),
            )
            steps = total // chunk
            top, norm, acc = lax.fori_loop(0, steps, step, state, unroll=steps <= 4)
            result = acc / norm
            ot[t] = result
            lse[t] = jnp.broadcast_to(top + jnp.log(norm), (HALO, rows))
            att_send[t] = result.astype(BF16)
            give_att(t, 0)
            return carry

        lax.fori_loop(0, SPANS, tile, 0)
        keep2 = [
            pltpu.make_async_copy(ot, ot_out, keep_sem.at[3]),
            pltpu.make_async_copy(lse, lse_out, keep_sem.at[4]),
        ]
        for copy in keep2:
            copy.start()
        for copy in keep + keep2:
            copy.wait()

    wout_copy.wait()
    attended = []
    for side in range(n_head):
        for h in range(heads):
            arrived(att_recv.at[side, h], att_rsem.at[side, h])
        attended.append(att_recv[side].reshape(heads * HEAD_DIM, rows))
    att_ref[...] = attended[0]
    branch = dot(attended[0].astype(F32).T.astype(BF16), wout_ref[...]) + dot(
        attended[1].astype(F32).T.astype(BF16), other_wout[...]
    )
    hidden = x + (branch + row_of(outb_ref))
    hidden_ref[...] = hidden
    rim[0] = hidden[0:HALO]
    rim[1] = hidden[rows - HALO : rows]
    swap_rims(seq, head, n_seq, rim, rim_sem)
    rim_ref[...] = rim[2:4]

    def sent_stats(i, carry):
        arrived(stats.at[seq], stat_ssem.at[i])
        return carry

    lax.fori_loop(1, n_seq, sent_stats, 0)

    def sent_kv(i, carry):
        @pl.when(i + offset * per_head != seq)
        def _():
            arrived(kv_send.at[i // per_head], kv_ssem.at[i])

        return carry

    lax.fori_loop(0, heads * per_head, sent_kv, 0)

    def sent_q(h, carry):
        @pl.when((h + offset) * per_head + seq // SPANS != seq)
        def _():
            arrived(qt_send.at[h], qt_ssem.at[h])

        return carry

    lax.fori_loop(0, heads, sent_q, 0)

    @pl.when(active)
    def _():
        def sent_att(t, carry):
            @pl.when(part * SPANS + t != seq)
            def _():
                arrived(att_send.at[t], att_ssem.at[0, t])

            arrived(att_send.at[t], att_ssem.at[1, t])
            return carry

        lax.fori_loop(0, SPANS, sent_att, 0)


def swap_rims(seq, head, n_seq, rim, rim_sem):
    @pl.when(seq > 0)
    def _():
        pltpu.make_async_remote_copy(
            src_ref=rim.at[0],
            dst_ref=rim.at[3],
            send_sem=rim_sem.at[0],
            recv_sem=rim_sem.at[3],
            device_id=(seq - 1, head),
            device_id_type=MESH,
        ).start()

    @pl.when(seq < n_seq - 1)
    def _():
        pltpu.make_async_remote_copy(
            src_ref=rim.at[1],
            dst_ref=rim.at[2],
            send_sem=rim_sem.at[1],
            recv_sem=rim_sem.at[2],
            device_id=(seq + 1, head),
            device_id_type=MESH,
        ).start()

    @pl.when(seq == 0)
    def _():
        rim[2] = jnp.zeros(rim.shape[1:], rim.dtype)

    @pl.when(seq == n_seq - 1)
    def _():
        rim[3] = jnp.zeros(rim.shape[1:], rim.dtype)

    @pl.when(seq > 0)
    def _():
        arrived(rim.at[0], rim_sem.at[0])
        arrived(rim.at[2], rim_sem.at[2])

    @pl.when(seq < n_seq - 1)
    def _():
        arrived(rim.at[1], rim_sem.at[1])
        arrived(rim.at[3], rim_sem.at[3])


def thirds(row):
    high = row.astype(BF16).astype(F32)
    middle = (row - high).astype(BF16).astype(F32)
    return high, middle, row - high - middle


def query_block(block, first, lengths_ref, total):
    rows = block.shape[1]
    clip = clip_of(first + iota((1, rows), 1), lengths_ref)
    row = iota((LANES, rows), 0)
    marks = jnp.where((row < CLIPS) & (row != clip), FAR, 0.0)
    if total is not None:
        for i, third in enumerate(thirds(total)):
            marks = jnp.where(row == CLIPS + i, -third, marks)
    return jnp.concatenate(
        [block, jnp.zeros((LANES - HEAD_DIM, rows), BF16), marks.astype(BF16)], axis=0
    )


def vmem(n):
    return [pl.BlockSpec(memory_space=pltpu.VMEM)] * n


def forward(n_seq, n_head, lengths, frames, gain, bias, wq, qb, wk, wv, vb, wout, outb):
    rows, width = frames.shape
    heads = wq.shape[1] // HEAD_DIM
    total = n_seq * rows
    per_head = n_seq // SPANS
    dma = pltpu.SemaphoreType.DMA
    shape = jax.ShapeDtypeStruct
    return pl.pallas_call(
        functools.partial(forward_kernel, n_seq, n_head),
        name="forward",
        out_shape=(
            shape((rows, width), F32),
            shape((2, HALO, width), F32),
            shape((heads * HEAD_DIM, rows), BF16),
            shape((HALO, width), F32),
            shape((total, 2 * LANES), BF16),
            shape((HEAD_DIM, total), BF16),
            shape((SPANS, HEAD_DIM, rows), BF16),
            shape((SPANS, HEAD_DIM, rows), F32),
            shape((SPANS, HALO, rows), F32),
        ),
        in_specs=[pl.BlockSpec(memory_space=pltpu.SMEM)] + vmem(10),
        out_specs=tuple(vmem(4) + [pl.BlockSpec(memory_space=pl.ANY)] * 5),
        scratch_shapes=[
            pltpu.VMEM((n_seq, HALO, LANES), F32),
            pltpu.VMEM(wout.shape, BF16),
            pltpu.VMEM((heads, rows, LANES), BF16),
            pltpu.VMEM((heads, HEAD_DIM, rows), BF16),
            pltpu.VMEM((total, 2 * LANES), BF16),
            pltpu.VMEM((LANES, total), BF16),
            pltpu.VMEM((SPANS, HEAD_DIM, rows), BF16),
            pltpu.VMEM((SPANS, HEAD_DIM, rows), F32),
            pltpu.VMEM((SPANS, HALO, rows), F32),
            pltpu.VMEM((SPANS, HEAD_DIM, rows), BF16),
            pltpu.VMEM((n_head, heads, HEAD_DIM, rows), BF16),
            pltpu.VMEM((4, HALO, width), F32),
            dma((n_seq,)),
            dma((n_seq,)),
            dma((2,)),
            dma((heads * per_head,)),
            dma((n_seq,)),
            dma((heads,)),
            dma((SPANS,)),
            dma((n_head, SPANS)),
            dma((n_head, heads)),
            dma((4,)),
            dma((5,)),
        ],
        compiler_params=pltpu.CompilerParams(
            collective_id=0, has_side_effects=True, vmem_limit_bytes=56 * 2**20
        ),
    )(lengths, frames, gain, bias, wq, qb, wk, wv, vb, wout, outb)


def middle_kernel(
    n_seq,
    n_head,
    lengths_ref,
    hidden_ref,
    rims_ref,
    cot_ref,
    att_ref,
    wout_ref,
    convw_ref,
    convb_ref,
    lng_ref,
    lnb_ref,
    wup_ref,
    upb_ref,
    wdown_ref,
    downb_ref,
    scale_ref,
    out_ref,
    hgrad_ref,
    dot_ref,
    ga_ref,
    gb_ref,
    vec_ref,
    upvec_ref,
    padded,
    gdown,
    ln_own,
    ln_other,
    proj_own,
    proj_other,
    rim,
    swap_sem,
    rim_sem,
):
    seq = lax.axis_index("seq")
    head = lax.axis_index("head")
    rows, width = hidden_ref.shape
    hidden_units = wup_ref.shape[1]
    half = KERNEL // 2
    total = n_seq * rows
    barrier = pltpu.get_barrier_semaphore()

    def hail(where):
        pl.semaphore_signal(barrier, inc=1, device_id=where, device_id_type=MESH)

    hail((seq, 1 - head))
    pl.when(seq > 0)(lambda: hail((seq - 1, head)))
    pl.when(seq < n_seq - 1)(lambda: hail((seq + 1, head)))

    pos = seq * rows + iota((rows, 1), 0)
    own_clip = clip_of(pos, lengths_ref)
    masks = []
    for k in range(KERNEL):
        there = pos + (k - half)
        same = (clip_of(there, lengths_ref) == own_clip) & (there >= 0) & (there < total)
        masks.append(same.astype(F32))
    taps = convw_ref[...].T

    hidden = hidden_ref[...]
    padded[0:HALO] = rims_ref[0]
    padded[HALO : HALO + rows] = hidden
    padded[HALO + rows : 2 * HALO + rows] = rims_ref[1]

    def shifted(k):
        return padded[HALO + k - half : HALO + k - half + rows]

    mixed = jnp.broadcast_to(row_of(convb_ref), (rows, width))
    for k in range(KERNEL):
        mixed = mixed + shifted(k) * taps[k : k + 1] * masks[k]
    center = mixed - jnp.mean(mixed, axis=1, keepdims=True)
    ln_rstd = lax.rsqrt(jnp.mean(center * center, axis=1, keepdims=True) + EPS)
    ln_hat = center * ln_rstd
    ln_low = (ln_hat * row_of(lng_ref) + row_of(lnb_ref)).astype(BF16)
    pre = dot(ln_low, wup_ref[...]) + row_of(upb_ref)
    slope = 0.7978845608028654
    curve = 0.044715
    wave = jnp.tanh(slope * (pre + curve * (pre * pre * pre)))
    cdf = 0.5 * (1.0 + wave)
    act_low = (pre * cdf).astype(BF16)
    bend = cdf + 0.5 * pre * (1.0 - wave * wave) * (slope * (1.0 + 3.0 * curve * (pre * pre)))
    cot = cot_ref[...].astype(F32)
    proj_grad = (cot * row_of(scale_ref)).astype(BF16)
    act_grad = dot(proj_grad, wdown_ref[...], ((1,), (1,)))
    pre_low = (act_grad * bend).astype(BF16)
    ln_own[...] = dot(pre_low, wup_ref[...], ((1,), (1,))).astype(BF16)
    pl.semaphore_wait(
        barrier, 1 + (seq > 0).astype(jnp.int32) + (seq < n_seq - 1).astype(jnp.int32)
    )

    def swap(i, source, target):
        copy = pltpu.make_async_remote_copy(
            src_ref=source,
            dst_ref=target,
            send_sem=swap_sem.at[2 * i],
            recv_sem=swap_sem.at[2 * i + 1],
            device_id=(seq, 1 - head),
            device_id_type=MESH,
        )
        copy.start()
        return copy

    ln_copy = swap(0, ln_own, ln_other)
    proj_own[...] = dot(act_low, wdown_ref[...]).astype(BF16)
    proj_copy = swap(1, proj_own, proj_other)
    gdown[...] = dot(act_low.astype(F32).T.astype(BF16), proj_grad)
    gup = dot(ln_low.astype(F32).T.astype(BF16), pre_low)
    tall = width // n_seq
    for s in range(n_seq):
        put_block(gb_ref, s, gup[tall * s : tall * (s + 1)])
    upvec_ref[...] = jnp.broadcast_to(
        jnp.sum(pre_low.astype(F32), axis=0, keepdims=True), (HALO, hidden_units)
    )

    ln_copy.wait()
    ln_grad = ln_own[...].astype(F32) + ln_other[...].astype(F32)
    hat_grad = ln_grad * row_of(lng_ref)
    mixed_grad = ln_rstd * (
        hat_grad
        - jnp.mean(hat_grad, axis=1, keepdims=True)
        - ln_hat * jnp.mean(hat_grad * ln_hat, axis=1, keepdims=True)
    )
    rim[0] = mixed_grad[0:HALO]
    rim[1] = mixed_grad[rows - HALO : rows]
    swap_rims(seq, head, n_seq, rim, rim_sem)
    tap_grads = [
        jnp.sum(mixed_grad * shifted(k) * masks[k], axis=0, keepdims=True) for k in range(KERNEL)
    ]
    padded[0:HALO] = rim[2]
    padded[HALO : HALO + rows] = mixed_grad
    padded[HALO + rows : 2 * HALO + rows] = rim[3]
    hidden_grad = cot
    for k in range(KERNEL):
        mirror = KERNEL - 1 - k
        hidden_grad = hidden_grad + shifted(mirror) * taps[k : k + 1] * masks[mirror]
    hgrad_ref[...] = hidden_grad
    branch_grad = hidden_grad.astype(BF16)
    dot_ref[...] = (
        dot(wout_ref[...], branch_grad, ((1,), (1,))).astype(BF16).reshape(dot_ref.shape)
    )
    gout = dot(att_ref[...], branch_grad)
    tall_down = hidden_units // n_seq
    tall_out = gout.shape[0] // n_seq
    for s in range(n_seq):
        block = jnp.concatenate(
            [
                gdown[tall_down * s : tall_down * (s + 1)],
                gout[tall_out * s : tall_out * (s + 1)],
            ],
            axis=0,
        )
        put_block(ga_ref, s, block)
    proj_copy.wait()
    projected = proj_own[...].astype(F32) + proj_other[...].astype(F32) + row_of(downb_ref)
    out_ref[...] = (hidden + row_of(scale_ref) * projected).astype(BF16)

    def total_of(member):
        return jnp.sum(member, axis=0, keepdims=True)

    vec_ref[...] = jnp.concatenate(
        [total_of(branch_grad.astype(F32))]
        + tap_grads
        + [
            total_of(mixed_grad),
            total_of(ln_grad * ln_hat),
            total_of(ln_grad),
            total_of(proj_grad.astype(F32)),
            total_of(cot * projected),
            jnp.zeros((3, width), F32),
        ],
        axis=0,
    )


def put_block(ref, s, block):
    spare = ref.shape[3] - block.shape[0]
    if spare:
        block = jnp.concatenate([block, jnp.zeros((spare, block.shape[1]), F32)], axis=0)
    ref[s % 2, s // 2 % 2, s // 4] = block.astype(ref.dtype)


def whole_tiles(rows):
    return -(-rows // 16) * 16


def block_shapes(n_seq, width, heads, hidden_units):
    tall_a = whole_tiles((hidden_units + heads * HEAD_DIM) // n_seq)
    tall_b = whole_tiles(width // n_seq)
    deep = (n_seq // 4,)
    return (
        (deep + (tall_a, width), BF16),
        (deep + (tall_b, hidden_units), BF16),
        (deep + (tall_b, 3 * heads * HEAD_DIM), BF16),
        (deep + (24, LANES), F32),
    )


def middle(n_seq, n_head, lengths, hidden, rims, cot, att, wout, convw, convb, lng, lnb, wup, upb, wdown, downb, scale):
    rows, width = hidden.shape
    hidden_units = wup.shape[1]
    heads = wout.shape[0] // HEAD_DIM
    dma = pltpu.SemaphoreType.DMA
    shape = jax.ShapeDtypeStruct
    blocks = block_shapes(n_seq, width, heads, hidden_units)
    return pl.pallas_call(
        functools.partial(middle_kernel, n_seq, n_head),
        name="middle",
        out_shape=(
            shape((rows, width), BF16),
            shape((rows, width), F32),
            shape((heads, HEAD_DIM, rows), BF16),
            shape((2, 2) + blocks[0][0], BF16),
            shape((2, 2) + blocks[1][0], BF16),
            shape((16, width), F32),
            shape((HALO, hidden_units), F32),
        ),
        in_specs=[pl.BlockSpec(memory_space=pltpu.SMEM)] + vmem(14),
        out_specs=tuple(vmem(7)),
        scratch_shapes=[
            pltpu.VMEM((rows + 2 * HALO, width), F32),
            pltpu.VMEM((hidden_units, width), F32),
            pltpu.VMEM((rows, width), BF16),
            pltpu.VMEM((rows, width), BF16),
            pltpu.VMEM((rows, width), BF16),
            pltpu.VMEM((rows, width), BF16),
            pltpu.VMEM((4, HALO, width), F32),
            dma((4,)),
            dma((4,)),
        ],
        compiler_params=pltpu.CompilerParams(
            collective_id=1, has_side_effects=True, vmem_limit_bytes=56 * 2**20
        ),
    )(lengths, hidden, rims, cot, att, wout, convw, convb, lng, lnb, wup, upb, wdown, downb, scale)


class Reduction:
    def __init__(self, seq, head, n_seq, source, half_in, half, far_in, far, done, sems):
        self.seq, self.head, self.deep = seq, head, n_seq // 4
        self.source, self.half_in, self.half = source, half_in, half
        self.far_in, self.far, self.done, self.sems = far_in, far, done, sems
        self.low = lax.rem(seq, 2)
        self.next = lax.rem(seq // 2, 2)
        self.place = seq // 4

    def copy(self, source, target, i, other):
        return pltpu.make_async_remote_copy(
            src_ref=source,
            dst_ref=target,
            send_sem=self.sems.at[2 * i],
            recv_sem=self.sems.at[2 * i + 1],
            device_id=(other, self.head),
            device_id_type=MESH,
        )

    def near(self):
        return self.copy(
            self.source.at[1 - self.low], self.half_in, 0, self.seq + 1 - 2 * self.low
        )

    def start(self):
        self.near().start()

    def beside(self):
        return self.copy(
            self.half.at[1 - self.next], self.far_in, 1, self.seq + 2 - 4 * self.next
        )

    def second(self):
        self.near().wait()

        def add(z, carry):
            for b in range(2):
                self.half[b, z] = (
                    self.source[self.low, b, z].astype(F32) + self.half_in[b, z].astype(F32)
                ).astype(self.half.dtype)
            return carry

        lax.fori_loop(0, self.deep, add, 0)
        self.beside().start()

    def along(self, i):
        other = lax.rem(self.place + i, self.deep)
        return pltpu.make_async_remote_copy(
            src_ref=self.far.at[other],
            dst_ref=self.done.at[self.place],
            send_sem=self.sems.at[4 + 2 * i],
            recv_sem=self.sems.at[4 + 2 * self.deep + self.place],
            device_id=(other * 4 + self.next * 2 + self.low, self.head),
            device_id_type=MESH,
        )

    def third(self):
        self.beside().wait()

        def add(z, carry):
            self.far[z] = (
                self.half[self.next, z].astype(F32) + self.far_in[z].astype(F32)
            ).astype(self.far.dtype)
            return carry

        lax.fori_loop(0, self.deep, add, 0)

        def give(i, carry):
            self.along(i).start()
            return carry

        lax.fori_loop(1, self.deep, give, 0)

    def finish(self):
        self.done[self.place] = self.far[self.place]

        def take(i, carry):
            other = lax.rem(self.place + i, self.deep)
            arrived(self.done.at[other], self.sems.at[4 + 2 * self.deep + other])
            arrived(self.far.at[other], self.sems.at[4 + 2 * i])
            return carry

        lax.fori_loop(1, self.deep, take, 0)

    def result(self):
        out = self.done[0].astype(F32)
        for z in range(1, self.deep):
            out = out + self.done[z].astype(F32)
        return out


def reduction_scratch(n_seq, blocks):
    out = []
    deep = n_seq // 4
    for dims, kind in blocks:
        out += [
            pltpu.VMEM((2,) + dims, kind),
            pltpu.VMEM((2,) + dims, kind),
            pltpu.VMEM(dims, kind),
            pltpu.VMEM(dims, kind),
            pltpu.VMEM(dims, kind),
            pltpu.SemaphoreType.DMA((4 + 3 * deep,)),
        ]
    return out


def backward_kernel(
    n_seq,
    n_head,
    lengths_ref,
    dot_ref,
    kv_ref,
    kvt_ref,
    qt_ref,
    ot_ref,
    lse_ref,
    ga_ref,
    gb_ref,
    vec_ref,
    upvec_ref,
    frames_ref,
    stat_ref,
    gain_ref,
    bias_ref,
    wq_ref,
    wk_ref,
    wv_ref,
    ngrad_ref,
    mean_ref,
    suma_ref,
    sumb_ref,
    sumc_ref,
    sumv_ref,
    dot_in,
    q_block,
    d_block,
    qd_rows,
    keys_in,
    keys_flip,
    dkv_sum,
    dq_sum,
    dkv_send,
    dq_send,
    dkv_in,
    dq_in,
    part_own,
    part_other,
    stats,
    gc,
    gv,
    dot_ssem,
    dot_rsem,
    dkv_ssem,
    dkv_rsem,
    dq_ssem,
    dq_rsem,
    swap_sem,
    keys_sem,
    stat_ssem,
    stat_rsem,
    *reduce_scratch,
):
    seq = lax.axis_index("seq")
    head = lax.axis_index("head")
    rows, width = frames_ref.shape
    heads = wq_ref.shape[1] // HEAD_DIM
    per_head = n_seq // SPANS
    offset = (SPANS - heads) // 2
    total = n_seq * rows
    span = seq // per_head
    active = (span >= offset) & (span < offset + heads)
    own_head = span - offset
    part = lax.rem(seq, per_head)
    chunk = min(total, 1024)
    chunk_homes = chunk // rows
    met = greet_all(seq, head, n_seq, n_head)
    reductions = [
        Reduction(seq, head, n_seq, source, *reduce_scratch[6 * i : 6 * i + 6])
        for i, source in enumerate((ga_ref, gb_ref, gc, gv))
    ]
    met()

    def give_dot(h, carry):
        dest = (h + offset) * per_head + seq // SPANS
        tile = lax.rem(seq, SPANS)
        source = dot_ref.at[h]
        target = dot_in.at[tile]

        @pl.when(dest != seq)
        def _():
            pltpu.make_async_remote_copy(
                src_ref=source,
                dst_ref=target,
                send_sem=dot_ssem.at[h],
                recv_sem=dot_rsem.at[tile],
                device_id=(dest, head),
                device_id_type=MESH,
            ).start()

        @pl.when(dest == seq)
        def _():
            pltpu.make_async_copy(source, target, dot_rsem.at[tile]).start()

        return carry

    lax.fori_loop(0, heads, give_dot, 0)
    for reduction in reductions[:2]:
        reduction.start()

    @pl.when(active)
    def _():
        def prepare(t, carry):
            arrived(dot_in.at[t], dot_rsem.at[t])
            queries = qt_ref[t]
            grads = dot_in[t]
            zeros = jnp.zeros((HEAD_DIM, rows), BF16)
            first = part * SPANS * rows + t * rows
            q_block[t] = query_block(queries, first, lengths_ref, lse_ref[t, 0:1])
            delta = jnp.sum(grads.astype(F32) * ot_ref[t], axis=0, keepdims=True)
            row = iota((LANES, rows), 0)
            marks = jnp.zeros((LANES, rows), F32)
            for i, third in enumerate(thirds(delta)):
                marks = jnp.where(row == CLIPS + i, -third, marks)
            d_block[t] = jnp.concatenate([zeros, grads, marks.astype(BF16)], axis=0)
            both = jnp.concatenate([queries, grads], axis=0).astype(F32).T
            lane = iota((rows, LANES), 1)
            qd_rows[t, 0:rows] = jnp.where(lane < HEAD_DIM, both, 0.0).astype(BF16)
            qd_rows[t, rows:] = jnp.where(lane < HEAD_DIM, 0.0, both).astype(BF16)
            dq_sum[t] = jnp.zeros((HEAD_DIM, rows), F32)
            return carry

        lax.fori_loop(0, SPANS, prepare, 0)

    slots = dkv_send.shape[0]
    resident = total <= RESIDENT

    def give_dkv(home, carry):
        source = dkv_send.at[lax.rem(home, slots)]
        target = dkv_in.at[part, own_head]
        sem = dkv_rsem.at[part, own_head]

        @pl.when(home != seq)
        def _():
            pltpu.make_async_remote_copy(
                src_ref=source,
                dst_ref=target,
                send_sem=dkv_ssem.at[home],
                recv_sem=sem,
                device_id=(home, head),
                device_id_type=MESH,
            ).start()

        @pl.when(home == seq)
        def _():
            pltpu.make_async_copy(source, target, sem).start()

        return carry

    def sent_dkv(home, carry):
        @pl.when((home >= 0) & (home != seq))
        def _():
            arrived(dkv_send.at[lax.rem(home, slots)], dkv_ssem.at[home])

        return carry

    all_keys, all_flip = (kv_ref, kvt_ref) if resident else (keys_in, keys_flip)

    def key_step(c, carry):
        place = pl.ds(pl.multiple_of(c * chunk, chunk), chunk)
        here = place
        if not resident:
            here = pl.ds(0, chunk)
            copies = [
                pltpu.make_async_copy(kv_ref.at[place, :], keys_in, keys_sem.at[0]),
                pltpu.make_async_copy(kvt_ref.at[:, place], keys_flip, keys_sem.at[1]),
            ]
            for copy in copies:
                copy.start()
            for copy in copies:
                copy.wait()
        dkv_sum[...] = jnp.zeros((chunk, LANES), F32)

        def tile(t, inner):
            keys = all_keys[here, :]
            probs = jnp.exp(dot(keys, q_block[t]))
            grads = (probs * dot(keys, d_block[t])).astype(BF16)
            dkv_sum[...] += dot(
                jnp.concatenate([grads, probs.astype(BF16)], axis=1), qd_rows[t]
            )
            dq_sum[t] += dot(all_flip[:, here], grads)
            return inner

        lax.fori_loop(0, SPANS, tile, 0)
        for j in range(chunk_homes):
            home = c * chunk_homes + j
            if slots < n_seq:
                sent_dkv(home - slots, 0)
            dkv_send[lax.rem(home, slots)] = dkv_sum[rows * j : rows * (j + 1)].astype(BF16)
        lax.fori_loop(c * chunk_homes, (c + 1) * chunk_homes, give_dkv, 0)
        return carry

    steps = total // chunk
    for phase in range(4):
        @pl.when(active)
        def _():
            lax.fori_loop(phase * steps // 4, (phase + 1) * steps // 4, key_step, 0)

        for reduction in reductions[:2]:
            if phase == 0:
                reduction.second()
            if phase == 2:
                reduction.third()

    def give_dq(t, carry):
        home = part * SPANS + t
        dq_send[t] = (dq_sum[t] * HEAD_DIM**-0.5).astype(BF16)
        source = dq_send.at[t]
        target = dq_in.at[own_head]
        sem = dq_rsem.at[own_head]

        @pl.when(home != seq)
        def _():
            pltpu.make_async_remote_copy(
                src_ref=source,
                dst_ref=target,
                send_sem=dq_ssem.at[t],
                recv_sem=sem,
                device_id=(home, head),
                device_id_type=MESH,
            ).start()

        @pl.when(home == seq)
        def _():
            pltpu.make_async_copy(source, target, sem).start()

        return carry

    @pl.when(active)
    def _():
        lax.fori_loop(0, SPANS, give_dq, 0)

    rows_clip = clip_of(seq * rows + iota((rows, 1), 0), lengths_ref)
    table = stat_ref[...]
    x = frames_ref[...].astype(F32)
    hat = (x - by_clip(rows_clip, table, 0)) * by_clip(rows_clip, table, CLIPS)
    normed_flip = (hat * row_of(gain_ref) + row_of(bias_ref)).astype(BF16).astype(F32).T.astype(BF16)

    for h in range(heads):
        arrived(dq_in.at[h], dq_rsem.at[h])
        for p in range(per_head):
            arrived(dkv_in.at[p, h], dkv_rsem.at[p, h])
    dq = dq_in[...].reshape(heads * HEAD_DIM, rows).astype(F32).T.astype(BF16)
    dk, dv = [], []
    for h in range(heads):
        both = dkv_in[0, h].astype(F32)
        for p in range(1, per_head):
            both = both + dkv_in[p, h].astype(F32)
        dk.append(both[:, 0:HEAD_DIM])
        dv.append(both[:, HEAD_DIM:])
    dk = jnp.concatenate(dk, axis=1).astype(BF16)
    dv = jnp.concatenate(dv, axis=1).astype(BF16)
    flipped = ((1,), (1,))
    part_own[...] = (
        dot(dq, wq_ref[...], flipped) + dot(dk, wk_ref[...], flipped) + dot(dv, wv_ref[...], flipped)
    ).astype(BF16)
    part_copy = pltpu.make_async_remote_copy(
        src_ref=part_own,
        dst_ref=part_other,
        send_sem=swap_sem.at[0],
        recv_sem=swap_sem.at[1],
        device_id=(seq, 1 - head),
        device_id_type=MESH,
    )
    part_copy.start()
    scaled = part_own[...].astype(F32) * row_of(gain_ref)
    sums = []
    for member in (scaled, scaled * hat):
        for c in range(CLIPS):
            sums.append(jnp.sum(jnp.where(rows_clip == c, member, 0.0), axis=0, keepdims=True))
    sums.append(jnp.zeros((HALO - 2 * CLIPS, width), F32))
    groups = group_matrix(width)
    me = seq * n_head + head
    everyone = n_seq * n_head
    stats[me] = dot(jnp.concatenate(sums, axis=0), groups, precision=HIGHEST)

    def give_stats(i, carry):
        other = lax.rem(me + i, everyone)
        pltpu.make_async_remote_copy(
            src_ref=stats.at[me],
            dst_ref=stats.at[me],
            send_sem=stat_ssem.at[i],
            recv_sem=stat_rsem.at[me],
            device_id=(other // n_head, lax.rem(other, n_head)),
            device_id_type=MESH,
        ).start()
        return carry

    lax.fori_loop(1, everyone, give_stats, 0)

    gqkv = jnp.concatenate([dot(normed_flip, dq), dot(normed_flip, dk), dot(normed_flip, dv)], axis=1)
    tall = width // n_seq
    for s in range(n_seq):
        put_block(gc, s, gqkv[tall * s : tall * (s + 1)])
    reductions[2].start()

    part_copy.wait()
    normed_grad = part_own[...].astype(F32) + part_other[...].astype(F32)
    ngrad_ref[...] = normed_grad
    vectors = jnp.concatenate(
        [
            vec_ref[0:13],
            jnp.sum(normed_grad * hat, axis=0, keepdims=True),
            jnp.sum(normed_grad, axis=0, keepdims=True),
        ],
        axis=0,
    )
    q_sum = jnp.sum(dq.astype(F32), axis=0, keepdims=True)
    v_sum = jnp.sum(dv.astype(F32), axis=0, keepdims=True)
    up_sum = upvec_ref[0:1]

    def piece(member, s):
        wide = member.shape[1] // n_seq
        return jnp.concatenate(
            [
                member[:, wide * s : wide * (s + 1)],
                jnp.zeros((member.shape[0], LANES - wide), F32),
            ],
            axis=1,
        )

    for s in range(n_seq):
        block = [piece(member, s) for member in (vectors, q_sum, v_sum, up_sum)]
        put_block(gv, s, jnp.concatenate(block, axis=0))
    reductions[3].start()
    for reduction in reductions[2:]:
        reduction.second()

    def take_stats(i, carry):
        other = lax.rem(me + i, everyone)
        arrived(stats.at[other], stat_rsem.at[other])
        return carry

    lax.fori_loop(1, everyone, take_stats, 0)
    summed = lax.fori_loop(
        0, everyone, lambda i, acc: acc + stats[i], jnp.zeros((HALO, LANES), F32)
    ) / members_of(lengths_ref, width)
    mean_ref[...] = dot(summed, groups, flipped, HIGHEST)
    for reduction in reductions[2:]:
        reduction.third()
    for reduction, out in zip(reductions, (suma_ref, sumb_ref, sumc_ref, sumv_ref)):
        reduction.finish()
        out[...] = reduction.result()

    def sent_stats(i, carry):
        arrived(stats.at[me], stat_ssem.at[i])
        return carry

    lax.fori_loop(1, everyone, sent_stats, 0)

    def sent_dot(h, carry):
        @pl.when((h + offset) * per_head + seq // SPANS != seq)
        def _():
            arrived(dot_ref.at[h], dot_ssem.at[h])

        return carry

    lax.fori_loop(0, heads, sent_dot, 0)

    @pl.when(active)
    def _():
        lax.fori_loop(n_seq - slots, n_seq, sent_dkv, 0)

        def sent_dq(t, carry):
            @pl.when(part * SPANS + t != seq)
            def _():
                arrived(dq_send.at[t], dq_ssem.at[t])

            return carry

        lax.fori_loop(0, SPANS, sent_dq, 0)


def backward(n_seq, n_head, hidden_units, lengths, dots, kept, ga, gb, vec, upvec, frames, stat, gain, bias, wq, wk, wv):
    rows, width = frames.shape
    heads = wq.shape[1] // HEAD_DIM
    total = n_seq * rows
    per_head = n_seq // SPANS
    chunk = min(total, 1024)
    resident = total <= RESIDENT
    part = 16 if resident else chunk
    keys = pl.BlockSpec(memory_space=pltpu.VMEM if resident else pl.ANY)
    dma = pltpu.SemaphoreType.DMA
    shape = jax.ShapeDtypeStruct
    blocks = block_shapes(n_seq, width, heads, hidden_units)
    return pl.pallas_call(
        functools.partial(backward_kernel, n_seq, n_head),
        name="backward",
        out_shape=(shape((rows, width), F32), shape((HALO, width), F32))
        + tuple(shape(dims[1:], F32) for dims, kind in blocks),
        in_specs=[pl.BlockSpec(memory_space=pltpu.SMEM)] + vmem(1) + [keys] * 2 + vmem(14),
        out_specs=tuple(vmem(6)),
        scratch_shapes=[
            pltpu.VMEM((SPANS, HEAD_DIM, rows), BF16),
            pltpu.VMEM((SPANS, 2 * LANES, rows), BF16),
            pltpu.VMEM((SPANS, 2 * LANES, rows), BF16),
            pltpu.VMEM((SPANS, 2 * rows, LANES), BF16),
            pltpu.VMEM((part, 2 * LANES), BF16),
            pltpu.VMEM((HEAD_DIM, max(part, LANES)), BF16),
            pltpu.VMEM((chunk, LANES), F32),
            pltpu.VMEM((SPANS, HEAD_DIM, rows), F32),
            pltpu.VMEM((min(n_seq, 16), rows, LANES), BF16),
            pltpu.VMEM((SPANS, HEAD_DIM, rows), BF16),
            pltpu.VMEM((per_head, heads, rows, LANES), BF16),
            pltpu.VMEM((heads, HEAD_DIM, rows), BF16),
            pltpu.VMEM((rows, width), BF16),
            pltpu.VMEM((rows, width), BF16),
            pltpu.VMEM((n_seq * n_head, HALO, LANES), F32),
            pltpu.VMEM((2, 2) + blocks[2][0], BF16),
            pltpu.VMEM((2, 2) + blocks[3][0], F32),
            dma((heads,)),
            dma((SPANS,)),
            dma((n_seq,)),
            dma((per_head, heads)),
            dma((SPANS,)),
            dma((heads,)),
            dma((2,)),
            dma((2,)),
            dma((n_seq * n_head,)),
            dma((n_seq * n_head,)),
        ]
        + reduction_scratch(n_seq, blocks),
        compiler_params=pltpu.CompilerParams(
            collective_id=2, has_side_effects=True, vmem_limit_bytes=60 * 2**20
        ),
    )(lengths, dots, *kept, ga, gb, vec, upvec, frames, stat, gain, bias, wq, wk, wv)


def ending_kernel(
    n_seq,
    lengths_ref,
    frames_ref,
    gain_ref,
    stat_ref,
    mean_ref,
    ngrad_ref,
    hgrad_ref,
    result_ref,
    suma_ref,
    sumb_ref,
    sumc_ref,
    sumv_ref,
    output_ref,
    fgrad_ref,
    gn_gain_ref,
    gn_bias_ref,
    wq_ref,
    qb_ref,
    wk_ref,
    wv_ref,
    vb_ref,
    wout_ref,
    outb_ref,
    convw_ref,
    convb_ref,
    lng_ref,
    lnb_ref,
    wup_ref,
    upb_ref,
    wdown_ref,
    downb_ref,
    scale_ref,
):
    seq = lax.axis_index("seq")
    rows, width = frames_ref.shape
    output_ref[...] = result_ref[...]
    rows_clip = clip_of(seq * rows + iota((rows, 1), 0), lengths_ref)
    table = stat_ref[...]
    means = mean_ref[...]
    rstd = by_clip(rows_clip, table, CLIPS)
    hat = (frames_ref[...].astype(F32) - by_clip(rows_clip, table, 0)) * rstd
    scaled = ngrad_ref[...] * row_of(gain_ref)
    fgrad_ref[...] = hgrad_ref[...] + rstd * (
        scaled - by_clip(rows_clip, means, 0) - hat * by_clip(rows_clip, means, CLIPS)
    )
    wide = wq_ref.shape[1]
    tall = wq_ref.shape[0]
    wq_ref[...] = sumc_ref[0:tall, 0:wide]
    wk_ref[...] = sumc_ref[0:tall, wide : 2 * wide]
    wv_ref[...] = sumc_ref[0:tall, 2 * wide : 3 * wide]
    wup_ref[...] = sumb_ref[0 : wup_ref.shape[0], :]
    tall_down = wdown_ref.shape[0]
    wdown_ref[...] = suma_ref[0:tall_down]
    wout_ref[...] = suma_ref[tall_down : tall_down + wout_ref.shape[0]]
    vectors = sumv_ref[...]

    def put(ref, row):
        count = ref.shape[0]
        ref[...] = vectors[row : row + 1, 0:count].reshape(count)

    put(outb_ref, 0)
    convw_ref[...] = vectors[0:HALO].T[0:tall, 1 : 1 + KERNEL]
    for i, ref in enumerate(
        (convb_ref, lng_ref, lnb_ref, downb_ref, scale_ref, gn_gain_ref, gn_bias_ref, qb_ref, vb_ref, upb_ref)
    ):
        put(ref, 8 + i)


def ending(n_seq, lengths, frames, gain, stat, means, ngrad, hgrad, result, sums, heads, hidden_units):
    rows, width = frames.shape
    shape = jax.ShapeDtypeStruct
    tall = width // n_seq
    wide = heads * HEAD_DIM
    thin = shape((tall,), F32)
    return pl.pallas_call(
        functools.partial(ending_kernel, n_seq),
        name="ending",
        out_shape=(
            shape((rows, width), BF16),
            shape((rows, width), F32),
            thin,
            thin,
            shape((tall, wide), F32),
            shape((wide // n_seq,), F32),
            shape((tall, wide), F32),
            shape((tall, wide), F32),
            shape((wide // n_seq,), F32),
            shape((wide // n_seq, width), F32),
            thin,
            shape((tall, KERNEL), F32),
            thin,
            thin,
            thin,
            shape((tall, hidden_units), F32),
            shape((hidden_units // n_seq,), F32),
            shape((hidden_units // n_seq, width), F32),
            thin,
            thin,
        ),
        in_specs=[pl.BlockSpec(memory_space=pltpu.SMEM)] + vmem(11),
        out_specs=tuple(vmem(20)),
        compiler_params=pltpu.CompilerParams(vmem_limit_bytes=56 * 2**20),
    )(lengths, frames, gain, stat, means, ngrad, hgrad, result, *sums)


def shards(
    n_seq,
    n_head,
    frames,
    lengths,
    gn_gain,
    gn_bias,
    w_query,
    q_bias,
    w_key,
    w_value,
    v_bias,
    w_out,
    out_bias,
    conv_weight,
    conv_bias,
    ln_gain,
    ln_bias,
    w_up,
    up_bias,
    w_down,
    down_bias,
    layer_scale,
    out_grad,
):
    heads = w_query.shape[1] // HEAD_DIM
    hidden_units = w_up.shape[1]
    hidden, rims, att, stat, *kept = forward(
        n_seq, n_head, lengths, frames, gn_gain, gn_bias, w_query, q_bias, w_key, w_value, v_bias, w_out, out_bias
    )
    result, hgrad, dots, ga, gb, vec, upvec = middle(
        n_seq,
        n_head,
        lengths,
        hidden,
        rims,
        out_grad,
        att,
        w_out,
        conv_weight,
        conv_bias,
        ln_gain,
        ln_bias,
        w_up,
        up_bias,
        w_down,
        down_bias,
        layer_scale,
    )
    ngrad, means, *sums = backward(
        n_seq,
        n_head,
        hidden_units,
        lengths,
        dots,
        kept,
        ga,
        gb,
        vec,
        upvec,
        frames,
        stat,
        gn_gain,
        gn_bias,
        w_query,
        w_key,
        w_value,
    )
    return ending(
        n_seq, lengths, frames, gn_gain, stat, means, ngrad, hgrad, result, sums, heads, hidden_units
    )


def solution(mesh):
    rows = P("seq", None)
    return jax.shard_map(
        functools.partial(shards, mesh.shape["seq"], mesh.shape["head"]),
        mesh=mesh,
        in_specs=(
            rows,
            P(),
            P(),
            P(),
            P(None, "head"),
            P("head"),
            P(None, "head"),
            P(None, "head"),
            P("head"),
            P("head", None),
            P(),
            P(),
            P(),
            P(),
            P(),
            P(None, "head"),
            P("head"),
            P("head", None),
            P(),
            P(),
            rows,
        ),
        out_specs=(
            rows,
            rows,
            P("seq"),
            P("seq"),
            P("seq", "head"),
            P(("head", "seq")),
            P("seq", "head"),
            P("seq", "head"),
            P(("head", "seq")),
            P(("head", "seq"), None),
            P("seq"),
            rows,
            P("seq"),
            P("seq"),
            P("seq"),
            P("seq", "head"),
            P(("head", "seq")),
            P(("head", "seq"), None),
            P("seq"),
            P("seq"),
        ),
        check_vma=False,
    )
```

time: 926 us -> 227 us (0.25)
  waiting for transfers between devices: 537 us -> 0 us
  Pallas kernels: 0 us -> 223 us
  blocking collectives: 137 us -> 0 us
  matrix products: 123 us -> 0 us
  local copies, waits for them, and re-layouts: 52.5 us -> 3.08 us
  other arithmetic: 46.5 us -> 0 us
  between operations: 17.4 us -> 0.69 us
    reduce_scatter x6 -> x0, waiting for transfers between devices: 344 us -> none  [the longest x1 71.5 us: shards(): lax.psum_scatter(grad_w_up, 'seq', scatter_dimension=0, tiled=True)]
    pallas_call x0 -> x4, Pallas kernels: none -> 223 us  [the longest x1 138 us: backward(): pl.pallas_call(functools.partial(backward_kernel, n_seq, n_head), name='b...]
    dot_general x32 -> x0, matrix products: 123 us -> none  [the longest x1 18.1 us: query_step(): jnp.einsum('hqk,khd->qhd', score_grad, part_keys, preferred_element_type=...]
    psum x3 -> x0, waiting for transfers between devices: 117 us -> none  [the longest x1 47.7 us: shards(): lax.psum(jnp.dot(act_low, w_down, preferred_element_type=jnp.float32), 'h...]
    psum x2 -> x0, blocking collectives: 96.4 us -> none  [the longest x1 61.5 us: shards(): part_one, part_two = lax.psum((part_one, part_two), 'seq')]
    all_gather x4 -> x0, waiting for transfers between devices: 75.1 us -> none  [the longest x1 37.1 us: shards(): lax.all_gather(keys, 'seq', axis=0, tiled=True)]
    all_gather x2 -> x0, blocking collectives: 40.4 us -> none  [the longest x1 21.2 us: shards(): lax.all_gather(log_total.T, 'seq', axis=0, tiled=True)]
    reduce_sum x14 -> x0, other arithmetic: 34.1 us -> none  [the longest x1 12.9 us: forward_step(): running_sum = running_sum * factor + jnp.sum(weights, axis=2)]
  transfers between devices with their start and end apart: 18 -> 0, of which waited for: 14 -> 0; matrix products, arithmetic and copies ran while one was open for 15% -> 0% of each run, Pallas kernels for 0% -> 0%
where the time goes in v1:
time: 227 us; the launch traced here: 226 us
  Pallas kernels  223 us (98%)
  local copies, waits for them, and re-layouts  3.08 us (1%)
    pallas_call x1, Pallas kernels, backward(): pl.pallas_call(functools.partial(backward_kernel, n_seq, n_head), name='b...  138 us
    pallas_call x1, Pallas kernels, forward(): pl.pallas_call(functools.partial(forward_kernel, n_seq, n_head), name='fo...  50.5 us
    pallas_call x1, Pallas kernels, middle(): pl.pallas_call(functools.partial(middle_kernel, n_seq, n_head), name='mid...  30.3 us

profile of v1, /device:TPU:0, one launch (start us, length us, event | category | flops | bytes accessed | tf_op | source)
XLA Modules:
  0.0 226.4 jit_solution(12101865322431050803)
XLA Ops:
  0.7 1.7 copy.41.convw_ref
  2.3 50.5 %forward.1 = (f32[256,768]{1,0:T(8,128)}, f32[2,8,768]{2,1,0:T(8,128)}, bf16[384,256]{1,0:T(8,128)(2,1)}, f32[8,768]{1,0:T(8,128)}, bf16[4096,256]{1,0:T(8,128)(...) custom-call(s32[3]{0:T(128)} %lengths_ref.7, ...), custom_call_target="tpu_custom_call" | custom-call | tf_op jit(solution)/shard_map/forward/pallas_call | solution.py:488
  52.8 30.3 %middle.1 = (bf16[256,768]{1,0:T(8,128)(2,1)}, f32[256,768]{1,0:T(8,128)}, bf16[6,64,256]{2,1,0:T(8,128)(2,1)}, bf16[2,2,4,96,768]{4,3,2,1,0:T(8,128)(2,1)}, bf1...) custom-call(s32[3]{0:T(128)} %lengths_ref.7, f32[256,768]{1,0:T(8,128)} %get-tuple-element.43.hidden_ref, ...), custom_call_target="tpu_custom_call" | custom-call | tf_op jit(solution)/shard_map/middle/pallas_call | solution.py:739
  83.1 137.6 %backward.1 = (f32[256,768]{1,0:T(8,128)}, f32[8,768]{1,0:T(8,128)}, f32[96,768]{1,0:T(8,128)}, f32[48,1152]{1,0:T(8,128)}, f32[48,1152]{1,0:T(8,128)}, /*index=5*/f32[24,128]{1,0:T(8,128)}) custom-call(s32[3]{0:T(128)} %lengths_ref.7, bf16[6,64,256]{2,1,0:T(8,128)(2,1)} %get-tuple-element.46.dot_ref, bf16[4096,256]{1,0:T(8,128)(2,1)} %get-tuple-element.47.kv_ref, ...), custom_call_target="tpu_custom_call" | custom-call | tf_op jit(solution)/shard_map/backward/pallas_call | solution.py:1264
  220.7 4.3 %ending.1 = (bf16[256,768]{1,0:T(8,128)(2,1)}, f32[256,768]{1,0:T(8,128)}, f32[48]{0:T(128)}, f32[48]{0:T(128)}, f32[48,384]{1,0:T(8,128)}, /*index=5*/f32[24]{0...) custom-call(s32[3]{0:T(128)} %lengths_ref.7, ...), custom_call_target="tpu_custom_call" | custom-call | tf_op jit(solution)/shard_map/ending/pallas_call | solution.py:1383
  225.0 1.4 copy.42

commit v2 on v0

v2 whole, which is shorter than its diff:
```python
import functools
import types

import jax
import jax.numpy as jnp
from jax import lax
from jax.experimental import pallas as pl
from jax.experimental.pallas import tpu as pltpu
from jax.sharding import PartitionSpec as P

HEAD_DIM = 64
GROUPS = 32
KERNEL = 7
CLIPS = 3
SPANS = 8
LANES = 128
HALO = 8
MARKS = 16
WIDE = 2
CHUNK = 1024
RESIDENT = 8192
EPS = 1e-6
FAR = -1e30
HIGHEST = lax.Precision.HIGHEST
F32 = jnp.float32
BF16 = jnp.bfloat16
MESH = pl.DeviceIdType.MESH
DMA = pltpu.SemaphoreType.DMA
FLIPPED = ((1,), (1,))

ARGUMENTS = (
    "frames",
    "lengths",
    "gn_gain",
    "gn_bias",
    "w_query",
    "q_bias",
    "w_key",
    "w_value",
    "v_bias",
    "w_out",
    "out_bias",
    "taps",
    "conv_bias",
    "ln_gain",
    "ln_bias",
    "w_up",
    "up_bias",
    "w_down",
    "down_bias",
    "layer_scale",
    "out_grad",
)
INPUTS = ("lengths",) + tuple(name for name in ARGUMENTS if name != "lengths")
SUMS = ("g_up", "g_down", "g_out", "g_kv", "g_q", "g_vec")


def iota(shape, dim):
    return lax.broadcasted_iota(jnp.int32, shape, dim)


def dot(a, b, dims=((1,), (0,)), precision=None):
    return lax.dot_general(a, b, (dims, ((), ())), precision=precision, preferred_element_type=F32)


def flip(member):
    return member.astype(F32).T.astype(BF16)


def row_of(ref):
    return ref[...].reshape(1, ref.shape[0])


def total_of(member):
    return jnp.sum(member, axis=0, keepdims=True)


def clip_of(pos, lengths):
    end = jnp.int32(0)
    clip = jnp.zeros(pos.shape, jnp.int32)
    for c in range(CLIPS):
        end = end + lengths[c]
        clip = clip + (pos >= end).astype(jnp.int32)
    return clip


def arrived(ref, sem):
    pltpu.make_async_copy(ref, ref, sem).wait()


def remote(source, target, send_sem, recv_sem, where):
    return pltpu.make_async_remote_copy(
        src_ref=source,
        dst_ref=target,
        send_sem=send_sem,
        recv_sem=recv_sem,
        device_id=where,
        device_id_type=MESH,
    )


def greet_all(seq, head, n_seq, n_head):
    barrier = pltpu.get_barrier_semaphore()
    count = n_seq * n_head

    def hail(i, carry):
        other = lax.rem(seq * n_head + head + i, count)
        pl.semaphore_signal(
            barrier, inc=1, device_id=(other // n_head, lax.rem(other, n_head)), device_id_type=MESH
        )
        return carry

    lax.fori_loop(1, count, hail, 0)
    return lambda: pl.semaphore_wait(barrier, count - 1)


def group_matrix(width):
    channel = iota((width, LANES), 0)
    first = iota((width, LANES), 1) * (width // GROUPS)
    return ((channel >= first) & (channel < first + width // GROUPS)).astype(F32)


def by_clip(rows_clip, table, first):
    out = table[first + CLIPS - 1 : first + CLIPS, :]
    for c in range(CLIPS - 2, -1, -1):
        out = jnp.where(rows_clip == c, table[first + c : first + c + 1, :], out)
    return out


def sums_by_clip(members, rows_clip, width):
    sums = []
    for member in members:
        for c in range(CLIPS):
            sums.append(total_of(jnp.where(rows_clip == c, member, 0.0)))
    sums.append(jnp.zeros((HALO - 2 * CLIPS, width), F32))
    return dot(jnp.concatenate(sums, axis=0), group_matrix(width), precision=HIGHEST)


def members_of(lengths, width):
    row = iota((HALO, 1), 0)
    out = jnp.ones((HALO, 1), F32)
    for c in range(CLIPS):
        count = (lengths[c] * (width // GROUPS)).astype(F32)
        out = jnp.where((row == c) | (row == c + CLIPS), count, out)
    return out


def thirds(row):
    high = row.astype(BF16).astype(F32)
    middle = (row - high).astype(BF16).astype(F32)
    return high, middle, row - high - middle


def mark_rows(clip, total):
    row = iota((MARKS, total.shape[1]), 0)
    marks = jnp.zeros(row.shape, F32)
    if clip is not None:
        marks = jnp.where((row < CLIPS) & (row != clip), FAR, marks)
    for i, third in enumerate(thirds(total)):
        marks = jnp.where(row == CLIPS + i, -third, marks)
    return marks.astype(BF16)


def put_block(ref, s, block):
    spare = ref.shape[4] - block.shape[0]
    if spare:
        block = jnp.concatenate([block, jnp.zeros((spare, block.shape[1]), F32)], axis=0)
    ref[s % 2, s // 2 % 2, s // 4 % 2, s // 8] = block.astype(ref.dtype)


class Reduction:
    def __init__(self, seq, head, source, arrivals, sems):
        self.seq, self.head = seq, head
        self.source, self.arrivals, self.sems = source, arrivals, sems
        self.bits = [lax.rem(seq // 2**i, 2) for i in range(4)]

    def copy(self, i):
        bit = self.bits[i]
        return remote(
            self.source.at[(*self.bits[:i], 1 - bit)],
            self.arrivals[i],
            self.sems.at[2 * i],
            self.sems.at[2 * i + 1],
            (self.seq + (1 - 2 * bit) * 2**i, self.head),
        )

    def start(self):
        self.copy(0).start()

    def add(self, i, place):
        mine = (*self.bits[: i + 1], *place)
        return self.source[mine].astype(F32) + self.arrivals[i][place].astype(F32)

    def advance(self, i):
        self.copy(i - 1).wait()
        bit = self.bits[i]
        deep = 3 - i

        def step(n, lead):
            place = (lead, *[lax.rem(n // 2**k, 2) for k in range(deep)])
            self.source[(*self.bits[:i], *place)] = self.add(i - 1, place).astype(self.source.dtype)

        def both(lead):
            lax.fori_loop(0, 2**deep, lambda n, carry: (step(n, lead), carry)[1], 0)

        both(1 - bit)
        self.copy(i).start()
        both(bit)

    def finish(self):
        self.copy(3).wait()
        return self.add(3, ())


def layer_kernel(n_seq, n_head, inside, names, *refs):
    r = types.SimpleNamespace(**dict(zip(names, refs)))
    seq = lax.axis_index("seq")
    head = lax.axis_index("head")
    rows, width = r.frames.shape
    hidden_units = r.w_up.shape[1]
    heads = r.w_query.shape[1] // HEAD_DIM
    per_head = n_seq // SPANS
    pairs = per_head // 2
    offset = (SPANS - heads) // 2
    total = n_seq * rows
    span = seq // per_head
    active = (span >= offset) & (span < offset + heads)
    own_head = span - offset
    part = lax.rem(seq, per_head)
    low = lax.rem(seq, 2)
    sibling = (seq + 1 - 2 * low, head)
    opposite = (seq, 1 - head)
    steps = total // CHUNK
    homes = CHUNK // rows
    own_chunk = seq // homes
    resident = total <= RESIDENT
    met = greet_all(seq, head, n_seq, n_head)

    def loop(first, last, body):
        def step(i, carry):
            body(i)
            return carry

        lax.fori_loop(first, last, step, 0)

    def give(source, target, send_sem, recv_sem, dest):
        @pl.when(dest != seq)
        def _():
            remote(source, target, send_sem, recv_sem, (dest, head)).start()

        @pl.when(dest == seq)
        def _():
            pltpu.make_async_copy(source, target, recv_sem).start()

    def given(source, send_sem, dest):
        @pl.when(dest != seq)
        def _():
            arrived(source, send_sem)

    x = r.frames[...].astype(F32)
    pos = seq * rows + iota((rows, 1), 0)
    rows_clip = clip_of(pos, r.lengths)
    r.stats[seq] = sums_by_clip((x, x * x), rows_clip, width)
    met()

    def stats_copy(i):
        other = lax.rem(seq + i, n_seq)
        return remote(
            r.stats.at[seq], r.stats.at[seq], r.stat_ssem.at[i], r.stat_rsem.at[seq], (other, head)
        )

    loop(1, n_seq, lambda i: stats_copy(i).start())
    wout_copy = remote(r.w_out, r.other_wout, r.wout_sem.at[0], r.wout_sem.at[1], opposite)
    wout_copy.start()

    def key_marks(first, place):
        lane = iota((rows, LANES), 1)
        clip = clip_of(first + iota((rows, 1), 0), r.lengths)
        marks = (clip == lane) | ((lane >= CLIPS) & (lane < CLIPS + 3))
        r.kv[pl.ds(pl.multiple_of(place, rows), rows), LANES:] = marks.astype(F32).astype(BF16)

    if resident:
        loop(0, n_seq, lambda i: key_marks(i * rows, i * rows))

    tiles = SPANS // WIDE
    across = WIDE * rows

    def clear(t):
        r.q_block[t, HEAD_DIM:] = jnp.zeros((2 * LANES - HEAD_DIM, across), BF16)
        r.d_block[t] = jnp.zeros((2 * LANES, across), BF16)
        r.ot[t] = jnp.zeros((HEAD_DIM, across), F32)
        r.dq_sum[t] = jnp.zeros((HEAD_DIM, across), F32)
        r.top[t] = jnp.full((HALO, across), FAR, F32)
        r.norm[t] = jnp.zeros((HALO, across), F32)

    loop(0, tiles, clear)

    def lanes_of(j):
        return slice(rows * j, rows * (j + 1))

    def stats_take(i):
        other = lax.rem(seq + i, n_seq)
        arrived(r.stats.at[other], r.stat_rsem.at[other])

    loop(1, n_seq, stats_take)
    summed = lax.fori_loop(
        0, n_seq, lambda i, acc: acc + r.stats[i], jnp.zeros((HALO, LANES), F32)
    ) / members_of(r.lengths, width)
    mean = summed[0:CLIPS]
    rstd = lax.rsqrt(summed[CLIPS : 2 * CLIPS] - mean * mean + EPS)
    spare_rows = jnp.zeros((HALO - 2 * CLIPS, LANES), F32)
    table = dot(
        jnp.concatenate([mean, rstd, spare_rows], axis=0), group_matrix(width), FLIPPED, HIGHEST
    )
    frame_rstd = by_clip(rows_clip, table, CLIPS)
    hat = (x - by_clip(rows_clip, table, 0)) * frame_rstd
    normed = (hat * row_of(r.gn_gain) + row_of(r.gn_bias)).astype(BF16)

    kv_home = r.kv if resident else r.kv_far

    def kv_place(s):
        return kv_home.at[pl.ds(pl.multiple_of(s * rows, rows), rows), 0:LANES]

    k_all = dot(normed, r.w_key[...])
    v_all = dot(normed, r.w_value[...]) + row_of(r.v_bias)
    for h in range(heads):
        lanes = slice(HEAD_DIM * h, HEAD_DIM * (h + 1))
        r.kv_send[h] = jnp.concatenate([k_all[:, lanes], v_all[:, lanes]], axis=1).astype(BF16)

    def far_first(i):
        return jnp.where(seq < n_seq // 2, heads - 1 - i, i)

    def kv_dest(i):
        h = far_first(i // pairs)
        return h, (h + offset) * per_head + 2 * lax.rem(i, pairs) + low

    def give_kv(i):
        h, dest = kv_dest(i)
        give(r.kv_send.at[h], kv_place(seq), r.kv_ssem.at[i], r.kv_rsem.at[seq], dest)

    loop(0, heads * pairs, give_kv)
    q_all = (dot(normed, r.w_query[...]) + row_of(r.q_bias)).astype(BF16).astype(F32)
    q_flip = (q_all * HEAD_DIM**-0.5).T.astype(BF16)
    for h in range(heads):
        r.qt_send[h] = q_flip[HEAD_DIM * h : HEAD_DIM * (h + 1), :]
    own_tile = lax.rem(seq, SPANS)

    def q_dest(i):
        h = far_first(i)
        return h, (h + offset) * per_head + seq // SPANS

    def give_q(i):
        h, dest = q_dest(i)
        give(r.qt_send.at[h], r.qt.at[own_tile], r.qt_ssem.at[i], r.qt_rsem.at[own_tile], dest)

    loop(0, heads, give_q)
    r.normed_flip[...] = flip(normed)
    r.hat[...] = hat

    def near_first(i):
        turn = jnp.where(own_chunk < steps // 2, i, steps - i)
        return lax.rem(own_chunk + turn, steps)

    def relay(c):
        for k in range(homes // 2):
            s = c * homes + 2 * k + low
            arrived(kv_place(s), r.kv_rsem.at[s])
            remote(kv_place(s), kv_place(s), r.relay_sem.at[s], r.kv_rsem.at[s], sibling).start()

    def settle(c):
        for k in range(homes // 2):
            s = c * homes + 2 * k + 1 - low
            arrived(kv_place(s), r.kv_rsem.at[s])

    def load(c, first_time):
        if resident:
            here = pl.ds(pl.multiple_of(c * CHUNK, CHUNK), CHUNK)
        else:
            slot = lax.rem(c, 2) * CHUNK
            here = pl.ds(pl.multiple_of(slot, CHUNK), CHUNK)
            place = pl.ds(pl.multiple_of(c * CHUNK, CHUNK), CHUNK)
            copy = pltpu.make_async_copy(
                r.kv_far.at[place], r.kv.at[here, 0:LANES], r.load_sem.at[0]
            )
            copy.start()
            copy.wait()
            for j in range(homes):
                key_marks(c * CHUNK + j * rows, slot + j * rows)
        if first_time or not resident:
            r.kvt[:, here] = flip(r.kv[here, 0:LANES])
        return here

    def forward_chunk(i):
        c = near_first(i)
        settle(c)
        here = load(c, True)

        def score(t):
            r.scores[t % 2] = dot(r.kv[here, :], r.q_block[t])

        score(0)
        for t in range(tiles):
            if t + 1 < tiles:
                score(t + 1)
            if t == tiles // 2:
                pl.when(i + 1 < steps)(lambda: relay(near_first(i + 1)))
            scores = r.scores[t % 2]
            top = r.top[t, 0:1]
            new_top = jnp.maximum(top, jnp.max(scores, axis=0, keepdims=True))
            weights = jnp.exp(scores - new_top)
            factor = jnp.exp(top - new_top)
            r.top[t, 0:1] = new_top
            r.norm[t, 0:1] = r.norm[t, 0:1] * factor + total_of(weights)
            r.ot[t] = r.ot[t] * factor + dot(r.kvt[HEAD_DIM:, here], weights.astype(BF16))

    def give_att(t):
        home = part * SPANS + t
        give(
            r.att_send.at[t],
            r.att_recv.at[0, own_head],
            r.att_ssem.at[t],
            r.att_rsem.at[0, own_head],
            home,
        )

    @pl.when(active)
    def _():
        relay(near_first(0))

        def clip_row(t):
            return clip_of(
                (part * SPANS + t * WIDE) * rows + iota((1, across), 1), r.lengths
            )

        def take_q(t):
            for j in range(WIDE):
                arrived(r.qt.at[t * WIDE + j], r.qt_rsem.at[t * WIDE + j])
                r.q_block[t, 0:HEAD_DIM, lanes_of(j)] = r.qt[t * WIDE + j]
            r.q_block[t, LANES : LANES + MARKS] = mark_rows(
                clip_row(t), jnp.zeros((1, across), F32)
            )

        loop(0, tiles, take_q)
        loop(0, steps, forward_chunk)

        def close(t):
            norm = r.norm[t, 0:1]
            result = r.ot[t] / norm
            r.ot[t] = result
            r.top[t, 0:1] = r.top[t, 0:1] + jnp.log(norm)
            for j in range(WIDE):
                r.att_send[t * WIDE + j] = result[:, lanes_of(j)].astype(BF16)
                give_att(t * WIDE + j)

        loop(0, tiles, close)

    wout_copy.wait()

    def att_across(h):
        return remote(
            r.att_recv.at[0, h],
            r.att_recv.at[1, h],
            r.cross_sem.at[h],
            r.att_rsem.at[1, h],
            opposite,
        )

    def pass_att(h):
        arrived(r.att_recv.at[0, h], r.att_rsem.at[0, h])
        att_across(h).start()

    loop(0, heads, pass_att)
    att_shape = (heads * HEAD_DIM, rows)
    branch = dot(flip(r.att_recv[0].reshape(att_shape)), r.w_out[...])
    loop(0, heads, lambda h: att_across(h).wait())
    branch = branch + dot(flip(r.att_recv[1].reshape(att_shape)), r.other_wout[...])
    hidden = x + (branch + row_of(r.out_bias))

    def rim_copy(k, source, target, there):
        return remote(
            r.rim.at[k, source],
            r.rim.at[k, target],
            r.rim_sem.at[k, source],
            r.rim_sem.at[k, target],
            (there, head),
        )

    def give_rims(k, member):
        r.rim[k, 0] = member[0:HALO]
        r.rim[k, 1] = member[rows - HALO : rows]

        @pl.when(seq > 0)
        def _():
            rim_copy(k, 0, 3, seq - 1).start()

        @pl.when(seq == 0)
        def _():
            r.rim[k, 2] = jnp.zeros((HALO, width), F32)

        @pl.when(seq < n_seq - 1)
        def _():
            rim_copy(k, 1, 2, seq + 1).start()

        @pl.when(seq == n_seq - 1)
        def _():
            r.rim[k, 3] = jnp.zeros((HALO, width), F32)

    def take_rims(k, padded):
        @pl.when(seq > 0)
        def _():
            arrived(r.rim.at[k, 0], r.rim_sem.at[k, 0])
            arrived(r.rim.at[k, 2], r.rim_sem.at[k, 2])

        @pl.when(seq < n_seq - 1)
        def _():
            arrived(r.rim.at[k, 1], r.rim_sem.at[k, 1])
            arrived(r.rim.at[k, 3], r.rim_sem.at[k, 3])

        padded[0:HALO] = r.rim[k, 2]
        padded[HALO + rows : 2 * HALO + rows] = r.rim[k, 3]

    half = KERNEL // 2
    give_rims(0, hidden)
    r.padded[HALO : HALO + rows] = hidden
    taps = r.taps[...]
    masks = []
    for k in range(KERNEL):
        there = pos + (k - half)
        same = (clip_of(there, r.lengths) == rows_clip) & (there >= 0) & (there < total)
        masks.append(same.astype(F32))
    cot = r.out_grad[...].astype(F32)
    proj_grad = (cot * row_of(r.layer_scale)).astype(BF16)
    act_grad = dot(proj_grad, r.w_down[...], FLIPPED)
    take_rims(0, r.padded)

    def shifted(padded, k):
        return padded[HALO + k - half : HALO + k - half + rows]

    mixed = jnp.broadcast_to(row_of(r.conv_bias), (rows, width))
    for k in range(KERNEL):
        mixed = mixed + shifted(r.padded, k) * taps[k : k + 1] * masks[k]
    center = mixed - jnp.mean(mixed, axis=1, keepdims=True)
    ln_rstd = lax.rsqrt(jnp.mean(center * center, axis=1, keepdims=True) + EPS)
    ln_hat = center * ln_rstd
    ln_low = (ln_hat * row_of(r.ln_gain) + row_of(r.ln_bias)).astype(BF16)
    pre = dot(ln_low, r.w_up[...]) + row_of(r.up_bias)
    slope = 0.7978845608028654
    curve = 0.044715
    wave = jnp.tanh(slope * (pre + curve * (pre * pre * pre)))
    cdf = 0.5 * (1.0 + wave)
    act_low = (pre * cdf).astype(BF16)
    bend = cdf + 0.5 * pre * (1.0 - wave * wave) * (slope * (1.0 + 3.0 * curve * (pre * pre)))
    pre_low = (act_grad * bend).astype(BF16)

    def swap(i, mine, other):
        return remote(mine, other, r.swap_sem.at[i, 0], r.swap_sem.at[i, 1], opposite)

    r.ln_own[...] = dot(pre_low, r.w_up[...], FLIPPED).astype(BF16)
    ln_copy = swap(0, r.ln_own, r.ln_other)
    ln_copy.start()
    reductions = {}

    def reduce_blocks(name, member):
        if not inside:
            getattr(r, name)[...] = member.astype(getattr(r, name).dtype)
            return
        tall = member.shape[0] // n_seq
        for s in range(n_seq):
            put_block(getattr(r, name + "_source"), s, member[tall * s : tall * (s + 1)])
        reduce_start(name)

    def reduce_start(name):
        arrivals = [getattr(r, "%s_in%d" % (name, i)) for i in range(4)]
        source, sems = getattr(r, name + "_source"), getattr(r, name + "_sems")
        reductions[name] = Reduction(seq, head, source, arrivals, sems)
        reductions[name].start()

    def advance(i, *names):
        for name in names:
            if inside:
                reductions[name].advance(i)

    reduce_blocks("g_up", dot(flip(ln_low), pre_low))
    r.proj_own[...] = dot(act_low, r.w_down[...]).astype(BF16)
    proj_copy = swap(1, r.proj_own, r.proj_other)
    proj_copy.start()
    advance(1, "g_up")
    reduce_blocks("g_down", dot(flip(act_low), proj_grad))
    up_sum = total_of(pre_low.astype(F32))
    advance(1, "g_down")

    ln_copy.wait()
    ln_grad = r.ln_own[...].astype(F32) + r.ln_other[...].astype(F32)
    hat_grad = ln_grad * row_of(r.ln_gain)
    mixed_grad = ln_rstd * (
        hat_grad
        - jnp.mean(hat_grad, axis=1, keepdims=True)
        - ln_hat * jnp.mean(hat_grad * ln_hat, axis=1, keepdims=True)
    )
    give_rims(1, mixed_grad)
    r.padded_grad[HALO : HALO + rows] = mixed_grad
    tap_grads = [total_of(mixed_grad * shifted(r.padded, k) * masks[k]) for k in range(KERNEL)]
    take_rims(1, r.padded_grad)
    hidden_grad = cot
    for k in range(KERNEL):
        mirror = KERNEL - 1 - k
        hidden_grad = hidden_grad + shifted(r.padded_grad, mirror) * taps[k : k + 1] * masks[mirror]
    r.hidden_grad[...] = hidden_grad
    branch_grad = hidden_grad.astype(BF16)
    r.dot_send[...] = dot(r.w_out[...], branch_grad, FLIPPED).astype(BF16).reshape(r.dot_send.shape)

    def give_dot(i):
        h, dest = q_dest(i)
        give(r.dot_send.at[h], r.dot_in.at[own_tile], r.dot_ssem.at[i], r.dot_rsem.at[own_tile], dest)

    loop(0, heads, give_dot)
    advance(2, "g_up")
    reduce_blocks("g_out", dot(r.att_recv[0].reshape(att_shape), branch_grad))
    proj_copy.wait()
    projected = r.proj_own[...].astype(F32) + r.proj_other[...].astype(F32) + row_of(r.down_bias)
    r.result[...] = (hidden + row_of(r.layer_scale) * projected).astype(BF16)
    r.vectors[0:16] = jnp.concatenate(
        [total_of(branch_grad.astype(F32))]
        + tap_grads
        + [
            total_of(mixed_grad),
            total_of(ln_grad * ln_hat),
            total_of(ln_grad),
            total_of(proj_grad.astype(F32)),
            total_of(cot * projected),
            jnp.zeros((3, width), F32),
        ],
        axis=0,
    )
    advance(1, "g_out")

    @pl.when(active)
    def _():
        def prepare(t):
            clip = clip_of((part * SPANS + t * WIDE) * rows + iota((1, across), 1), r.lengths)
            r.q_block[t, LANES : LANES + MARKS] = mark_rows(clip, r.top[t, 0:1])
            lane = iota((rows, LANES), 1)
            deltas = []
            for j in range(WIDE):
                arrived(r.dot_in.at[t * WIDE + j], r.dot_rsem.at[t * WIDE + j])
                grads = r.dot_in[t * WIDE + j]
                r.d_block[t, HEAD_DIM:LANES, lanes_of(j)] = grads
                deltas.append(total_of(grads.astype(F32) * r.ot[t, :, lanes_of(j)]))
                both = jnp.concatenate([r.qt[t * WIDE + j], grads], axis=0).astype(F32).T
                r.qd_rows[t, lanes_of(j)] = jnp.where(lane < HEAD_DIM, both, 0.0).astype(BF16)
                r.qd_rows[t, lanes_of(WIDE + j)] = jnp.where(lane < HEAD_DIM, 0.0, both).astype(BF16)
            r.d_block[t, LANES : LANES + MARKS] = mark_rows(None, jnp.concatenate(deltas, axis=1))

        loop(0, tiles, prepare)

    def far_chunk(i):
        return jnp.where(own_chunk < steps // 2, steps - 1 - i, i)

    slots = r.dkv_send.shape[0]
    couples = homes // 2

    def pair_copy(i, k):
        slot = lax.rem(i, 2)
        return remote(
            r.pair_send.at[slot, k],
            r.pair_in.at[slot, k],
            r.pair_sem.at[0, slot, k],
            r.pair_sem.at[1, slot, k],
            sibling,
        )

    def dkv_home(i, k):
        return far_chunk(i) * homes + 2 * k + low

    def dkv_sent(i, k):
        slot = lax.rem(i * couples + k, slots)
        given(r.dkv_send.at[slot], r.dkv_ssem.at[slot], dkv_home(i, k))

    def dkv_finish(i):
        for k in range(couples):
            pair_copy(i, k).wait()
            slot = lax.rem(i * couples + k, slots)
            if slots < steps * couples:
                pl.when(i * couples + k >= slots)(lambda: dkv_sent(i - slots // couples, k))
            r.dkv_send[slot] = (
                r.dkv_keep[k] + r.pair_in[lax.rem(i, 2), k].astype(F32)
            ).astype(BF16)
            give(
                r.dkv_send.at[slot],
                r.dkv_in.at[part // 2, own_head],
                r.dkv_ssem.at[slot],
                r.dkv_rsem.at[part // 2, own_head],
                dkv_home(i, k),
            )

    def backward_chunk(i):
        here = load(far_chunk(i), False)
        r.dkv_sum[...] = jnp.zeros((CHUNK, LANES), F32)

        def tile(t):
            keys = r.kv[here, :]
            probs = jnp.exp(dot(keys, r.q_block[t]))
            grads = (probs * dot(keys, r.d_block[t])).astype(BF16)
            r.dkv_sum[...] += dot(
                jnp.concatenate([grads, probs.astype(BF16)], axis=1), r.qd_rows[t]
            )
            r.dq_sum[t] += dot(r.kvt[0:HEAD_DIM, here], grads)

        loop(0, tiles, tile)
        pl.when(i > 0)(lambda: dkv_finish(i - 1))
        for k in range(couples):
            other = pl.ds(pl.multiple_of((2 * k + 1 - low) * rows, rows), rows)
            mine = pl.ds(pl.multiple_of((2 * k + low) * rows, rows), rows)
            r.pair_send[lax.rem(i, 2), k] = r.dkv_sum[other].astype(BF16)
            pair_copy(i, k).start()
            r.dkv_keep[k] = r.dkv_sum[mine]

    for phase in range(4):

        @pl.when(active)
        def _():
            loop(phase * steps // 4, (phase + 1) * steps // 4, backward_chunk)

        if phase == 0:
            advance(2, "g_down")
            advance(3, "g_up")
        if phase == 1:
            advance(2, "g_out")
        if phase == 2:
            advance(3, "g_down")
            advance(3, "g_out")

    def give_dq(t):
        give(
            r.dq_send.at[t],
            r.dq_in.at[own_head],
            r.dq_ssem.at[t],
            r.dq_rsem.at[own_head],
            part * SPANS + t,
        )

    @pl.when(active)
    def _():
        def close(t):
            for j in range(WIDE):
                grads = r.dq_sum[t, :, lanes_of(j)] * HEAD_DIM**-0.5
                r.dq_send[t * WIDE + j] = grads.astype(BF16)
                give_dq(t * WIDE + j)

        loop(0, tiles, close)
        dkv_finish(steps - 1)

    for h in range(heads):
        for p in range(pairs):
            arrived(r.dkv_in.at[p, h], r.dkv_rsem.at[p, h])
    dk, dv = [], []
    for h in range(heads):
        both = r.dkv_in[0, h].astype(F32)
        for p in range(1, pairs):
            both = both + r.dkv_in[p, h].astype(F32)
        dk.append(both[:, 0:HEAD_DIM])
        dv.append(both[:, HEAD_DIM:])
    dk = jnp.concatenate(dk, axis=1).astype(BF16)
    dv = jnp.concatenate(dv, axis=1).astype(BF16)
    normed_flip = r.normed_flip[...]
    reduce_blocks(
        "g_kv", jnp.concatenate([dot(normed_flip, dk), dot(normed_flip, dv)], axis=1)
    )
    kv_part = dot(dk, r.w_key[...], FLIPPED) + dot(dv, r.w_value[...], FLIPPED)
    for h in range(heads):
        arrived(r.dq_in.at[h], r.dq_rsem.at[h])
    dq = flip(r.dq_in[...].reshape(att_shape))
    r.part_own[...] = (kv_part + dot(dq, r.w_query[...], FLIPPED)).astype(BF16)
    part_copy = swap(2, r.part_own, r.part_other)
    part_copy.start()
    reduce_blocks("g_q", dot(normed_flip, dq))
    advance(1, "g_kv")
    hat = r.hat[...]
    gain = row_of(r.gn_gain)
    scaled = r.part_own[...].astype(F32) * gain
    me = seq * n_head + head
    everyone = n_seq * n_head
    r.gstats[me] = sums_by_clip((scaled, scaled * hat), rows_clip, width)

    def gstats_copy(i):
        other = lax.rem(me + i, everyone)
        return remote(
            r.gstats.at[me],
            r.gstats.at[me],
            r.gstat_ssem.at[i],
            r.gstat_rsem.at[me],
            (other // n_head, lax.rem(other, n_head)),
        )

    loop(1, everyone, lambda i: gstats_copy(i).start())
    advance(1, "g_q")
    part_copy.wait()
    normed_grad = r.part_own[...].astype(F32) + r.part_other[...].astype(F32)
    r.vectors[13:14] = total_of(normed_grad * hat)
    r.vectors[14:15] = total_of(normed_grad)
    q_sum = total_of(dq.astype(F32))
    v_sum = total_of(dv.astype(F32))
    if inside:
        members = (r.vectors[0:15], q_sum, v_sum, up_sum)
        spare = jnp.zeros((HALO - 2, LANES), F32)
        for s in range(n_seq):
            block = []
            for member in members:
                wide = member.shape[1] // n_seq
                blank = jnp.zeros((member.shape[0], LANES - wide), F32)
                block.append(
                    jnp.concatenate([member[:, wide * s : wide * (s + 1)], blank], axis=1)
                )
            put_block(r.g_vec_source, s, jnp.concatenate(block + [spare], axis=0))
        reduce_start("g_vec")
    else:
        r.vec_out[...] = r.vectors[...]
        r.q_out[...] = q_sum
        r.v_out[...] = v_sum
        r.up_out[...] = up_sum
    advance(2, "g_kv")
    advance(1, "g_vec")

    def gstats_take(i):
        other = lax.rem(me + i, everyone)
        arrived(r.gstats.at[other], r.gstat_rsem.at[other])

    loop(1, everyone, gstats_take)
    summed = lax.fori_loop(
        0, everyone, lambda i, acc: acc + r.gstats[i], jnp.zeros((HALO, LANES), F32)
    ) / members_of(r.lengths, width)
    means = dot(summed, group_matrix(width), FLIPPED, HIGHEST)
    advance(2, "g_q")
    advance(2, "g_vec")
    advance(3, "g_kv")
    r.frames_grad[...] = r.hidden_grad[...] + frame_rstd * (
        normed_grad * gain - by_clip(rows_clip, means, 0) - hat * by_clip(rows_clip, means, CLIPS)
    )
    advance(3, "g_q", "g_vec")
    if inside:
        for name in SUMS:
            getattr(r, name)[...] = reductions[name].finish()

    loop(1, n_seq, lambda i: arrived(r.stats.at[seq], r.stat_ssem.at[i]))
    loop(1, everyone, lambda i: arrived(r.gstats.at[me], r.gstat_ssem.at[i]))

    def kv_given(i):
        h, dest = kv_dest(i)
        given(r.kv_send.at[h], r.kv_ssem.at[i], dest)

    loop(0, heads * pairs, kv_given)

    def q_given(i):
        h, dest = q_dest(i)
        given(r.qt_send.at[h], r.qt_ssem.at[i], dest)
        given(r.dot_send.at[h], r.dot_ssem.at[i], dest)

    loop(0, heads, q_given)

    @pl.when(active)
    def _():
        def relayed(i):
            s = 2 * i + low
            arrived(kv_place(s), r.relay_sem.at[s])

        loop(0, n_seq // 2, relayed)

        def tile_given(t):
            given(r.att_send.at[t], r.att_ssem.at[t], part * SPANS + t)
            given(r.dq_send.at[t], r.dq_ssem.at[t], part * SPANS + t)

        loop(0, SPANS, tile_given)

        def chunk_given(i):
            for k in range(couples):
                dkv_sent(i, k)

        loop(steps - slots // couples, steps, chunk_given)


def whole_tiles(rows):
    return -(-rows // 16) * 16


def vmem(*dims, kind=BF16):
    return pltpu.VMEM(dims, kind)


def layer(n_seq, n_head, arrays):
    rows, width = arrays["frames"].shape
    hidden_units = arrays["w_up"].shape[1]
    wide = arrays["w_query"].shape[1]
    heads = wide // HEAD_DIM
    per_head = n_seq // SPANS
    pairs = per_head // 2
    total = n_seq * rows
    homes = CHUNK // rows
    steps = total // CHUNK
    couples = homes // 2
    slots = min(4, steps) * couples
    resident = total <= RESIDENT
    inside = n_seq == 16 and width // n_seq % 16 == 0
    tile = (SPANS, HEAD_DIM, rows)
    tiles = SPANS // WIDE
    across = WIDE * rows
    shape = jax.ShapeDtypeStruct
    matrices = {
        "g_up": (width, hidden_units),
        "g_down": (hidden_units, width),
        "g_out": (wide, width),
        "g_kv": (width, 2 * wide),
        "g_q": (width, wide),
    }
    outputs = {
        "result": shape((rows, width), BF16),
        "frames_grad": shape((rows, width), F32),
    }
    blocks = {}
    if inside:
        for name, (tall, long) in matrices.items():
            blocks[name] = (whole_tiles(tall // n_seq), long), BF16
        blocks["g_vec"] = (24, LANES), F32
        for name, (dims, kind) in blocks.items():
            outputs[name] = shape(dims, F32)
    else:
        for name, dims in matrices.items():
            outputs[name] = shape(dims, BF16)
        outputs["vec_out"] = shape((16, width), F32)
        outputs["q_out"] = shape((1, wide), F32)
        outputs["v_out"] = shape((1, wide), F32)
        outputs["up_out"] = shape((1, hidden_units), F32)
    if not resident:
        outputs["kv_far"] = shape((total, LANES), BF16)
    keys = total if resident else 2 * CHUNK
    scratch = {
        "stats": vmem(n_seq, HALO, LANES, kind=F32),
        "stat_ssem": DMA((n_seq,)),
        "stat_rsem": DMA((n_seq,)),
        "other_wout": vmem(wide, width),
        "wout_sem": DMA((2,)),
        "hat": vmem(rows, width, kind=F32),
        "normed_flip": vmem(width, rows),
        "kv_send": vmem(heads, rows, LANES),
        "kv_ssem": DMA((heads * pairs,)),
        "kv_rsem": DMA((n_seq,)),
        "relay_sem": DMA((n_seq,)),
        "kv": vmem(keys, 2 * LANES),
        "kvt": vmem(LANES, keys),
        "load_sem": DMA((1,)),
        "qt_send": vmem(heads, HEAD_DIM, rows),
        "qt_ssem": DMA((heads,)),
        "qt_rsem": DMA((SPANS,)),
        "qt": vmem(*tile),
        "q_block": vmem(tiles, 2 * LANES, across),
        "d_block": vmem(tiles, 2 * LANES, across),
        "qd_rows": vmem(tiles, 2 * across, LANES),
        "scores": vmem(2, CHUNK, across, kind=F32),
        "ot": vmem(tiles, HEAD_DIM, across, kind=F32),
        "top": vmem(tiles, HALO, across, kind=F32),
        "norm": vmem(tiles, HALO, across, kind=F32),
        "att_send": vmem(*tile),
        "att_ssem": DMA((SPANS,)),
        "att_recv": vmem(n_head, heads, HEAD_DIM, rows),
        "att_rsem": DMA((n_head, heads)),
        "cross_sem": DMA((heads,)),
        "rim": vmem(2, 4, HALO, width, kind=F32),
        "rim_sem": DMA((2, 4)),
        "padded": vmem(rows + 2 * HALO, width, kind=F32),
        "padded_grad": vmem(rows + 2 * HALO, width, kind=F32),
        "hidden_grad": vmem(rows, width, kind=F32),
        "ln_own": vmem(rows, width),
        "ln_other": vmem(rows, width),
        "proj_own": vmem(rows, width),
        "proj_other": vmem(rows, width),
        "part_own": vmem(rows, width),
        "part_other": vmem(rows, width),
        "swap_sem": DMA((3, 2)),
        "vectors": vmem(16, width, kind=F32),
        "dot_send": vmem(heads, HEAD_DIM, rows),
        "dot_ssem": DMA((heads,)),
        "dot_in": vmem(*tile),
        "dot_rsem": DMA((SPANS,)),
        "dkv_sum": vmem(CHUNK, LANES, kind=F32),
        "dkv_keep": vmem(couples, rows, LANES, kind=F32),
        "pair_send": vmem(2, couples, rows, LANES),
        "pair_in": vmem(2, couples, rows, LANES),
        "pair_sem": DMA((2, 2, couples)),
        "dkv_send": vmem(slots, rows, LANES),
        "dkv_ssem": DMA((slots,)),
        "dkv_in": vmem(pairs, heads, rows, LANES),
        "dkv_rsem": DMA((pairs, heads)),
        "dq_sum": vmem(tiles, HEAD_DIM, across, kind=F32),
        "dq_send": vmem(*tile),
        "dq_ssem": DMA((SPANS,)),
        "dq_in": vmem(heads, HEAD_DIM, rows),
        "dq_rsem": DMA((heads,)),
        "gstats": vmem(n_seq * n_head, HALO, LANES, kind=F32),
        "gstat_ssem": DMA((n_seq * n_head,)),
        "gstat_rsem": DMA((n_seq * n_head,)),
    }
    for name, (dims, kind) in blocks.items():
        scratch[name + "_source"] = vmem(2, 2, 2, 2, *dims, kind=kind)
        for i in range(4):
            scratch["%s_in%d" % (name, i)] = vmem(*[2] * (3 - i), *dims, kind=kind)
        scratch[name + "_sems"] = DMA((8,))
    names = [*INPUTS, *outputs, *scratch]
    whole = pl.BlockSpec(memory_space=pltpu.VMEM)
    results = pl.pallas_call(
        functools.partial(layer_kernel, n_seq, n_head, inside, names),
        name="layer",
        out_shape=tuple(outputs.values()),
        in_specs=[pl.BlockSpec(memory_space=pltpu.SMEM)] + [whole] * (len(INPUTS) - 1),
        out_specs=tuple(
            pl.BlockSpec(memory_space=pl.ANY) if name == "kv_far" else whole for name in outputs
        ),
        scratch_shapes=list(scratch.values()),
        compiler_params=pltpu.CompilerParams(
            collective_id=0, has_side_effects=True, vmem_limit_bytes=60 * 2**20
        ),
    )(*[arrays[name] for name in INPUTS])
    results = dict(zip(outputs, results))
    if not inside:
        for name in matrices:
            results[name] = lax.psum_scatter(
                results[name].astype(F32), "seq", scatter_dimension=0, tiled=True
            )
        thin = [results["vec_out"][0:15]]
        thin += [results[name] for name in ("q_out", "v_out", "up_out")]
        thin = [lax.psum_scatter(t, "seq", scatter_dimension=1, tiled=True) for t in thin]
        thin = [jnp.pad(t, ((0, 0), (0, LANES - t.shape[1]))) for t in thin]
        results["g_vec"] = jnp.pad(jnp.concatenate(thin, axis=0), ((0, 6), (0, 0)))
    return results


def ending_kernel(
    result_ref,
    fgrad_ref,
    up_ref,
    down_ref,
    out_ref,
    kv_ref,
    q_ref,
    vec_ref,
    output,
    frames_grad,
    gn_gain,
    gn_bias,
    w_query,
    q_bias,
    w_key,
    w_value,
    v_bias,
    w_out,
    out_bias,
    taps,
    conv_bias,
    ln_gain,
    ln_bias,
    w_up,
    up_bias,
    w_down,
    down_bias,
    layer_scale,
):
    output[...] = result_ref[...]
    frames_grad[...] = fgrad_ref[...]
    wide = w_query.shape[1]
    tall = w_query.shape[0]
    w_query[...] = q_ref[0:tall, :]
    w_key[...] = kv_ref[0:tall, 0:wide]
    w_value[...] = kv_ref[0:tall, wide:]
    w_up[...] = up_ref[0:tall, :]
    w_down[...] = down_ref[0 : w_down.shape[0], :]
    w_out[...] = out_ref[0 : w_out.shape[0], :]
    taps[...] = vec_ref[1 : 1 + KERNEL, 0:tall]
    vectors = [(out_bias, 0)]
    vectors += zip(
        (conv_bias, ln_gain, ln_bias, down_bias, layer_scale, gn_gain, gn_bias, q_bias, v_bias, up_bias),
        range(1 + KERNEL, 24),
    )
    for ref, row in vectors:
        count = ref.shape[0]
        ref[...] = vec_ref[row : row + 1, 0:count].reshape(count)


def ending(n_seq, sums, wide, hidden_units):
    rows, width = sums["result"].shape
    shape = lambda *dims: jax.ShapeDtypeStruct(dims, F32)
    tall = width // n_seq
    thin = shape(tall)
    whole = pl.BlockSpec(memory_space=pltpu.VMEM)
    return pl.pallas_call(
        ending_kernel,
        name="ending",
        out_shape=(
            jax.ShapeDtypeStruct((rows, width), BF16),
            shape(rows, width),
            thin,
            thin,
            shape(tall, wide),
            shape(wide // n_seq),
            shape(tall, wide),
            shape(tall, wide),
            shape(wide // n_seq),
            shape(wide // n_seq, width),
            thin,
            shape(KERNEL, tall),
            thin,
            thin,
            thin,
            shape(tall, hidden_units),
            shape(hidden_units // n_seq),
            shape(hidden_units // n_seq, width),
            thin,
            thin,
        ),
        in_specs=[whole] * 8,
        out_specs=tuple([whole] * 20),
        compiler_params=pltpu.CompilerParams(vmem_limit_bytes=56 * 2**20),
    )(sums["result"], sums["frames_grad"], *[sums[name] for name in SUMS])


def shards(n_seq, n_head, *args):
    arrays = dict(zip(ARGUMENTS, args))
    arrays["taps"] = arrays["taps"].T
    sums = layer(n_seq, n_head, arrays)
    out = list(ending(n_seq, sums, arrays["w_query"].shape[1], arrays["w_up"].shape[1]))
    out[11] = out[11].T
    return tuple(out)


def solution(mesh):
    rows = P("seq", None)
    both = P(("head", "seq"))
    return jax.shard_map(
        functools.partial(shards, mesh.shape["seq"], mesh.shape["head"]),
        mesh=mesh,
        in_specs=(
            rows,
            P(),
            P(),
            P(),
            P(None, "head"),
            P("head"),
            P(None, "head"),
            P(None, "head"),
            P("head"),
            P("head", None),
            P(),
            P(),
            P(),
            P(),
            P(),
            P(None, "head"),
            P("head"),
            P("head", None),
            P(),
            P(),
            rows,
        ),
        out_specs=(
            rows,
            rows,
            P("seq"),
            P("seq"),
            P("seq", "head"),
            both,
            P("seq", "head"),
            P("seq", "head"),
            both,
            P(("head", "seq"), None),
            P("seq"),
            rows,
            P("seq"),
            P("seq"),
            P("seq"),
            P("seq", "head"),
            both,
            P(("head", "seq"), None),
            P("seq"),
            P("seq"),
        ),
        check_vma=False,
    )
```

time: 926 us -> 165 us (0.18)
  waiting for transfers between devices: 537 us -> 0 us
  Pallas kernels: 0 us -> 164 us
  blocking collectives: 137 us -> 0 us
  matrix products: 123 us -> 0 us
  local copies, waits for them, and re-layouts: 52.5 us -> 0 us
  other arithmetic: 46.5 us -> 0 us
  between operations: 17.4 us -> 0.86 us
    reduce_scatter x6 -> x0, waiting for transfers between devices: 344 us -> none  [the longest x1 71.5 us: shards(): lax.psum_scatter(grad_w_up, 'seq', scatter_dimension=0, tiled=True)]
    pallas_call x0 -> x2, Pallas kernels: none -> 164 us  [the longest x1 161 us: layer(): pl.pallas_call(functools.partial(layer_kernel, n_seq, n_head, inside, nam...]
    dot_general x32 -> x0, matrix products: 123 us -> none  [the longest x1 18.1 us: query_step(): jnp.einsum('hqk,khd->qhd', score_grad, part_keys, preferred_element_type=...]
    psum x3 -> x0, waiting for transfers between devices: 117 us -> none  [the longest x1 47.7 us: shards(): lax.psum(jnp.dot(act_low, w_down, preferred_element_type=jnp.float32), 'h...]
    psum x2 -> x0, blocking collectives: 96.4 us -> none  [the longest x1 61.5 us: shards(): part_one, part_two = lax.psum((part_one, part_two), 'seq')]
    all_gather x4 -> x0, waiting for transfers between devices: 75.1 us -> none  [the longest x1 37.1 us: shards(): lax.all_gather(keys, 'seq', axis=0, tiled=True)]
    all_gather x2 -> x0, blocking collectives: 40.4 us -> none  [the longest x1 21.2 us: shards(): lax.all_gather(log_total.T, 'seq', axis=0, tiled=True)]
    reduce_sum x14 -> x0, other arithmetic: 34.1 us -> none  [the longest x1 12.9 us: forward_step(): running_sum = running_sum * factor + jnp.sum(weights, axis=2)]
  transfers between devices with their start and end apart: 18 -> 0, of which waited for: 14 -> 0; matrix products, arithmetic and copies ran while one was open for 15% -> 0% of each run, Pallas kernels for 0% -> 0%
where the time goes in v2:
time: 165 us
  Pallas kernels  164 us (99%)
    pallas_call x1, Pallas kernels, layer(): pl.pallas_call(functools.partial(layer_kernel, n_seq, n_head, inside, nam...  161 us

profile of v2, /device:TPU:0, one launch (start us, length us, event | category | flops | bytes accessed | tf_op | source)
XLA Modules:
  0.0 164.5 jit_solution(5816034015005787924)
XLA Ops:
  0.7 160.8 %layer.1 = (bf16[256,768]{1,0:T(8,128)(2,1)}, f32[256,768]{1,0:T(8,128)}, f32[48,1152]{1,0:T(8,128)}, f32[80,768]{1,0:T(8,128)}, f32[32,768]{1,0:T(8,128)}, /*in...) custom-call(s32[3]{0:T(128)} %refs_0_.1, bf16[256,768]{1,0:T(8,128)(2,1)} %refs_1_.1, f32[768]{0:T(1024)} %refs_2_.1, ...), custom_call_target="tpu_custom_call" | custom-call | tf_op jit(solution)/shard_map/layer/pallas_call | solution.py:1008
  161.5 2.8 %ending.1 = (bf16[256,768]{1,0:T(8,128)(2,1)}, f32[256,768]{1,0:T(8,128)}, f32[48]{0:T(128)}, f32[48]{0:T(128)}, f32[48,384]{1,0:T(8,128)}, /*index=5*/f32[24]{0...) custom-call(bf16[256,768]{1,0:T(8,128)(2,1)} %get-tuple-element.48.r, ...), custom_call_target="tpu_custom_call" | custom-call | tf_op jit(solution)/shard_map/ending/pallas_call | solution.py:1092

commit v3 on v2

--- a/solution.py
+++ b/solution.py
@@ -17,6 +17,8 @@
 HALO = 8
 MARKS = 16
 WIDE = 2
+X_FIRST = (0, 1, 2, 3)
+Z_FIRST = (0, 2, 3, 1)
 CHUNK = 1024
 RESIDENT = 8192
 EPS = 1e-6
@@ -28,32 +30,6 @@
 DMA = pltpu.SemaphoreType.DMA
 FLIPPED = ((1,), (1,))
 
-ARGUMENTS = (
-    "frames",
-    "lengths",
-    "gn_gain",
-    "gn_bias",
-    "w_query",
-    "q_bias",
-    "w_key",
-    "w_value",
-    "v_bias",
-    "w_out",
-    "out_bias",
-    "taps",
-    "conv_bias",
-    "ln_gain",
-    "ln_bias",
-    "w_up",
-    "up_bias",
-    "w_down",
-    "down_bias",
-    "layer_scale",
-    "out_grad",
-)
-INPUTS = ("lengths",) + tuple(name for name in ARGUMENTS if name != "lengths")
-SUMS = ("g_up", "g_down", "g_out", "g_kv", "g_q", "g_vec")
-
 
 def iota(shape, dim):
     return lax.broadcasted_iota(jnp.int32, shape, dim)
@@ -99,19 +75,19 @@
     )
 
 
-def greet_all(seq, head, n_seq, n_head):
+def greet(seq, head, n_seq):
     barrier = pltpu.get_barrier_semaphore()
-    count = n_seq * n_head
-
-    def hail(i, carry):
-        other = lax.rem(seq * n_head + head + i, count)
-        pl.semaphore_signal(
-            barrier, inc=1, device_id=(other // n_head, lax.rem(other, n_head)), device_id_type=MESH
-        )
+
+    def hail(*where):
+        pl.semaphore_signal(barrier, inc=1, device_id=where, device_id_type=MESH)
+
+    def step(i, carry):
+        hail(lax.rem(seq + i, n_seq), head)
         return carry
 
-    lax.fori_loop(1, count, hail, 0)
-    return lambda: pl.semaphore_wait(barrier, count - 1)
+    hail(seq, 1 - head)
+    lax.fori_loop(1, n_seq, step, 0)
+    return lambda: pl.semaphore_wait(barrier, n_seq)
 
 
 def group_matrix(width):
@@ -161,18 +137,18 @@
     return marks.astype(BF16)
 
 
-def put_block(ref, s, block):
+def put_block(ref, order, s, block):
     spare = ref.shape[4] - block.shape[0]
     if spare:
         block = jnp.concatenate([block, jnp.zeros((spare, block.shape[1]), F32)], axis=0)
-    ref[s % 2, s // 2 % 2, s // 4 % 2, s // 8] = block.astype(ref.dtype)
+    ref[tuple(s // 2**bit % 2 for bit in order)] = block.astype(ref.dtype)
 
 
 class Reduction:
-    def __init__(self, seq, head, source, arrivals, sems):
-        self.seq, self.head = seq, head
+    def __init__(self, seq, head, order, source, arrivals, sems):
+        self.seq, self.head, self.order = seq, head, order
         self.source, self.arrivals, self.sems = source, arrivals, sems
-        self.bits = [lax.rem(seq // 2**i, 2) for i in range(4)]
+        self.bits = [lax.rem(seq // 2**bit, 2) for bit in order]
 
     def copy(self, i):
         bit = self.bits[i]
@@ -181,7 +157,7 @@
             self.arrivals[i],
             self.sems.at[2 * i],
             self.sems.at[2 * i + 1],
-            (self.seq + (1 - 2 * bit) * 2**i, self.head),
+            (self.seq + (1 - 2 * bit) * 2 ** self.order[i], self.head),
         )
 
     def start(self):
@@ -234,7 +210,7 @@
     homes = CHUNK // rows
     own_chunk = seq // homes
     resident = total <= RESIDENT
-    met = greet_all(seq, head, n_seq, n_head)
+    met = greet(seq, head, n_seq)
 
     def loop(first, last, body):
         def step(i, carry):
@@ -321,17 +297,32 @@
     def kv_place(s):
         return kv_home.at[pl.ds(pl.multiple_of(s * rows, rows), rows), 0:LANES]
 
+    def near_head(i):
+        return jnp.where(seq < n_seq // 2, i, heads - 1 - i)
+
+    q_all = (dot(normed, r.w_query[...]) + row_of(r.q_bias)).astype(BF16).astype(F32)
+    q_flip = (q_all * HEAD_DIM**-0.5).T.astype(BF16)
+    for h in range(heads):
+        r.qt_send[h] = q_flip[HEAD_DIM * h : HEAD_DIM * (h + 1), :]
+    own_tile = lax.rem(seq, SPANS)
+
+    def q_dest(i):
+        h = near_head(heads - 1 - i)
+        return h, (h + offset) * per_head + seq // SPANS
+
+    def give_q(i):
+        h, dest = q_dest(i)
+        give(r.qt_send.at[h], r.qt.at[own_tile], r.qt_ssem.at[i], r.qt_rsem.at[own_tile], dest)
+
+    loop(0, heads, give_q)
     k_all = dot(normed, r.w_key[...])
     v_all = dot(normed, r.w_value[...]) + row_of(r.v_bias)
     for h in range(heads):
         lanes = slice(HEAD_DIM * h, HEAD_DIM * (h + 1))
         r.kv_send[h] = jnp.concatenate([k_all[:, lanes], v_all[:, lanes]], axis=1).astype(BF16)
 
-    def far_first(i):
-        return jnp.where(seq < n_seq // 2, heads - 1 - i, i)
-
     def kv_dest(i):
-        h = far_first(i // pairs)
+        h = near_head(i // pairs)
         return h, (h + offset) * per_head + 2 * lax.rem(i, pairs) + low
 
     def give_kv(i):
@@ -339,21 +330,6 @@
         give(r.kv_send.at[h], kv_place(seq), r.kv_ssem.at[i], r.kv_rsem.at[seq], dest)
 
     loop(0, heads * pairs, give_kv)
-    q_all = (dot(normed, r.w_query[...]) + row_of(r.q_bias)).astype(BF16).astype(F32)
-    q_flip = (q_all * HEAD_DIM**-0.5).T.astype(BF16)
-    for h in range(heads):
-        r.qt_send[h] = q_flip[HEAD_DIM * h : HEAD_DIM * (h + 1), :]
-    own_tile = lax.rem(seq, SPANS)
-
-    def q_dest(i):
-        h = far_first(i)
-        return h, (h + offset) * per_head + seq // SPANS
-
-    def give_q(i):
-        h, dest = q_dest(i)
-        give(r.qt_send.at[h], r.qt.at[own_tile], r.qt_ssem.at[i], r.qt_rsem.at[own_tile], dest)
-
-    loop(0, heads, give_q)
     r.normed_flip[...] = flip(normed)
     r.hat[...] = hat
 
@@ -390,6 +366,25 @@
             r.kvt[:, here] = flip(r.kv[here, 0:LANES])
         return here
 
+    def give_att(t):
+        home = part * SPANS + t
+        give(
+            r.att_send.at[t],
+            r.att_recv.at[0, own_head],
+            r.att_ssem.at[t],
+            r.att_rsem.at[0, own_head],
+            home,
+        )
+
+    def close(t):
+        norm = r.norm[t, 0:1]
+        result = r.ot[t] / norm
+        r.ot[t] = result
+        r.top[t, 0:1] = r.top[t, 0:1] + jnp.log(norm)
+        for j in range(WIDE):
+            r.att_send[t * WIDE + j] = result[:, lanes_of(j)].astype(BF16)
+            give_att(t * WIDE + j)
+
     def forward_chunk(i):
         c = near_first(i)
         settle(c)
@@ -412,16 +407,7 @@
             r.top[t, 0:1] = new_top
             r.norm[t, 0:1] = r.norm[t, 0:1] * factor + total_of(weights)
             r.ot[t] = r.ot[t] * factor + dot(r.kvt[HEAD_DIM:, here], weights.astype(BF16))
-
-    def give_att(t):
-        home = part * SPANS + t
-        give(
-            r.att_send.at[t],
-            r.att_recv.at[0, own_head],
-            r.att_ssem.at[t],
-            r.att_rsem.at[0, own_head],
-            home,
-        )
+            pl.when(i == steps - 1)(lambda: close(t))
 
     @pl.when(active)
     def _():
@@ -442,17 +428,6 @@
 
         loop(0, tiles, take_q)
         loop(0, steps, forward_chunk)
-
-        def close(t):
-            norm = r.norm[t, 0:1]
-            result = r.ot[t] / norm
-            r.ot[t] = result
-            r.top[t, 0:1] = r.top[t, 0:1] + jnp.log(norm)
-            for j in range(WIDE):
-                r.att_send[t * WIDE + j] = result[:, lanes_of(j)].astype(BF16)
-                give_att(t * WIDE + j)
-
-        loop(0, tiles, close)
 
     wout_copy.wait()
 
@@ -560,19 +535,21 @@
     ln_copy.start()
     reductions = {}
 
-    def reduce_blocks(name, member):
+    def reduce_blocks(name, member, order=X_FIRST):
         if not inside:
             getattr(r, name)[...] = member.astype(getattr(r, name).dtype)
             return
         tall = member.shape[0] // n_seq
         for s in range(n_seq):
-            put_block(getattr(r, name + "_source"), s, member[tall * s : tall * (s + 1)])
-        reduce_start(name)
-
-    def reduce_start(name):
+            put_block(
+                getattr(r, name + "_source"), order, s, member[tall * s : tall * (s + 1)]
+            )
+        reduce_start(name, order)
+
+    def reduce_start(name, order):
         arrivals = [getattr(r, "%s_in%d" % (name, i)) for i in range(4)]
         source, sems = getattr(r, name + "_source"), getattr(r, name + "_sems")
-        reductions[name] = Reduction(seq, head, source, arrivals, sems)
+        reductions[name] = Reduction(seq, head, order, source, arrivals, sems)
         reductions[name].start()
 
     def advance(i, *names):
@@ -587,7 +564,6 @@
     advance(1, "g_up")
     reduce_blocks("g_down", dot(flip(act_low), proj_grad))
     up_sum = total_of(pre_low.astype(F32))
-    advance(1, "g_down")
 
     ln_copy.wait()
     ln_grad = r.ln_own[...].astype(F32) + r.ln_other[...].astype(F32)
@@ -614,6 +590,7 @@
         give(r.dot_send.at[h], r.dot_in.at[own_tile], r.dot_ssem.at[i], r.dot_rsem.at[own_tile], dest)
 
     loop(0, heads, give_dot)
+    advance(1, "g_down")
     advance(2, "g_up")
     reduce_blocks("g_out", dot(r.att_recv[0].reshape(att_shape), branch_grad))
     proj_copy.wait()
@@ -639,16 +616,12 @@
         def prepare(t):
             clip = clip_of((part * SPANS + t * WIDE) * rows + iota((1, across), 1), r.lengths)
             r.q_block[t, LANES : LANES + MARKS] = mark_rows(clip, r.top[t, 0:1])
-            lane = iota((rows, LANES), 1)
             deltas = []
             for j in range(WIDE):
                 arrived(r.dot_in.at[t * WIDE + j], r.dot_rsem.at[t * WIDE + j])
                 grads = r.dot_in[t * WIDE + j]
                 r.d_block[t, HEAD_DIM:LANES, lanes_of(j)] = grads
                 deltas.append(total_of(grads.astype(F32) * r.ot[t, :, lanes_of(j)]))
-                both = jnp.concatenate([r.qt[t * WIDE + j], grads], axis=0).astype(F32).T
-                r.qd_rows[t, lanes_of(j)] = jnp.where(lane < HEAD_DIM, both, 0.0).astype(BF16)
-                r.qd_rows[t, lanes_of(WIDE + j)] = jnp.where(lane < HEAD_DIM, 0.0, both).astype(BF16)
             r.d_block[t, LANES : LANES + MARKS] = mark_rows(None, jnp.concatenate(deltas, axis=1))
 
         loop(0, tiles, prepare)
@@ -695,40 +668,35 @@
 
     def backward_chunk(i):
         here = load(far_chunk(i), False)
-        r.dkv_sum[...] = jnp.zeros((CHUNK, LANES), F32)
-
-        def tile(t):
+        for t in range(tiles):
             keys = r.kv[here, :]
             probs = jnp.exp(dot(keys, r.q_block[t]))
             grads = (probs * dot(keys, r.d_block[t])).astype(BF16)
-            r.dkv_sum[...] += dot(
-                jnp.concatenate([grads, probs.astype(BF16)], axis=1), r.qd_rows[t]
-            )
+            dk = dot(r.q_block[t, 0:HEAD_DIM], grads, FLIPPED)
+            dv = dot(r.d_block[t, HEAD_DIM:LANES], probs.astype(BF16), FLIPPED)
+            if t == 0:
+                r.dkv_sum[0:HEAD_DIM] = dk
+                r.dkv_sum[HEAD_DIM:] = dv
+            else:
+                r.dkv_sum[0:HEAD_DIM] += dk
+                r.dkv_sum[HEAD_DIM:] += dv
             r.dq_sum[t] += dot(r.kvt[0:HEAD_DIM, here], grads)
 
-        loop(0, tiles, tile)
         pl.when(i > 0)(lambda: dkv_finish(i - 1))
         for k in range(couples):
             other = pl.ds(pl.multiple_of((2 * k + 1 - low) * rows, rows), rows)
             mine = pl.ds(pl.multiple_of((2 * k + low) * rows, rows), rows)
-            r.pair_send[lax.rem(i, 2), k] = r.dkv_sum[other].astype(BF16)
+            r.pair_send[lax.rem(i, 2), k] = r.dkv_sum[:, other].astype(BF16)
             pair_copy(i, k).start()
-            r.dkv_keep[k] = r.dkv_sum[mine]
-
-    for phase in range(4):
-
-        @pl.when(active)
-        def _():
-            loop(phase * steps // 4, (phase + 1) * steps // 4, backward_chunk)
-
-        if phase == 0:
-            advance(2, "g_down")
-            advance(3, "g_up")
-        if phase == 1:
-            advance(2, "g_out")
-        if phase == 2:
-            advance(3, "g_down")
-            advance(3, "g_out")
+            r.dkv_keep[k] = r.dkv_sum[:, mine]
+
+    def backward_step(i):
+        pl.when(active)(lambda: backward_chunk(i))
+        if inside:
+            pl.when(i == 0)(lambda: advance(3, "g_up"))
+            pl.when(i == 1)(lambda: advance(2, "g_down", "g_out"))
+
+    loop(0, steps, backward_step)
 
     def give_dq(t):
         give(
@@ -750,54 +718,52 @@
         loop(0, tiles, close)
         dkv_finish(steps - 1)
 
+    advance(3, "g_down", "g_out")
+
     for h in range(heads):
         for p in range(pairs):
             arrived(r.dkv_in.at[p, h], r.dkv_rsem.at[p, h])
-    dk, dv = [], []
-    for h in range(heads):
-        both = r.dkv_in[0, h].astype(F32)
-        for p in range(1, pairs):
-            both = both + r.dkv_in[p, h].astype(F32)
-        dk.append(both[:, 0:HEAD_DIM])
-        dv.append(both[:, HEAD_DIM:])
-    dk = jnp.concatenate(dk, axis=1).astype(BF16)
-    dv = jnp.concatenate(dv, axis=1).astype(BF16)
+    dkv = r.dkv_in[0].astype(F32)
+    for p in range(1, pairs):
+        dkv = dkv + r.dkv_in[p].astype(F32)
+    dk = dkv[:, 0:HEAD_DIM].reshape(att_shape).T.astype(BF16)
+    dv = dkv[:, HEAD_DIM:].reshape(att_shape).T.astype(BF16)
     normed_flip = r.normed_flip[...]
-    reduce_blocks(
-        "g_kv", jnp.concatenate([dot(normed_flip, dk), dot(normed_flip, dv)], axis=1)
-    )
+    reduce_blocks("g_k", dot(normed_flip, dk))
+    reduce_blocks("g_v", dot(normed_flip, dv), Z_FIRST)
     kv_part = dot(dk, r.w_key[...], FLIPPED) + dot(dv, r.w_value[...], FLIPPED)
     for h in range(heads):
         arrived(r.dq_in.at[h], r.dq_rsem.at[h])
     dq = flip(r.dq_in[...].reshape(att_shape))
     r.part_own[...] = (kv_part + dot(dq, r.w_query[...], FLIPPED)).astype(BF16)
+    hat = r.hat[...]
+    gain = row_of(r.gn_gain)
+    own = r.part_own[...].astype(F32)
+    r.thin_own[...] = jnp.concatenate(
+        [total_of(own * hat), total_of(own), jnp.zeros((HALO - 2, width), F32)], axis=0
+    )
+    thin_copy = swap(3, r.thin_own, r.thin_other)
+    thin_copy.start()
     part_copy = swap(2, r.part_own, r.part_other)
     part_copy.start()
+    scaled = own * gain
+    r.gstats[seq] = sums_by_clip((scaled, scaled * hat), rows_clip, width)
+
+    def gstats_copy(i):
+        other = lax.rem(seq + i, n_seq)
+        return remote(
+            r.gstats.at[seq],
+            r.gstats.at[seq],
+            r.gstat_ssem.at[i],
+            r.gstat_rsem.at[seq],
+            (other, head),
+        )
+
+    loop(1, n_seq, lambda i: gstats_copy(i).start())
+    advance(1, "g_k", "g_v")
     reduce_blocks("g_q", dot(normed_flip, dq))
-    advance(1, "g_kv")
-    hat = r.hat[...]
-    gain = row_of(r.gn_gain)
-    scaled = r.part_own[...].astype(F32) * gain
-    me = seq * n_head + head
-    everyone = n_seq * n_head
-    r.gstats[me] = sums_by_clip((scaled, scaled * hat), rows_clip, width)
-
-    def gstats_copy(i):
-        other = lax.rem(me + i, everyone)
-        return remote(
-            r.gstats.at[me],
-            r.gstats.at[me],
-            r.gstat_ssem.at[i],
-            r.gstat_rsem.at[me],
-            (other // n_head, lax.rem(other, n_head)),
-        )
-
-    loop(1, everyone, lambda i: gstats_copy(i).start())
-    advance(1, "g_q")
-    part_copy.wait()
-    normed_grad = r.part_own[...].astype(F32) + r.part_other[...].astype(F32)
-    r.vectors[13:14] = total_of(normed_grad * hat)
-    r.vectors[14:15] = total_of(normed_grad)
+    thin_copy.wait()
+    r.vectors[13:15] = r.thin_own[0:2] + r.thin_other[0:2]
     q_sum = total_of(dq.astype(F32))
     v_sum = total_of(dv.astype(F32))
     if inside:
@@ -811,38 +777,43 @@
                 block.append(
                     jnp.concatenate([member[:, wide * s : wide * (s + 1)], blank], axis=1)
                 )
-            put_block(r.g_vec_source, s, jnp.concatenate(block + [spare], axis=0))
-        reduce_start("g_vec")
+            put_block(r.g_vec_source, Z_FIRST, s, jnp.concatenate(block + [spare], axis=0))
+        reduce_start("g_vec", Z_FIRST)
     else:
         r.vec_out[...] = r.vectors[...]
         r.q_out[...] = q_sum
         r.v_out[...] = v_sum
         r.up_out[...] = up_sum
-    advance(2, "g_kv")
-    advance(1, "g_vec")
+    advance(1, "g_q", "g_vec")
+    part_copy.wait()
+    normed_grad = r.part_own[...].astype(F32) + r.part_other[...].astype(F32)
+    advance(2, "g_k", "g_v")
 
     def gstats_take(i):
-        other = lax.rem(me + i, everyone)
+        other = lax.rem(seq + i, n_seq)
         arrived(r.gstats.at[other], r.gstat_rsem.at[other])
 
-    loop(1, everyone, gstats_take)
-    summed = lax.fori_loop(
-        0, everyone, lambda i, acc: acc + r.gstats[i], jnp.zeros((HALO, LANES), F32)
-    ) / members_of(r.lengths, width)
+    loop(1, n_seq, gstats_take)
+    r.gsum[0] = lax.fori_loop(
+        0, n_seq, lambda i, acc: acc + r.gstats[i], jnp.zeros((HALO, LANES), F32)
+    )
+    gsum_copy = swap(4, r.gsum.at[0], r.gsum.at[1])
+    gsum_copy.start()
+    advance(3, "g_k", "g_v")
+    advance(2, "g_q", "g_vec")
+    gsum_copy.wait()
+    summed = (r.gsum[0] + r.gsum[1]) / members_of(r.lengths, width)
     means = dot(summed, group_matrix(width), FLIPPED, HIGHEST)
-    advance(2, "g_q")
-    advance(2, "g_vec")
-    advance(3, "g_kv")
     r.frames_grad[...] = r.hidden_grad[...] + frame_rstd * (
         normed_grad * gain - by_clip(rows_clip, means, 0) - hat * by_clip(rows_clip, means, CLIPS)
     )
-    advance(3, "g_q", "g_vec")
+    advance(3, "g_vec", "g_q")
     if inside:
-        for name in SUMS:
+        for name in reductions:
             getattr(r, name)[...] = reductions[name].finish()
 
     loop(1, n_seq, lambda i: arrived(r.stats.at[seq], r.stat_ssem.at[i]))
-    loop(1, everyone, lambda i: arrived(r.gstats.at[me], r.gstat_ssem.at[i]))
+    loop(1, n_seq, lambda i: arrived(r.gstats.at[seq], r.gstat_ssem.at[i]))
 
     def kv_given(i):
         h, dest = kv_dest(i)
@@ -887,7 +858,7 @@
 
 
 def layer(n_seq, n_head, arrays):
-    rows, width = arrays["frames"].shape
+    rows, width = arrays.get("frames").shape
     hidden_units = arrays["w_up"].shape[1]
     wide = arrays["w_query"].shape[1]
     heads = wide // HEAD_DIM
@@ -904,112 +875,114 @@
     tiles = SPANS // WIDE
     across = WIDE * rows
     shape = jax.ShapeDtypeStruct
-    matrices = {
-        "g_up": (width, hidden_units),
-        "g_down": (hidden_units, width),
-        "g_out": (wide, width),
-        "g_kv": (width, 2 * wide),
-        "g_q": (width, wide),
-    }
-    outputs = {
-        "result": shape((rows, width), BF16),
-        "frames_grad": shape((rows, width), F32),
-    }
+    matrices = dict(
+        g_up=(width, hidden_units),
+        g_down=(hidden_units, width),
+        g_out=(wide, width),
+        g_k=(width, wide),
+        g_v=(width, wide),
+        g_q=(width, wide),
+    )
+    outputs = dict(result=shape((rows, width), BF16), frames_grad=shape((rows, width), F32))
     blocks = {}
     if inside:
         for name, (tall, long) in matrices.items():
             blocks[name] = (whole_tiles(tall // n_seq), long), BF16
-        blocks["g_vec"] = (24, LANES), F32
+        blocks.update(g_vec=((24, LANES), F32))
         for name, (dims, kind) in blocks.items():
             outputs[name] = shape(dims, F32)
     else:
         for name, dims in matrices.items():
             outputs[name] = shape(dims, BF16)
-        outputs["vec_out"] = shape((16, width), F32)
-        outputs["q_out"] = shape((1, wide), F32)
-        outputs["v_out"] = shape((1, wide), F32)
-        outputs["up_out"] = shape((1, hidden_units), F32)
+        outputs.update(
+            vec_out=shape((16, width), F32),
+            q_out=shape((1, wide), F32),
+            v_out=shape((1, wide), F32),
+            up_out=shape((1, hidden_units), F32),
+        )
     if not resident:
-        outputs["kv_far"] = shape((total, LANES), BF16)
+        outputs.update(kv_far=shape((total, LANES), BF16))
     keys = total if resident else 2 * CHUNK
-    scratch = {
-        "stats": vmem(n_seq, HALO, LANES, kind=F32),
-        "stat_ssem": DMA((n_seq,)),
-        "stat_rsem": DMA((n_seq,)),
-        "other_wout": vmem(wide, width),
-        "wout_sem": DMA((2,)),
-        "hat": vmem(rows, width, kind=F32),
-        "normed_flip": vmem(width, rows),
-        "kv_send": vmem(heads, rows, LANES),
-        "kv_ssem": DMA((heads * pairs,)),
-        "kv_rsem": DMA((n_seq,)),
-        "relay_sem": DMA((n_seq,)),
-        "kv": vmem(keys, 2 * LANES),
-        "kvt": vmem(LANES, keys),
-        "load_sem": DMA((1,)),
-        "qt_send": vmem(heads, HEAD_DIM, rows),
-        "qt_ssem": DMA((heads,)),
-        "qt_rsem": DMA((SPANS,)),
-        "qt": vmem(*tile),
-        "q_block": vmem(tiles, 2 * LANES, across),
-        "d_block": vmem(tiles, 2 * LANES, across),
-        "qd_rows": vmem(tiles, 2 * across, LANES),
-        "scores": vmem(2, CHUNK, across, kind=F32),
-        "ot": vmem(tiles, HEAD_DIM, across, kind=F32),
-        "top": vmem(tiles, HALO, across, kind=F32),
-        "norm": vmem(tiles, HALO, across, kind=F32),
-        "att_send": vmem(*tile),
-        "att_ssem": DMA((SPANS,)),
-        "att_recv": vmem(n_head, heads, HEAD_DIM, rows),
-        "att_rsem": DMA((n_head, heads)),
-        "cross_sem": DMA((heads,)),
-        "rim": vmem(2, 4, HALO, width, kind=F32),
-        "rim_sem": DMA((2, 4)),
-        "padded": vmem(rows + 2 * HALO, width, kind=F32),
-        "padded_grad": vmem(rows + 2 * HALO, width, kind=F32),
-        "hidden_grad": vmem(rows, width, kind=F32),
-        "ln_own": vmem(rows, width),
-        "ln_other": vmem(rows, width),
-        "proj_own": vmem(rows, width),
-        "proj_other": vmem(rows, width),
-        "part_own": vmem(rows, width),
-        "part_other": vmem(rows, width),
-        "swap_sem": DMA((3, 2)),
-        "vectors": vmem(16, width, kind=F32),
-        "dot_send": vmem(heads, HEAD_DIM, rows),
-        "dot_ssem": DMA((heads,)),
-        "dot_in": vmem(*tile),
-        "dot_rsem": DMA((SPANS,)),
-        "dkv_sum": vmem(CHUNK, LANES, kind=F32),
-        "dkv_keep": vmem(couples, rows, LANES, kind=F32),
-        "pair_send": vmem(2, couples, rows, LANES),
-        "pair_in": vmem(2, couples, rows, LANES),
-        "pair_sem": DMA((2, 2, couples)),
-        "dkv_send": vmem(slots, rows, LANES),
-        "dkv_ssem": DMA((slots,)),
-        "dkv_in": vmem(pairs, heads, rows, LANES),
-        "dkv_rsem": DMA((pairs, heads)),
-        "dq_sum": vmem(tiles, HEAD_DIM, across, kind=F32),
-        "dq_send": vmem(*tile),
-        "dq_ssem": DMA((SPANS,)),
-        "dq_in": vmem(heads, HEAD_DIM, rows),
-        "dq_rsem": DMA((heads,)),
-        "gstats": vmem(n_seq * n_head, HALO, LANES, kind=F32),
-        "gstat_ssem": DMA((n_seq * n_head,)),
-        "gstat_rsem": DMA((n_seq * n_head,)),
-    }
+    scratch = dict(
+        stats=vmem(n_seq, HALO, LANES, kind=F32),
+        stat_ssem=DMA((n_seq,)),
+        stat_rsem=DMA((n_seq,)),
+        other_wout=vmem(wide, width),
+        wout_sem=DMA((2,)),
+        hat=vmem(rows, width, kind=F32),
+        normed_flip=vmem(width, rows),
+        kv_send=vmem(heads, rows, LANES),
+        kv_ssem=DMA((heads * pairs,)),
+        kv_rsem=DMA((n_seq,)),
+        relay_sem=DMA((n_seq,)),
+        kv=vmem(keys, 2 * LANES),
+        kvt=vmem(LANES, keys),
+        load_sem=DMA((1,)),
+        qt_send=vmem(heads, HEAD_DIM, rows),
+        qt_ssem=DMA((heads,)),
+        qt_rsem=DMA((SPANS,)),
+        qt=vmem(*tile),
+        q_block=vmem(tiles, 2 * LANES, across),
+        d_block=vmem(tiles, 2 * LANES, across),
+        scores=vmem(2, CHUNK, across, kind=F32),
+        ot=vmem(tiles, HEAD_DIM, across, kind=F32),
+        top=vmem(tiles, HALO, across, kind=F32),
+        norm=vmem(tiles, HALO, across, kind=F32),
+        att_send=vmem(*tile),
+        att_ssem=DMA((SPANS,)),
+        att_recv=vmem(n_head, heads, HEAD_DIM, rows),
+        att_rsem=DMA((n_head, heads)),
+        cross_sem=DMA((heads,)),
+        rim=vmem(2, 4, HALO, width, kind=F32),
+        rim_sem=DMA((2, 4)),
+        padded=vmem(rows + 2 * HALO, width, kind=F32),
+        padded_grad=vmem(rows + 2 * HALO, width, kind=F32),
+        hidden_grad=vmem(rows, width, kind=F32),
+        ln_own=vmem(rows, width),
+        ln_other=vmem(rows, width),
+        proj_own=vmem(rows, width),
+        proj_other=vmem(rows, width),
+        part_own=vmem(rows, width),
+        part_other=vmem(rows, width),
+        swap_sem=DMA((5, 2)),
+        thin_own=vmem(HALO, width, kind=F32),
+        thin_other=vmem(HALO, width, kind=F32),
+        vectors=vmem(16, width, kind=F32),
+        dot_send=vmem(heads, HEAD_DIM, rows),
+        dot_ssem=DMA((heads,)),
+        dot_in=vmem(*tile),
+        dot_rsem=DMA((SPANS,)),
+        dkv_sum=vmem(LANES, CHUNK, kind=F32),
+        dkv_keep=vmem(couples, LANES, rows, kind=F32),
+        pair_send=vmem(2, couples, LANES, rows),
+        pair_in=vmem(2, couples, LANES, rows),
+        pair_sem=DMA((2, 2, couples)),
+        dkv_send=vmem(slots, LANES, rows),
+        dkv_ssem=DMA((slots,)),
+        dkv_in=vmem(pairs, heads, LANES, rows),
+        dkv_rsem=DMA((pairs, heads)),
+        dq_sum=vmem(tiles, HEAD_DIM, across, kind=F32),
+        dq_send=vmem(*tile),
+        dq_ssem=DMA((SPANS,)),
+        dq_in=vmem(heads, HEAD_DIM, rows),
+        dq_rsem=DMA((heads,)),
+        gstats=vmem(n_seq, HALO, LANES, kind=F32),
+        gstat_ssem=DMA((n_seq,)),
+        gstat_rsem=DMA((n_seq,)),
+        gsum=vmem(2, HALO, LANES, kind=F32),
+    )
     for name, (dims, kind) in blocks.items():
         scratch[name + "_source"] = vmem(2, 2, 2, 2, *dims, kind=kind)
         for i in range(4):
             scratch["%s_in%d" % (name, i)] = vmem(*[2] * (3 - i), *dims, kind=kind)
         scratch[name + "_sems"] = DMA((8,))
-    names = [*INPUTS, *outputs, *scratch]
+    names = [*arrays, *outputs, *scratch]
     whole = pl.BlockSpec(memory_space=pltpu.VMEM)
     results = pl.pallas_call(
         functools.partial(layer_kernel, n_seq, n_head, inside, names),
         name="layer",
         out_shape=tuple(outputs.values()),
-        in_specs=[pl.BlockSpec(memory_space=pltpu.SMEM)] + [whole] * (len(INPUTS) - 1),
+        in_specs=[pl.BlockSpec(memory_space=pltpu.SMEM)] + [whole] * (len(arrays) - 1),
         out_specs=tuple(
             pl.BlockSpec(memory_space=pl.ANY) if name == "kv_far" else whole for name in outputs
         ),
@@ -1017,19 +990,19 @@
         compiler_params=pltpu.CompilerParams(
             collective_id=0, has_side_effects=True, vmem_limit_bytes=60 * 2**20
         ),
-    )(*[arrays[name] for name in INPUTS])
+    )(*arrays.values())
     results = dict(zip(outputs, results))
     if not inside:
         for name in matrices:
             results[name] = lax.psum_scatter(
                 results[name].astype(F32), "seq", scatter_dimension=0, tiled=True
             )
-        thin = [results["vec_out"][0:15]]
-        thin += [results[name] for name in ("q_out", "v_out", "up_out")]
+        last = list(results.values())[len(matrices) + 2 :]
+        thin = [last[0][0:15], *last[1:4]]
         thin = [lax.psum_scatter(t, "seq", scatter_dimension=1, tiled=True) for t in thin]
         thin = [jnp.pad(t, ((0, 0), (0, LANES - t.shape[1]))) for t in thin]
         results["g_vec"] = jnp.pad(jnp.concatenate(thin, axis=0), ((0, 6), (0, 0)))
-    return results
+    return [results[name] for name in ("result", "frames_grad", *matrices, "g_vec")]
 
 
 def ending_kernel(
@@ -1038,7 +1011,8 @@
     up_ref,
     down_ref,
     out_ref,
-    kv_ref,
+    k_ref,
+    v_ref,
     q_ref,
     vec_ref,
     output,
@@ -1064,11 +1038,10 @@
 ):
     output[...] = result_ref[...]
     frames_grad[...] = fgrad_ref[...]
-    wide = w_query.shape[1]
     tall = w_query.shape[0]
     w_query[...] = q_ref[0:tall, :]
-    w_key[...] = kv_ref[0:tall, 0:wide]
-    w_value[...] = kv_ref[0:tall, wide:]
+    w_key[...] = k_ref[0:tall, :]
+    w_value[...] = v_ref[0:tall, :]
     w_up[...] = up_ref[0:tall, :]
     w_down[...] = down_ref[0 : w_down.shape[0], :]
     w_out[...] = out_ref[0 : w_out.shape[0], :]
@@ -1084,7 +1057,7 @@
 
 
 def ending(n_seq, sums, wide, hidden_units):
-    rows, width = sums["result"].shape
+    rows, width = sums[0].shape
     shape = lambda *dims: jax.ShapeDtypeStruct(dims, F32)
     tall = width // n_seq
     thin = shape(tall)
@@ -1114,17 +1087,62 @@
             thin,
             thin,
         ),
-        in_specs=[whole] * 8,
+        in_specs=[whole] * 9,
         out_specs=tuple([whole] * 20),
         compiler_params=pltpu.CompilerParams(vmem_limit_bytes=56 * 2**20),
-    )(sums["result"], sums["frames_grad"], *[sums[name] for name in SUMS])
-
-
-def shards(n_seq, n_head, *args):
-    arrays = dict(zip(ARGUMENTS, args))
-    arrays["taps"] = arrays["taps"].T
+    )(*sums)
+
+
+def shards(
+    n_seq,
+    n_head,
+    frames,
+    lengths,
+    gn_gain,
+    gn_bias,
+    w_query,
+    q_bias,
+    w_key,
+    w_value,
+    v_bias,
+    w_out,
+    out_bias,
+    conv_weight,
+    conv_bias,
+    ln_gain,
+    ln_bias,
+    w_up,
+    up_bias,
+    w_down,
+    down_bias,
+    layer_scale,
+    out_grad,
+):
+    arrays = dict(
+        lengths=lengths,
+        frames=frames,
+        gn_gain=gn_gain,
+        gn_bias=gn_bias,
+        w_query=w_query,
+        q_bias=q_bias,
+        w_key=w_key,
+        w_value=w_value,
+        v_bias=v_bias,
+        w_out=w_out,
+        out_bias=out_bias,
+        taps=conv_weight.T,
+        conv_bias=conv_bias,
+        ln_gain=ln_gain,
+        ln_bias=ln_bias,
+        w_up=w_up,
+        up_bias=up_bias,
+        w_down=w_down,
+        down_bias=down_bias,
+        layer_scale=layer_scale,
+        out_grad=out_grad,
+    )
     sums = layer(n_seq, n_head, arrays)
-    out = list(ending(n_seq, sums, arrays["w_query"].shape[1], arrays["w_up"].shape[1]))
+    out = list(ending(n_seq, sums, w_query.shape[1], w_up.shape[1]))
     out[11] = out[11].T
     return tuple(out)
 

time: 165 us -> 144 us (0.87)
  Pallas kernels: 164 us -> 142 us
    pallas_call x1, Pallas kernels: 161 us -> 139 us  [layer(): pl.pallas_call(functools.partial(layer_kernel, n_seq, n_head, inside, nam...]
where the time goes in v3:
time: 144 us; the launch traced here: 143 us
  Pallas kernels  142 us (99%)
    pallas_call x1, Pallas kernels, layer(): pl.pallas_call(functools.partial(layer_kernel, n_seq, n_head, inside, nam...  139 us

profile of v3, /device:TPU:0, one launch (start us, length us, event | category | flops | bytes accessed | tf_op | source)
XLA Modules:
  0.0 142.9 jit_solution(12243109051965223517)
XLA Ops:
  0.7 139.3 %layer.1 = (bf16[256,768]{1,0:T(8,128)(2,1)}, f32[256,768]{1,0:T(8,128)}, f32[48,1152]{1,0:T(8,128)}, f32[80,768]{1,0:T(8,128)}, f32[32,768]{1,0:T(8,128)}, /*in...) custom-call(s32[3]{0:T(128)} %refs_0_.1, bf16[256,768]{1,0:T(8,128)(2,1)} %refs_1_.1, ...), custom_call_target="tpu_custom_call" | custom-call | tf_op jit(solution)/shard_map/layer/pallas_call | solution.py:981
  139.9 2.8 %ending.1 = (bf16[256,768]{1,0:T(8,128)(2,1)}, f32[256,768]{1,0:T(8,128)}, f32[48]{0:T(128)}, f32[48]{0:T(128)}, f32[48,384]{1,0:T(8,128)}, /*index=5*/f32[24]{0...) custom-call(bf16[256,768]{1,0:T(8,128)(2,1)} %get-tuple-element.49.r, ...), custom_call_target="tpu_custom_call" | custom-call | tf_op jit(solution)/shard_map/ending/pallas_call | solution.py:1065

commit v4 on v3

--- a/solution.py
+++ b/solution.py
@@ -593,6 +593,116 @@
     advance(1, "g_down")
     advance(2, "g_up")
     reduce_blocks("g_out", dot(r.att_recv[0].reshape(att_shape), branch_grad))
+    advance(1, "g_out")
+
+    @pl.when(active)
+    def _():
+        def prepare(t):
+            clip = clip_of((part * SPANS + t * WIDE) * rows + iota((1, across), 1), r.lengths)
+            r.q_block[t, LANES : LANES + MARKS] = mark_rows(clip, r.top[t, 0:1])
+            deltas = []
+            for j in range(WIDE):
+                arrived(r.dot_in.at[t * WIDE + j], r.dot_rsem.at[t * WIDE + j])
+                grads = r.dot_in[t * WIDE + j]
+                r.d_block[t, HEAD_DIM:LANES, lanes_of(j)] = grads
+                deltas.append(total_of(grads.astype(F32) * r.ot[t, :, lanes_of(j)]))
+            r.d_block[t, LANES : LANES + MARKS] = mark_rows(None, jnp.concatenate(deltas, axis=1))
+
+        loop(0, tiles, prepare)
+
+    def far_chunk(i):
+        return jnp.where(own_chunk < steps // 2, steps - 1 - i, i)
+
+    slots = r.dkv_send.shape[0]
+    couples = homes // 2
+
+    def pair_copy(i, k):
+        slot = lax.rem(i, 2)
+        return remote(
+            r.pair_send.at[slot, k],
+            r.pair_in.at[slot, k],
+            r.pair_sem.at[0, slot, k],
+            r.pair_sem.at[1, slot, k],
+            sibling,
+        )
+
+    def dkv_home(i, k):
+        return far_chunk(i) * homes + 2 * k + low
+
+    def dkv_sent(i, k):
+        slot = lax.rem(i * couples + k, slots)
+        given(r.dkv_send.at[slot], r.dkv_ssem.at[slot], dkv_home(i, k))
+
+    def dkv_finish(i):
+        for k in range(couples):
+            pair_copy(i, k).wait()
+            slot = lax.rem(i * couples + k, slots)
+            if slots < steps * couples:
+                pl.when(i * couples + k >= slots)(lambda: dkv_sent(i - slots // couples, k))
+            r.dkv_send[slot] = (
+                r.dkv_keep[k] + r.pair_in[lax.rem(i, 2), k].astype(F32)
+            ).astype(BF16)
+            give(
+                r.dkv_send.at[slot],
+                r.dkv_in.at[part // 2, own_head],
+                r.dkv_ssem.at[slot],
+                r.dkv_rsem.at[part // 2, own_head],
+                dkv_home(i, k),
+            )
+
+    def backward_chunk(i):
+        here = load(far_chunk(i), False)
+        for t in range(tiles):
+            keys = r.kv[here, :]
+            probs = jnp.exp(dot(keys, r.q_block[t]))
+            grads = (probs * dot(keys, r.d_block[t])).astype(BF16)
+            dk = dot(r.q_block[t, 0:HEAD_DIM], grads, FLIPPED)
+            dv = dot(r.d_block[t, HEAD_DIM:LANES], probs.astype(BF16), FLIPPED)
+            if t == 0:
+                r.dkv_sum[0:HEAD_DIM] = dk
+                r.dkv_sum[HEAD_DIM:] = dv
+            else:
+                r.dkv_sum[0:HEAD_DIM] += dk
+                r.dkv_sum[HEAD_DIM:] += dv
+            r.dq_sum[t] += dot(r.kvt[0:HEAD_DIM, here], grads)
+
+        pl.when(i > 0)(lambda: dkv_finish(i - 1))
+        for k in range(couples):
+            other = pl.ds(pl.multiple_of((2 * k + 1 - low) * rows, rows), rows)
+            mine = pl.ds(pl.multiple_of((2 * k + low) * rows, rows), rows)
+            r.pair_send[lax.rem(i, 2), k] = r.dkv_sum[:, other].astype(BF16)
+            pair_copy(i, k).start()
+            r.dkv_keep[k] = r.dkv_sum[:, mine]
+
+    def backward_step(i):
+        pl.when(active)(lambda: backward_chunk(i))
+        if inside:
+            pl.when(i == 0)(lambda: advance(3, "g_up"))
+            pl.when(i == 1)(lambda: advance(2, "g_down"))
+
+    loop(0, steps, backward_step)
+
+    def give_dq(t):
+        give(
+            r.dq_send.at[t],
+            r.dq_in.at[own_head],
+            r.dq_ssem.at[t],
+            r.dq_rsem.at[own_head],
+            part * SPANS + t,
+        )
+
+    @pl.when(active)
+    def _():
+        def close(t):
+            for j in range(WIDE):
+                grads = r.dq_sum[t, :, lanes_of(j)] * HEAD_DIM**-0.5
+                r.dq_send[t * WIDE + j] = grads.astype(BF16)
+                give_dq(t * WIDE + j)
+
+        loop(0, tiles, close)
+        dkv_finish(steps - 1)
+
+    branch_grad = r.hidden_grad[...].astype(BF16)
     proj_copy.wait()
     projected = r.proj_own[...].astype(F32) + r.proj_other[...].astype(F32) + row_of(r.down_bias)
     r.result[...] = (hidden + row_of(r.layer_scale) * projected).astype(BF16)
@@ -609,116 +719,7 @@
         ],
         axis=0,
     )
-    advance(1, "g_out")
-
-    @pl.when(active)
-    def _():
-        def prepare(t):
-            clip = clip_of((part * SPANS + t * WIDE) * rows + iota((1, across), 1), r.lengths)
-            r.q_block[t, LANES : LANES + MARKS] = mark_rows(clip, r.top[t, 0:1])
-            deltas = []
-            for j in range(WIDE):
-                arrived(r.dot_in.at[t * WIDE + j], r.dot_rsem.at[t * WIDE + j])
-                grads = r.dot_in[t * WIDE + j]
-                r.d_block[t, HEAD_DIM:LANES, lanes_of(j)] = grads
-                deltas.append(total_of(grads.astype(F32) * r.ot[t, :, lanes_of(j)]))
-            r.d_block[t, LANES : LANES + MARKS] = mark_rows(None, jnp.concatenate(deltas, axis=1))
-
-        loop(0, tiles, prepare)
-
-    def far_chunk(i):
-        return jnp.where(own_chunk < steps // 2, steps - 1 - i, i)
-
-    slots = r.dkv_send.shape[0]
-    couples = homes // 2
-
-    def pair_copy(i, k):
-        slot = lax.rem(i, 2)
-        return remote(
-            r.pair_send.at[slot, k],
-            r.pair_in.at[slot, k],
-            r.pair_sem.at[0, slot, k],
-            r.pair_sem.at[1, slot, k],
-            sibling,
-        )
-
-    def dkv_home(i, k):
-        return far_chunk(i) * homes + 2 * k + low
-
-    def dkv_sent(i, k):
-        slot = lax.rem(i * couples + k, slots)
-        given(r.dkv_send.at[slot], r.dkv_ssem.at[slot], dkv_home(i, k))
-
-    def dkv_finish(i):
-        for k in range(couples):
-            pair_copy(i, k).wait()
-            slot = lax.rem(i * couples + k, slots)
-            if slots < steps * couples:
-                pl.when(i * couples + k >= slots)(lambda: dkv_sent(i - slots // couples, k))
-            r.dkv_send[slot] = (
-                r.dkv_keep[k] + r.pair_in[lax.rem(i, 2), k].astype(F32)
-            ).astype(BF16)
-            give(
-                r.dkv_send.at[slot],
-                r.dkv_in.at[part // 2, own_head],
-                r.dkv_ssem.at[slot],
-                r.dkv_rsem.at[part // 2, own_head],
-                dkv_home(i, k),
-            )
-
-    def backward_chunk(i):
-        here = load(far_chunk(i), False)
-        for t in range(tiles):
-            keys = r.kv[here, :]
-            probs = jnp.exp(dot(keys, r.q_block[t]))
-            grads = (probs * dot(keys, r.d_block[t])).astype(BF16)
-            dk = dot(r.q_block[t, 0:HEAD_DIM], grads, FLIPPED)
-            dv = dot(r.d_block[t, HEAD_DIM:LANES], probs.astype(BF16), FLIPPED)
-            if t == 0:
-                r.dkv_sum[0:HEAD_DIM] = dk
-                r.dkv_sum[HEAD_DIM:] = dv
-            else:
-                r.dkv_sum[0:HEAD_DIM] += dk
-                r.dkv_sum[HEAD_DIM:] += dv
-            r.dq_sum[t] += dot(r.kvt[0:HEAD_DIM, here], grads)
-
-        pl.when(i > 0)(lambda: dkv_finish(i - 1))
-        for k in range(couples):
-            other = pl.ds(pl.multiple_of((2 * k + 1 - low) * rows, rows), rows)
-            mine = pl.ds(pl.multiple_of((2 * k + low) * rows, rows), rows)
-            r.pair_send[lax.rem(i, 2), k] = r.dkv_sum[:, other].astype(BF16)
-            pair_copy(i, k).start()
-            r.dkv_keep[k] = r.dkv_sum[:, mine]
-
-    def backward_step(i):
-        pl.when(active)(lambda: backward_chunk(i))
-        if inside:
-            pl.when(i == 0)(lambda: advance(3, "g_up"))
-            pl.when(i == 1)(lambda: advance(2, "g_down", "g_out"))
-
-    loop(0, steps, backward_step)
-
-    def give_dq(t):
-        give(
-            r.dq_send.at[t],
-            r.dq_in.at[own_head],
-            r.dq_ssem.at[t],
-            r.dq_rsem.at[own_head],
-            part * SPANS + t,
-        )
-
-    @pl.when(active)
-    def _():
-        def close(t):
-            for j in range(WIDE):
-                grads = r.dq_sum[t, :, lanes_of(j)] * HEAD_DIM**-0.5
-                r.dq_send[t * WIDE + j] = grads.astype(BF16)
-                give_dq(t * WIDE + j)
-
-        loop(0, tiles, close)
-        dkv_finish(steps - 1)
-
-    advance(3, "g_down", "g_out")
+    advance(2, "g_out")
 
     for h in range(heads):
         for p in range(pairs):
@@ -761,6 +762,7 @@
 
     loop(1, n_seq, lambda i: gstats_copy(i).start())
     advance(1, "g_k", "g_v")
+    advance(3, "g_down", "g_out")
     reduce_blocks("g_q", dot(normed_flip, dq))
     thin_copy.wait()
     r.vectors[13:15] = r.thin_own[0:2] + r.thin_other[0:2]

time: 144 us -> 140 us (0.972)
  Pallas kernels: 142 us -> 139 us
    pallas_call x1, Pallas kernels: 139 us -> 136 us  [layer(): pl.pallas_call(functools.partial(layer_kernel, n_seq, n_head, inside, nam...]
where the time goes in v4:
time: 140 us; the launch traced here: 139 us
  Pallas kernels  139 us (99%)
    pallas_call x1, Pallas kernels, layer(): pl.pallas_call(functools.partial(layer_kernel, n_seq, n_head, inside, nam...  136 us

profile of v4, /device:TPU:0, one launch (start us, length us, event | category | flops | bytes accessed | tf_op | source)
XLA Modules:
  0.0 139.4 jit_solution(17303781399996735705)
XLA Ops:
  0.7 135.8 %layer.1 = (bf16[256,768]{1,0:T(8,128)(2,1)}, f32[256,768]{1,0:T(8,128)}, f32[48,1152]{1,0:T(8,128)}, f32[80,768]{1,0:T(8,128)}, f32[32,768]{1,0:T(8,128)}, /*in...) custom-call(s32[3]{0:T(128)} %refs_0_.1, bf16[256,768]{1,0:T(8,128)(2,1)} %refs_1_.1, ...), custom_call_target="tpu_custom_call" | custom-call | tf_op jit(solution)/shard_map/layer/pallas_call | solution.py:983
  136.4 2.8 %ending.1 = (bf16[256,768]{1,0:T(8,128)(2,1)}, f32[256,768]{1,0:T(8,128)}, f32[48]{0:T(128)}, f32[48]{0:T(128)}, f32[48,384]{1,0:T(8,128)}, /*index=5*/f32[24]{0...) custom-call(bf16[256,768]{1,0:T(8,128)(2,1)} %get-tuple-element.49.r, ...), custom_call_target="tpu_custom_call" | custom-call | tf_op jit(solution)/shard_map/ending/pallas_call | solution.py:1067

commit v5 on v4

--- a/solution.py
+++ b/solution.py
@@ -307,7 +307,7 @@
     own_tile = lax.rem(seq, SPANS)
 
     def q_dest(i):
-        h = near_head(heads - 1 - i)
+        h = near_head(i)
         return h, (h + offset) * per_head + seq // SPANS
 
     def give_q(i):
@@ -334,8 +334,10 @@
     r.hat[...] = hat
 
     def near_first(i):
-        turn = jnp.where(own_chunk < steps // 2, i, steps - i)
-        return lax.rem(own_chunk + turn, steps)
+        below = own_chunk < steps // 2
+        place = jnp.where(below, own_chunk, steps - 1 - own_chunk)
+        place = jnp.where(i <= place, place - i, i)
+        return jnp.where(below, place, steps - 1 - place)
 
     def relay(c):
         for k in range(homes // 2):
@@ -727,16 +729,18 @@
     dkv = r.dkv_in[0].astype(F32)
     for p in range(1, pairs):
         dkv = dkv + r.dkv_in[p].astype(F32)
+    normed_flip = r.normed_flip[...]
     dk = dkv[:, 0:HEAD_DIM].reshape(att_shape).T.astype(BF16)
+    reduce_blocks("g_k", dot(normed_flip, dk))
     dv = dkv[:, HEAD_DIM:].reshape(att_shape).T.astype(BF16)
-    normed_flip = r.normed_flip[...]
-    reduce_blocks("g_k", dot(normed_flip, dk))
     reduce_blocks("g_v", dot(normed_flip, dv), Z_FIRST)
-    kv_part = dot(dk, r.w_key[...], FLIPPED) + dot(dv, r.w_value[...], FLIPPED)
     for h in range(heads):
         arrived(r.dq_in.at[h], r.dq_rsem.at[h])
     dq = flip(r.dq_in[...].reshape(att_shape))
-    r.part_own[...] = (kv_part + dot(dq, r.w_query[...], FLIPPED)).astype(BF16)
+    reduce_blocks("g_q", dot(normed_flip, dq))
+    advance(1, "g_k", "g_v")
+    part_sum = dot(dk, r.w_key[...], FLIPPED) + dot(dv, r.w_value[...], FLIPPED)
+    r.part_own[...] = (part_sum + dot(dq, r.w_query[...], FLIPPED)).astype(BF16)
     hat = r.hat[...]
     gain = row_of(r.gn_gain)
     own = r.part_own[...].astype(F32)
@@ -761,9 +765,8 @@
         )
 
     loop(1, n_seq, lambda i: gstats_copy(i).start())
-    advance(1, "g_k", "g_v")
+    advance(1, "g_q")
     advance(3, "g_down", "g_out")
-    reduce_blocks("g_q", dot(normed_flip, dq))
     thin_copy.wait()
     r.vectors[13:15] = r.thin_own[0:2] + r.thin_other[0:2]
     q_sum = total_of(dq.astype(F32))
@@ -786,11 +789,11 @@
         r.q_out[...] = q_sum
         r.v_out[...] = v_sum
         r.up_out[...] = up_sum
-    advance(1, "g_q", "g_vec")
+    advance(2, "g_k", "g_v")
+    advance(1, "g_vec")
     part_copy.wait()
     normed_grad = r.part_own[...].astype(F32) + r.part_other[...].astype(F32)
-    advance(2, "g_k", "g_v")
-
+    advance(2, "g_q")
     def gstats_take(i):
         other = lax.rem(seq + i, n_seq)
         arrived(r.gstats.at[other], r.gstat_rsem.at[other])
@@ -802,14 +805,14 @@
     gsum_copy = swap(4, r.gsum.at[0], r.gsum.at[1])
     gsum_copy.start()
     advance(3, "g_k", "g_v")
-    advance(2, "g_q", "g_vec")
+    advance(2, "g_vec")
+    advance(3, "g_q", "g_vec")
     gsum_copy.wait()
     summed = (r.gsum[0] + r.gsum[1]) / members_of(r.lengths, width)
     means = dot(summed, group_matrix(width), FLIPPED, HIGHEST)
     r.frames_grad[...] = r.hidden_grad[...] + frame_rstd * (
         normed_grad * gain - by_clip(rows_clip, means, 0) - hat * by_clip(rows_clip, means, CLIPS)
     )
-    advance(3, "g_vec", "g_q")
     if inside:
         for name in reductions:
             getattr(r, name)[...] = reductions[name].finish()

time: 140 us -> 138 us (0.986)
  Pallas kernels: 139 us -> 136 us
    pallas_call x1, Pallas kernels: 136 us -> 134 us  [layer(): pl.pallas_call(functools.partial(layer_kernel, n_seq, n_head, inside, nam...]
where the time goes in v5:
time: 138 us; the launch traced here: 137 us
  Pallas kernels  136 us (99%)
    pallas_call x1, Pallas kernels, layer(): pl.pallas_call(functools.partial(layer_kernel, n_seq, n_head, inside, nam...  134 us
    pallas_call x1, Pallas kernels, ending(): pl.pallas_call(ending_kernel, name='ending', out_shape=(jax.ShapeDtypeStr...  2.8 us

profile of v5, /device:TPU:0, one launch (start us, length us, event | category | flops | bytes accessed | tf_op | source)
XLA Modules:
  0.0 137.3 jit_solution(12170807058155976783)
XLA Ops:
  0.7 133.7 %layer.1 = (bf16[256,768]{1,0:T(8,128)(2,1)}, f32[256,768]{1,0:T(8,128)}, f32[48,1152]{1,0:T(8,128)}, f32[80,768]{1,0:T(8,128)}, f32[32,768]{1,0:T(8,128)}, /*in...) custom-call(s32[3]{0:T(128)} %refs_0_.1, bf16[256,768]{1,0:T(8,128)(2,1)} %refs_1_.1, ...), custom_call_target="tpu_custom_call" | custom-call | tf_op jit(solution)/shard_map/layer/pallas_call | solution.py:986
  134.4 2.8 %ending.1 = (bf16[256,768]{1,0:T(8,128)(2,1)}, f32[256,768]{1,0:T(8,128)}, f32[48]{0:T(128)}, f32[48]{0:T(128)}, f32[48,384]{1,0:T(8,128)}, /*index=5*/f32[24]{0...) custom-call(bf16[256,768]{1,0:T(8,128)(2,1)} %get-tuple-element.49.r, ...), custom_call_target="tpu_custom_call" | custom-call | tf_op jit(solution)/shard_map/ending/pallas_call | solution.py:1070
